TPU v7x, 32 devices: a whole 2x2x4 slice. The times are simulated.
32 devices in a mesh: grp: 2 (over x), sta: 16 (over z, y, core).
Axes of the slice: x: 2, y: 2, z: 4, core: 2. Of those that a mesh axis runs over, the one named last changes fastest.
Arguments:
- spectra: bfloat16 [2, 8, 16, 64, 2048], P(None, 'grp', None, 'sta'), parts along dimension 1, may hold values from -6 to 6
- block_counts: int32 [16], replicated, may hold values from 1 to 4, as said below
- window_masks: int32 [8, 16, 16], P('grp'), parts along dimension 0, may hold values from 0 to 1, as said below
- pair_table: int32 [4, 8, 2], replicated, may hold values from 0 to 15, as said below
Outputs:
- stacks: float32 [8, 32, 16, 2048], P('grp', 'sta'), parts along dimension 0
There are 2 independent parts, one for each index of `grp`. A program takes and returns all parts, laid end to end along the dimension named above; an argument that names none is the same for every part. Nothing has to cross between parts.
Inputs may be any that keep to these rules, and one draw needn't show every extreme that they name: `block_counts`: the largest is 4. `window_masks`: some block-days have no valid window. `pair_table`: in each round every block appears in exactly one pair.
All inputs are finite; a program needn't handle non-finite values.
Results may differ from a plain program's by a relative error of at most 0.0038.
Values may be sent and summed in bfloat16 or wider, within the bound.
No kernel may reach another device: no remote copies, remote signals or barrier semaphores. Data moves between devices by JAX's collectives and lax.ppermute only.
A program may use at most 320 MiB of HBM per device.

v0:
```python
import math

import jax
import jax.numpy as jnp
from jax import lax
from jax.sharding import PartitionSpec as P

LAGS = 2048


def phase_table(freq_count, lag_count):
    freqs = jnp.arange(freq_count, dtype=jnp.int32)
    shifts = jnp.mod(jnp.arange(lag_count, dtype=jnp.int32) - lag_count // 2, 2 * freq_count)
    phases = jnp.mod(freqs[:, None] * shifts[None, :], 2 * freq_count)
    angles = phases.astype(jnp.float32) * (math.pi / freq_count)
    return jnp.concatenate([jnp.cos(angles), -jnp.sin(angles)], axis=0).astype(jnp.bfloat16)


def cross_local(blocks, weights, first, second):
    left = jnp.take(blocks, first, axis=3)
    right = jnp.take(blocks, second, axis=3)
    pattern = "dwpif,dwpjf->dpijf"
    real_part = jnp.einsum(pattern, left[0], right[0], preferred_element_type=jnp.float32)
    real_part = real_part + jnp.einsum(
        pattern, left[1], right[1], preferred_element_type=jnp.float32
    )
    imag_part = jnp.einsum(pattern, left[1], right[0], preferred_element_type=jnp.float32)
    imag_part = imag_part - jnp.einsum(
        pattern, left[0], right[1], preferred_element_type=jnp.float32
    )
    joint = jnp.einsum(
        "dwp,dwp->dp", jnp.take(weights, first, axis=2), jnp.take(weights, second, axis=2)
    )
    inverse = 1.0 / jnp.maximum(joint, 1.0)
    real_part = jnp.cumsum(real_part * inverse[:, :, None, None, None], axis=0)
    imag_part = jnp.cumsum(imag_part * inverse[:, :, None, None, None], axis=0)
    stacked = jnp.stack([real_part, imag_part]).astype(jnp.bfloat16)
    ordered = jnp.transpose(stacked, (2, 1, 3, 4, 0, 5))
    return ordered.reshape(
        ordered.shape[0] * ordered.shape[1],
        ordered.shape[2] * ordered.shape[3],
        2,
        ordered.shape[5],
    )


def local(spectra, block_counts, window_masks, pair_table):
    device = lax.axis_index("sta")
    devices = lax.axis_size("sta")
    slot_count = spectra.shape[3]
    total_bins = spectra.shape[4]
    local_bins = total_bins // devices
    own_count = lax.dynamic_slice_in_dim(block_counts, device, 1)[0]
    own_masks = lax.dynamic_slice_in_dim(window_masks, device, 1, 2)[:, :, 0]
    live_slots = jnp.arange(slot_count, dtype=jnp.int32) < own_count
    keeper = (own_masks[:, :, None] > 0) & live_slots[None, None, :]
    cleaned = spectra * keeper[None, :, :, :, None].astype(jnp.bfloat16)
    regrouped = lax.all_to_all(cleaned, "sta", split_axis=4, concat_axis=3, tiled=True)
    day_count = regrouped.shape[1]
    window_count = regrouped.shape[2]
    blocks = regrouped.reshape(2, day_count, window_count, devices, slot_count, local_bins)
    weights = window_masks.astype(jnp.float32)
    phase_rows = phase_table(total_bins, LAGS)
    lag_scale = 1.0 / math.sqrt(total_bins)
    round_count = pair_table.shape[0]
    pending = [
        cross_local(blocks, weights, pair_table[round_index, :, 0], pair_table[round_index, :, 1])
        for round_index in range(round_count)
    ]
    outputs = []
    for stacked in pending:
        received = lax.all_to_all(stacked, "sta", split_axis=0, concat_axis=3, tiled=True)
        lagged = (
            jnp.dot(
                received.reshape(-1, 2 * total_bins), phase_rows, preferred_element_type=jnp.float32
            )
            * lag_scale
        )
        outputs.append(lagged.reshape(received.shape[0], received.shape[1], LAGS))
    return jnp.stack(outputs)


def solution(mesh):
    placed = (P(None, "grp", None, "sta", None), P(), P("grp", None, None), P())
    return jax.shard_map(
        local, mesh=mesh, in_specs=placed, out_specs=P("grp", "sta", None, None), check_vma=False
    )
```

profile of v0, /device:TPU:1, one launch (start us, length us, event | category | flops | bytes accessed | tf_op | source)
XLA Modules:
  0.0 566.6 jit_solution(2605613430282778577)
XLA Ops:
  5.6 20.8 %copy.164 = bf16[2,4,16,4,2048]{2,3,1,0,4:T(4,128)(2,1)} copy(bf16[2,4,16,4,2048]{4,3,2,1,0:T(4,128)(2,1)S(1)} %broadcast_multiply_fusion) | data formatting | bytes 4194304 | tf_op jit(solution)/shard_map/mul | solution.py:57
  26.5 20.8 %reshape.271 = bf16[16,2,32768]{2,1,0:T(2,128)(2,1)} reshape(bf16[2048,2,4,4,16]{4,3,2,1,0:T(4,128)(2,1)} %bitcast.233) | data formatting | bytes 4194304
  47.3 8.0 %all-to-all-start = ((bf16[16,2,32768]{2,1,0:T(2,128)(2,1)}), bf16[16,2,32768]{2,1,0:T(2,128)(2,1)S(1)}, u32[]{:S(2)}, u32[]{:S(2)}) async-start(bf16[16,2,32768]{2,1,0:T(2,128)(2,1)} %reshape.271), calls=%async_computation | async-start | bytes 4194304 | tf_op jit(solution)/shard_map/all_to_all | solution.py:58
  62.0 69.0 %cosine_convert_fusion = (bf16[2048,2048]{1,0:T(8,128)(2,1)}, bf16[2048,2048]{1,0:T(8,128)(2,1)}) fusion(s32[2048]{0:T(1024)S(1)} %add_select_fusion.1), kind=kLoop, calls=%fused_computation.24 | loop fusion | flops 71303168 | bytes 16785408 | tf_op jit(solution)/shard_map/convert.6
  131.0 14.3 %reshape.272 = bf16[2048,2,4,4,16]{4,3,2,1,0:T(4,128)(2,1)} reshape(bf16[16,2,32768]{2,1,0:T(2,128)(2,1)S(1)} %all-to-all-done) | data formatting | bytes 4194304
  145.3 20.5 %copy.166 = bf16[2,4,16,4,16,128]{5,2,3,4,1,0:T(8,128)(2,1)S(1)} copy(bf16[2,4,16,4,16,128]{2,3,1,0,5,4:T(4,128)(2,1)} %bitcast.234) | data formatting | bytes 4194304 | tf_op jit(solution)/shard_map/all_to_all | solution.py:58
  193.2 8.9 %fusion.55 = f32[4,8,128,4,4]{4,3,2,1,0:T(4,128)} fusion(bf16[4,16,8,4,128]{1,3,4,2,0:T(4,128)(2,1)} %copy.167, bf16[4,16,8,4,128]{1,3,4,2,0:T(4,128)(2,1)} %copy.168), kind=kOutput, calls=%fused_computation.153 | convolution fusion | flops 2097152 | bytes 1310720 | tf_op jit(solution)/shard_map/dwpif,dwpjf->dpijf/dot_general | solution.py:23
  202.1 8.3 %fusion.57 = f32[4,8,128,4,4]{4,3,2,1,0:T(4,128)} fusion(bf16[4,16,8,4,128]{1,3,4,2,0:T(4,128)(2,1)S(1)} %copy-done, bf16[4,16,8,4,128]{1,3,4,2,0:T(4,128)(2,1)} %copy.170), kind=kOutput, calls=%fused_computation.155 | convolution fusion | flops 2097152 | bytes 1310720 | tf_op jit(solution)/shard_map/dwpif,dwpjf->dpijf/dot_general | solution.py:27
  210.5 8.5 %fusion.56 = f32[4,8,128,4,4]{4,3,2,1,0:T(4,128)} fusion(bf16[4,16,8,4,128]{1,3,4,2,0:T(4,128)(2,1)S(1)} %copy-done.8, bf16[4,16,8,4,128]{1,3,4,2,0:T(4,128)(2,1)} %copy.170), kind=kOutput, calls=%fused_computation.154 | convolution fusion | flops 2097152 | bytes 1310720 | tf_op jit(solution)/shard_map/dwpif,dwpjf->dpijf/dot_general | solution.py:24
  253.0 9.0 %fusion.59 = f32[4,8,128,4,4]{4,3,2,1,0:T(4,128)} fusion(bf16[4,16,8,4,128]{1,3,4,2,0:T(4,128)(2,1)} %copy.180, bf16[4,16,8,4,128]{1,3,4,2,0:T(4,128)(2,1)} %copy.181), kind=kOutput, calls=%fused_computation.157 | convolution fusion | flops 2097152 | bytes 1310720 | tf_op jit(solution)/shard_map/dwpif,dwpjf->dpijf/dot_general | solution.py:23
  262.0 8.3 %fusion.61 = f32[4,8,128,4,4]{4,3,2,1,0:T(4,128)} fusion(bf16[4,16,8,4,128]{1,3,4,2,0:T(4,128)(2,1)S(1)} %copy-done.1, bf16[4,16,8,4,128]{1,3,4,2,0:T(4,128)(2,1)} %copy.183), kind=kOutput, calls=%fused_computation.159 | convolution fusion | flops 2097152 | bytes 1310720 | tf_op jit(solution)/shard_map/dwpif,dwpjf->dpijf/dot_general | solution.py:27
  270.3 8.5 %fusion.60 = f32[4,8,128,4,4]{4,3,2,1,0:T(4,128)} fusion(bf16[4,16,8,4,128]{1,3,4,2,0:T(4,128)(2,1)S(1)} %copy-done.9, bf16[4,16,8,4,128]{1,3,4,2,0:T(4,128)(2,1)} %copy.183), kind=kOutput, calls=%fused_computation.158 | convolution fusion | flops 2097152 | bytes 1310720 | tf_op jit(solution)/shard_map/dwpif,dwpjf->dpijf/dot_general | solution.py:24
  313.0 9.0 %fusion.64 = f32[4,8,128,4,4]{4,3,2,1,0:T(4,128)} fusion(bf16[4,16,8,4,128]{1,3,4,2,0:T(4,128)(2,1)} %copy.194, bf16[4,16,8,4,128]{1,3,4,2,0:T(4,128)(2,1)} %copy.195), kind=kOutput, calls=%fused_computation.162 | convolution fusion | flops 2097152 | bytes 1310720 | tf_op jit(solution)/shard_map/dwpif,dwpjf->dpijf/dot_general | solution.py:24
  322.0 8.4 %fusion.66 = f32[4,8,128,4,4]{4,3,2,1,0:T(4,128)} fusion(bf16[4,16,8,4,128]{1,3,4,2,0:T(4,128)(2,1)S(1)} %copy-done.2, bf16[4,16,8,4,128]{1,3,4,2,0:T(4,128)(2,1)} %copy.193), kind=kOutput, calls=%fused_computation.164 | convolution fusion | flops 2097152 | bytes 1310720 | tf_op jit(solution)/shard_map/dwpif,dwpjf->dpijf/dot_general | solution.py:28
  330.3 8.8 %fusion.63 = f32[4,8,128,4,4]{4,3,2,1,0:T(4,128)} fusion(bf16[4,16,8,4,128]{1,3,4,2,0:T(4,128)(2,1)S(1)} %copy-done.10, bf16[4,16,8,4,128]{1,3,4,2,0:T(4,128)(2,1)} %copy.193), kind=kOutput, calls=%fused_computation.161 | convolution fusion | flops 2097152 | bytes 1310720 | tf_op jit(solution)/shard_map/dwpif,dwpjf->dpijf/dot_general | solution.py:23
  368.6 8.9 %fusion.68 = f32[4,8,128,4,4]{4,3,2,1,0:T(4,128)} fusion(bf16[4,16,8,4,128]{1,3,4,2,0:T(4,128)(2,1)} %copy.206, bf16[4,16,8,4,128]{1,3,4,2,0:T(4,128)(2,1)} %copy.207), kind=kOutput, calls=%fused_computation.166 | convolution fusion | flops 2097152 | bytes 1310720 | tf_op jit(solution)/shard_map/dwpif,dwpjf->dpijf/dot_general | solution.py:24
  397.6 8.6 %fusion.20 = bf16[1,4,8,4,4,128]{3,4,5,2,1,0:T(4,128)(2,1)} fusion(f32[4,8,128,4,4]{4,3,2,1,0:T(4,128)} %fusion.55, f32[4,8,128,4,4]{4,3,2,1,0:T(4,128)} %fusion.56, f32[4,8]{1,0:T(4,128)S(1)} %maximum_divide_fusion.3), kind=kOutput, calls=%fused_computation.42 | output fusion | flops 327680 | bytes 655488 | tf_op jit(solution)/shard_map/jit(cumsum)/reduce_window_sum | solution.py:35
  410.9 8.7 %fusion.18 = bf16[1,4,8,4,4,128]{3,4,5,2,1,0:T(4,128)(2,1)} fusion(f32[4,8,128,4,4]{4,3,2,1,0:T(4,128)} %fusion.57, f32[4,8,128,4,4]{4,3,2,1,0:T(4,128)} %fusion.58, f32[4,8]{1,0:T(4,128)S(1)} %maximum_divide_fusion.3), kind=kOutput, calls=%fused_computation.40 | output fusion | flops 327680 | bytes 655488 | tf_op jit(solution)/shard_map/jit(cumsum)/reduce_window_sum | solution.py:36
  431.5 8.6 %fusion.16 = bf16[1,4,8,4,4,128]{3,4,5,2,1,0:T(4,128)(2,1)} fusion(f32[4,8,128,4,4]{4,3,2,1,0:T(4,128)} %fusion.59, f32[4,8,128,4,4]{4,3,2,1,0:T(4,128)} %fusion.60, f32[4,8]{1,0:T(4,128)S(1)} %maximum_divide_fusion.2), kind=kOutput, calls=%fused_computation.38 | output fusion | flops 327680 | bytes 655488 | tf_op jit(solution)/shard_map/jit(cumsum)/reduce_window_sum | solution.py:35
  444.7 8.7 %fusion.14 = bf16[1,4,8,4,4,128]{3,4,5,2,1,0:T(4,128)(2,1)} fusion(f32[4,8,128,4,4]{4,3,2,1,0:T(4,128)} %fusion.61, f32[4,8,128,4,4]{4,3,2,1,0:T(4,128)} %fusion.62, f32[4,8]{1,0:T(4,128)S(1)} %maximum_divide_fusion.2), kind=kOutput, calls=%fused_computation.36 | output fusion | flops 327680 | bytes 655488 | tf_op jit(solution)/shard_map/jit(cumsum)/reduce_window_sum | solution.py:36
  459.0 8.6 %fusion.12 = bf16[1,4,8,4,4,128]{3,4,5,2,1,0:T(4,128)(2,1)} fusion(f32[4,8,128,4,4]{4,3,2,1,0:T(4,128)} %fusion.63, f32[4,8,128,4,4]{4,3,2,1,0:T(4,128)} %fusion.64, f32[4,8]{1,0:T(4,128)S(1)} %copy-done.15), kind=kOutput, calls=%fused_computation.34 | output fusion | flops 327680 | bytes 655488 | tf_op jit(solution)/shard_map/jit(cumsum)/reduce_window_sum | solution.py:35
  467.6 8.8 %fusion.10 = bf16[1,4,8,4,4,128]{3,4,5,2,1,0:T(4,128)(2,1)} fusion(f32[4,8,128,4,4]{4,3,2,1,0:T(4,128)} %fusion.65, f32[4,8,128,4,4]{4,3,2,1,0:T(4,128)} %fusion.66, f32[4,8]{1,0:T(4,128)S(1)} %copy-done.15), kind=kOutput, calls=%fused_computation.32 | output fusion | flops 327680 | bytes 655488 | tf_op jit(solution)/shard_map/jit(cumsum)/reduce_window_sum | solution.py:36
  476.4 8.6 %fusion.8 = bf16[1,4,8,4,4,128]{3,4,5,2,1,0:T(4,128)(2,1)} fusion(f32[4,8,128,4,4]{4,3,2,1,0:T(4,128)} %fusion.67, f32[4,8,128,4,4]{4,3,2,1,0:T(4,128)} %fusion.68, f32[4,8]{1,0:T(4,128)S(1)} %copy-done.14), kind=kOutput, calls=%fused_computation.30 | output fusion | flops 327680 | bytes 655488 | tf_op jit(solution)/shard_map/jit(cumsum)/reduce_window_sum | solution.py:35
  491.4 8.8 %fusion.6 = bf16[1,4,8,4,4,128]{3,4,5,2,1,0:T(4,128)(2,1)} fusion(f32[4,8,128,4,4]{4,3,2,1,0:T(4,128)} %fusion.69, f32[4,8,128,4,4]{4,3,2,1,0:T(4,128)} %fusion.70, f32[4,8]{1,0:T(4,128)S(1)} %copy-done.14), kind=kOutput, calls=%fused_computation.28 | output fusion | flops 327680 | bytes 655488 | tf_op jit(solution)/shard_map/jit(cumsum)/reduce_window_sum | solution.py:36
  (150 shorter events, 256.3 us)
Async XLA Ops:
  26.5 28.8 %copy-start.16 = (s32[4,8,2]{1,2,0:T(2,128)S(1)}, s32[4,8,2]{1,2,0:T(2,128)}, u32[]{:S(2)}) copy-start(s32[4,8,2]{1,2,0:T(2,128)} %param.11) | copy-start | bytes 772
  26.5 28.8 %copy-start.13 = (s32[4,16,16]{2,1,0:T(8,128)S(1)}, s32[4,16,16]{2,1,0:T(8,128)}, u32[]{:S(2)}) copy-start(s32[4,16,16]{2,1,0:T(8,128)} %param.10) | copy-start | bytes 12292
  47.3 83.7 %all-to-all-start = ((bf16[16,2,32768]{2,1,0:T(2,128)(2,1)}), bf16[16,2,32768]{2,1,0:T(2,128)(2,1)S(1)}, u32[]{:S(2)}, u32[]{:S(2)}) async-start(bf16[16,2,32768]{2,1,0:T(2,128)(2,1)} %reshape.271), calls=%async_computation | async-start | bytes 4194304 | tf_op jit(solution)/shard_map/all_to_all | solution.py:58
  193.2 9.0 %copy-start = (bf16[4,16,8,4,128]{1,3,4,2,0:T(4,128)(2,1)S(1)}, bf16[4,16,8,4,128]{1,3,4,2,0:T(4,128)(2,1)}, u32[]{:S(2)}) copy-start(bf16[4,16,8,4,128]{1,3,4,2,0:T(4,128)(2,1)} %copy.167) | copy-start | bytes 1572868
  202.1 8.3 %copy-start.8 = (bf16[4,16,8,4,128]{1,3,4,2,0:T(4,128)(2,1)S(1)}, bf16[4,16,8,4,128]{1,3,4,2,0:T(4,128)(2,1)}, u32[]{:S(2)}) copy-start(bf16[4,16,8,4,128]{1,3,4,2,0:T(4,128)(2,1)} %copy.169) | copy-start | bytes 1572868
  210.5 8.5 %copy-start.4 = (bf16[4,16,8,4,128]{1,3,4,2,0:T(4,128)(2,1)S(1)}, bf16[4,16,8,4,128]{1,3,4,2,0:T(4,128)(2,1)}, u32[]{:S(2)}) copy-start(bf16[4,16,8,4,128]{1,3,4,2,0:T(4,128)(2,1)} %copy.168) | copy-start | bytes 1572868
  253.0 9.0 %copy-start.1 = (bf16[4,16,8,4,128]{1,3,4,2,0:T(4,128)(2,1)S(1)}, bf16[4,16,8,4,128]{1,3,4,2,0:T(4,128)(2,1)}, u32[]{:S(2)}) copy-start(bf16[4,16,8,4,128]{1,3,4,2,0:T(4,128)(2,1)} %copy.180) | copy-start | bytes 1572868
  262.0 8.4 %copy-start.9 = (bf16[4,16,8,4,128]{1,3,4,2,0:T(4,128)(2,1)S(1)}, bf16[4,16,8,4,128]{1,3,4,2,0:T(4,128)(2,1)}, u32[]{:S(2)}) copy-start(bf16[4,16,8,4,128]{1,3,4,2,0:T(4,128)(2,1)} %copy.182) | copy-start | bytes 1572868
  270.3 8.5 %copy-start.5 = (bf16[4,16,8,4,128]{1,3,4,2,0:T(4,128)(2,1)S(1)}, bf16[4,16,8,4,128]{1,3,4,2,0:T(4,128)(2,1)}, u32[]{:S(2)}) copy-start(bf16[4,16,8,4,128]{1,3,4,2,0:T(4,128)(2,1)} %copy.181) | copy-start | bytes 1572868
  313.0 9.0 %copy-start.2 = (bf16[4,16,8,4,128]{1,3,4,2,0:T(4,128)(2,1)S(1)}, bf16[4,16,8,4,128]{1,3,4,2,0:T(4,128)(2,1)}, u32[]{:S(2)}) copy-start(bf16[4,16,8,4,128]{1,3,4,2,0:T(4,128)(2,1)} %copy.194) | copy-start | bytes 1572868
  322.0 8.4 %copy-start.10 = (bf16[4,16,8,4,128]{1,3,4,2,0:T(4,128)(2,1)S(1)}, bf16[4,16,8,4,128]{1,3,4,2,0:T(4,128)(2,1)}, u32[]{:S(2)}) copy-start(bf16[4,16,8,4,128]{1,3,4,2,0:T(4,128)(2,1)} %copy.192) | copy-start | bytes 1572868
  330.3 8.8 %copy-start.6 = (bf16[4,16,8,4,128]{1,3,4,2,0:T(4,128)(2,1)S(1)}, bf16[4,16,8,4,128]{1,3,4,2,0:T(4,128)(2,1)}, u32[]{:S(2)}) copy-start(bf16[4,16,8,4,128]{1,3,4,2,0:T(4,128)(2,1)} %copy.195) | copy-start | bytes 1572868
  368.6 8.9 %copy-start.3 = (bf16[4,16,8,4,128]{1,3,4,2,0:T(4,128)(2,1)S(1)}, bf16[4,16,8,4,128]{1,3,4,2,0:T(4,128)(2,1)}, u32[]{:S(2)}) copy-start(bf16[4,16,8,4,128]{1,3,4,2,0:T(4,128)(2,1)} %copy.206) | copy-start | bytes 1572868
  368.6 8.9 %copy-start.12 = (bf16[4,16,8,4,128]{1,3,4,2,0:T(4,128)(2,1)S(1)}, bf16[4,16,8,4,128]{1,3,4,2,0:T(4,128)(2,1)}, u32[]{:S(2)}) copy-start(bf16[4,16,8,4,128]{1,3,4,2,0:T(4,128)(2,1)} %copy.205) | copy-start | bytes 1572868
  377.5 6.7 %copy-start.11 = (bf16[4,16,8,4,128]{1,3,4,2,0:T(4,128)(2,1)S(1)}, bf16[4,16,8,4,128]{1,3,4,2,0:T(4,128)(2,1)}, u32[]{:S(2)}) copy-start(bf16[4,16,8,4,128]{1,3,4,2,0:T(4,128)(2,1)} %copy.204) | copy-start | bytes 1572868
  384.3 6.8 %copy-start.7 = (bf16[4,16,8,4,128]{1,3,4,2,0:T(4,128)(2,1)S(1)}, bf16[4,16,8,4,128]{1,3,4,2,0:T(4,128)(2,1)}, u32[]{:S(2)}) copy-start(bf16[4,16,8,4,128]{1,3,4,2,0:T(4,128)(2,1)} %copy.207) | copy-start | bytes 1572868
  425.1 59.9 %all-to-all-start.1 = ((bf16[32,16,2,128]{3,1,2,0:T(8,128)(2,1)}), bf16[32,16,2,128]{3,1,2,0:T(8,128)(2,1)S(1)}, u32[]{:S(2)}, u32[]{:S(2)}) async-start(bf16[32,16,2,128]{3,1,2,0:T(8,128)(2,1)} %bitcast.28), calls=%async_computation.1 | async-start | bytes 524288 | tf_op jit(solution)/shard_map/all_to_all | solution.py:72
  444.7 14.2 %copy-start.15 = (f32[4,8]{1,0:T(4,128)S(1)}, f32[4,8]{1,0:T(4,128)}, u32[]{:S(2)}) copy-start(f32[4,8]{1,0:T(4,128)} %maximum_divide_fusion.1) | copy-start | bytes 388
  467.6 8.8 %copy-start.14 = (f32[4,8]{1,0:T(4,128)S(1)}, f32[4,8]{1,0:T(4,128)}, u32[]{:S(2)}) copy-start(f32[4,8]{1,0:T(4,128)} %maximum_divide_fusion) | copy-start | bytes 388
  485.1 35.8 %all-to-all-start.2 = ((bf16[32,16,2,128]{3,1,2,0:T(8,128)(2,1)}), bf16[32,16,2,128]{3,1,2,0:T(8,128)(2,1)S(1)}, u32[]{:S(2)}, u32[]{:S(2)}) async-start(bf16[32,16,2,128]{3,1,2,0:T(8,128)(2,1)} %bitcast.49), calls=%async_computation.2 | async-start | bytes 524288 | tf_op jit(solution)/shard_map/all_to_all | solution.py:72
  520.9 21.2 %all-to-all-start.3 = ((bf16[32,16,2,128]{3,1,2,0:T(8,128)(2,1)}), bf16[32,16,2,128]{3,1,2,0:T(8,128)(2,1)S(1)}, u32[]{:S(2)}, u32[]{:S(2)}) async-start(bf16[32,16,2,128]{3,1,2,0:T(8,128)(2,1)} %bitcast.70), calls=%async_computation.3 | async-start | bytes 524288 | tf_op jit(solution)/shard_map/all_to_all | solution.py:72
  542.0 15.5 %all-to-all-start.4 = ((bf16[32,16,2,128]{3,1,2,0:T(8,128)(2,1)}), bf16[32,16,2,128]{3,1,2,0:T(8,128)(2,1)S(1)}, u32[]{:S(2)}, u32[]{:S(2)}) async-start(bf16[32,16,2,128]{3,1,2,0:T(8,128)(2,1)} %bitcast.91), calls=%async_computation.4 | async-start | bytes 524288 | tf_op jit(solution)/shard_map/all_to_all | solution.py:72
where the time goes:
time: 573 us; the launch traced here: 567 us
  local copies, waits for them, and re-layouts  221 us (39%)
  matrix products  156 us (27%)
  other arithmetic  154 us (27%)
  starting transfers between devices  32.7 us (6%)
    another operation x1, other arithmetic  69 us
    another operation x8, local copies, waits for them, and re-layouts  37.2 us
    unnamed x38, local copies, waits for them, and re-layouts  35.3 us
    another operation x4, other arithmetic, cross_local(): imag_part = jnp.cumsum(imag_part * inverse[:, :, None, None, None], axis=0)  35.1 us
    dot_general x4, matrix products, cross_local(): jnp.einsum(pattern, left[1], right[1], preferred_element_type=jnp.float32)  34.9 us
    another operation x4, other arithmetic, cross_local(): real_part = jnp.cumsum(real_part * inverse[:, :, None, None, None], axis=0)  34.5 us
    dot_general x4, matrix products, cross_local(): jnp.einsum(pattern, left[0], right[0], preferred_element_type=jnp.float32)  33.4 us
    dot_general x4, matrix products, cross_local(): jnp.einsum(pattern, left[1], right[0], preferred_element_type=jnp.float32)  30 us
  transfers between devices with their start and end apart: 5, of which 1 were waited for; matrix products, arithmetic and copies ran while one was open for 32% of the time, Pallas kernels for 0%

commit v1 on v0

v1 whole, which is shorter than its diff:
```python
import functools
import math

import jax
import jax.numpy as jnp
import ml_dtypes
import numpy as np
from jax import lax
from jax.experimental import pallas as pl
from jax.experimental.pallas import tpu as pltpu
from jax.sharding import PartitionSpec as P

LAGS = 2048
MIB = 1 << 20


def phase_table(freq_count, lag_count, devices):
    freqs = np.arange(freq_count, dtype=np.int64)
    shifts = np.mod(np.arange(lag_count, dtype=np.int64) - lag_count // 2, 2 * freq_count)
    phases = np.mod(freqs[:, None] * shifts[None, :], 2 * freq_count)
    angles = np.arange(2 * freq_count) * (math.pi / freq_count)
    cosines = np.cos(angles).astype(np.float32).astype(ml_dtypes.bfloat16)[phases]
    sines = (-np.sin(angles)).astype(np.float32).astype(ml_dtypes.bfloat16)[phases]
    bins = freq_count // devices
    both = np.stack([cosines, sines]).reshape(2, devices, bins, lag_count)
    return np.ascontiguousarray(both.transpose(1, 0, 2, 3)).reshape(2 * freq_count, lag_count)


def pack_kernel(devices, counts_ref, masks_ref, spectra_ref, out_ref, rows_ref):
    me = lax.axis_index("sta")
    windows, slots = spectra_ref.shape[2], spectra_ref.shape[3]
    bins = out_ref.shape[-1]
    count = counts_ref[me]
    lane = lax.broadcasted_iota(jnp.int32, masks_ref.shape[1:], 1)
    mine = jnp.where(lane == me, masks_ref[0], 0)
    keep = (jnp.sum(mine, axis=1, keepdims=True) > 0).astype(jnp.float32)
    for owner in range(devices):
        for w in range(windows):
            rows_ref[owner, w * slots : (w + 1) * slots, :] = spectra_ref[
                0, 0, w, :, owner * bins : (owner + 1) * bins
            ].astype(jnp.float32)
    for slot in range(slots):
        live = keep * jnp.where(slot < count, 1.0, 0.0)
        wide = jnp.broadcast_to(live, (windows, bins))
        for owner in range(devices):
            picked = rows_ref[owner, pl.ds(slot, windows, stride=slots), :]
            out_ref[owner, 0, 0, slot] = (picked * wide).astype(jnp.bfloat16)


def pack(spectra, block_counts, window_masks, devices):
    parts, days, windows, slots, total = spectra.shape
    bins = total // devices
    return pl.pallas_call(
        functools.partial(pack_kernel, devices),
        grid=(parts, days),
        in_specs=[
            pl.BlockSpec(memory_space=pltpu.SMEM),
            pl.BlockSpec((1,) + window_masks.shape[1:], lambda c, d: (d, 0, 0)),
            pl.BlockSpec((1, 1, windows, slots, total), lambda c, d: (c, d, 0, 0, 0)),
        ],
        out_specs=pl.BlockSpec(
            (devices, 1, 1, slots, windows, bins), lambda c, d: (0, c, d, 0, 0, 0)
        ),
        out_shape=jax.ShapeDtypeStruct(
            (devices, parts, days, slots, windows, bins), jnp.bfloat16
        ),
        scratch_shapes=[pltpu.VMEM((devices, windows * slots, bins), jnp.float32)],
        compiler_params=pltpu.CompilerParams(vmem_limit_bytes=32 * MIB),
        name="pack",
    )(block_counts, window_masks, spectra)


def window_sums(terms, rows):
    for step in (1, 2, 4):
        own = (rows & step) == 0
        terms = [
            jnp.where(own, first, second) + pltpu.roll(jnp.where(own, second, first), 8 - step, 0)
            for first, second in zip(terms[::2], terms[1::2])
        ]
    return terms[0]


def cross_kernel(pairs_ref, inverse_ref, blocks_ref, out_ref):
    days, slots = blocks_ref.shape[2], blocks_ref.shape[3]
    bins = blocks_ref.shape[-1]
    block_count = blocks_ref.shape[0]
    rounds, pairs = pairs_ref.shape[0], pairs_ref.shape[1]
    rows = lax.broadcasted_iota(jnp.int32, (8, bins), 0)
    held = days * pairs // block_count

    def one_pair(index, carry):
        r, p = index // pairs, index % pairs
        a, b = pairs_ref[r, p, 0], pairs_ref[r, p, 1]
        total = None
        for d in range(days):
            scale = inverse_ref[(d * block_count + a) * block_count + b]
            left = [[blocks_ref[a, c, d, s].astype(jnp.float32) for s in range(slots)] for c in range(2)]
            right = [[blocks_ref[b, c, d, s].astype(jnp.float32) for s in range(slots)] for c in range(2)]
            fresh = []
            for half in range(slots * slots // 8):
                real, imag = [], []
                for k in range(8):
                    i, j = divmod(half * 8 + k, slots)
                    re = left[0][i] * right[0][j] + left[1][i] * right[1][j]
                    im = left[1][i] * right[0][j] - left[0][i] * right[1][j]
                    real.append(re[:8] + re[8:])
                    imag.append(im[:8] + im[8:])
                fresh.append((window_sums(real, rows) * scale, window_sums(imag, rows) * scale))
            if total is None:
                total = fresh
            else:
                total = [(t[0] + n[0], t[1] + n[1]) for t, n in zip(total, fresh)]
            row = pl.multiple_of(r * held * slots * slots + (d % held) * slots * slots, 16)
            place = (p * days + d) // held
            for c in range(2):
                out_ref[place, c, pl.ds(row, slots * slots), :] = jnp.concatenate(
                    [t[c] for t in total], axis=0
                ).astype(jnp.bfloat16)
        return carry

    lax.fori_loop(0, rounds * pairs, one_pair, 0)


def cross(blocks, inverse, pair_table):
    devices, parts, days, slots, windows, bins = blocks.shape
    rounds, pairs, _ = pair_table.shape
    held = days * pairs // devices
    return pl.pallas_call(
        cross_kernel,
        in_specs=[
            pl.BlockSpec(memory_space=pltpu.SMEM),
            pl.BlockSpec(memory_space=pltpu.SMEM),
            pl.BlockSpec(memory_space=pltpu.VMEM),
        ],
        out_specs=pl.BlockSpec(memory_space=pltpu.VMEM),
        out_shape=jax.ShapeDtypeStruct(
            (devices, parts, rounds * held * slots * slots, bins), jnp.bfloat16
        ),
        compiler_params=pltpu.CompilerParams(vmem_limit_bytes=40 * MIB),
        name="cross",
    )(pair_table, inverse, blocks)


def lag_kernel(scale, stacked_ref, table_ref, out_ref, left_ref):
    devices, parts, rows, bins = stacked_ref.shape

    @pl.when(pl.program_id(0) == 0)
    def _():
        for src in range(devices):
            for c in range(parts):
                at = (src * parts + c) * bins
                left_ref[:, at : at + bins] = stacked_ref[src, c]

    out_ref[...] = (
        jnp.dot(left_ref[...], table_ref[...], preferred_element_type=jnp.float32) * scale
    )


def lags(stacked, table, scale):
    devices, parts, rows, bins = stacked.shape
    depth, lag_count = table.shape
    tile = 256
    return pl.pallas_call(
        functools.partial(lag_kernel, scale),
        grid=(lag_count // tile,),
        in_specs=[
            pl.BlockSpec((devices, parts, rows, bins), lambda t: (0, 0, 0, 0)),
            pl.BlockSpec((depth, tile), lambda t: (0, t)),
        ],
        out_specs=pl.BlockSpec((rows, tile), lambda t: (0, t)),
        out_shape=jax.ShapeDtypeStruct((rows, lag_count), jnp.float32),
        scratch_shapes=[pltpu.VMEM((rows, depth), jnp.bfloat16)],
        compiler_params=pltpu.CompilerParams(vmem_limit_bytes=32 * MIB),
        name="lags",
    )(stacked, table)


def local(table, spectra, block_counts, window_masks, pair_table):
    devices = lax.axis_size("sta")
    parts, days, windows, slots, total = spectra.shape
    rounds, pairs, _ = pair_table.shape
    held = days * pairs // devices
    packed = pack(spectra, block_counts, window_masks, devices)
    blocks = lax.all_to_all(packed, "sta", split_axis=0, concat_axis=0, tiled=True)
    weights = window_masks.astype(jnp.float32)
    joint = jnp.einsum("dwa,dwb->dab", weights, weights)
    inverse = (1.0 / jnp.maximum(joint, 1.0)).reshape(-1)
    stacked = cross(blocks, inverse, pair_table)
    received = lax.all_to_all(stacked, "sta", split_axis=0, concat_axis=0, tiled=True)
    lagged = lags(received, table, 1.0 / math.sqrt(total))
    return lagged.reshape(rounds, held, slots * slots, LAGS)


def solution(mesh):
    devices = mesh.shape["sta"]
    placed = (P(None, "grp", None, "sta", None), P(), P("grp", None, None), P())

    def run(spectra, block_counts, window_masks, pair_table):
        table = phase_table(spectra.shape[-1], LAGS, devices)
        return jax.shard_map(
            functools.partial(local, table),
            mesh=mesh,
            in_specs=placed,
            out_specs=P("grp", "sta", None, None),
            check_vma=False,
        )(spectra, block_counts, window_masks, pair_table)

    return run
```

time: 573 us -> 112 us (0.20); the launches traced: 567 us -> 112 us
  local copies, waits for them, and re-layouts: 221 us -> 10.3 us
  matrix products: 156 us -> 0.2 us
  other arithmetic: 154 us -> 0 us
  waiting for transfers between devices: 1.78 us -> 41.1 us
  blocking collectives: 0 us -> 35.9 us
  starting transfers between devices: 32.7 us -> 7.48 us
  Pallas kernels: 0 us -> 16.8 us
    dot_general x20 -> x1, matrix products: 156 us -> 0.2 us  [local(): joint = jnp.einsum('dwa,dwb->dab', weights, weights)]
    another operation x10 -> x0, other arithmetic: 140 us -> none
    squeeze x24 -> x0, local copies, waits for them, and re-layouts: 86.7 us -> none  [the longest x8 28.9 us: cross_local(): left[0]]
    all_to_all x5 -> x1, waiting for transfers between devices: 1.78 us -> 41.1 us  [local(): lax.all_to_all(packed, 'sta', split_axis=0, concat_axis=0, tiled=True)]
    another operation x8 -> x0, local copies, waits for them, and re-layouts: 37.2 us -> none
    all_to_all x0 -> x1, blocking collectives: none -> 35.9 us  [local(): lax.all_to_all(stacked, 'sta', split_axis=0, concat_axis=0, tiled=True)]
    all_to_all x5 -> x1, starting transfers between devices: 32.7 us -> 7.48 us  [local(): lax.all_to_all(packed, 'sta', split_axis=0, concat_axis=0, tiled=True)]
    unnamed x38 -> x15, local copies, waits for them, and re-layouts: 35.3 us -> 10.2 us
  transfers between devices with their start and end apart: 5 -> 1, of which waited for: 1 -> 1; matrix products, arithmetic and copies ran while one was open for 32% -> 0% of each run, Pallas kernels for 0% -> 0%
where the time goes in v1:
time: 112 us
  waiting for transfers between devices  41.1 us (37%)
  blocking collectives  35.9 us (32%)
  Pallas kernels  16.8 us (15%)
  local copies, waits for them, and re-layouts  10.3 us (9%)
  starting transfers between devices  7.48 us (7%)
    all_to_all x1, waiting for transfers between devices, local(): lax.all_to_all(packed, 'sta', split_axis=0, concat_axis=0, tiled=True)  41.1 us
    all_to_all x1, blocking collectives, local(): lax.all_to_all(stacked, 'sta', split_axis=0, concat_axis=0, tiled=True)  35.9 us
    unnamed x15, local copies, waits for them, and re-layouts  10.2 us
    pallas_call x1, Pallas kernels, cross(): pl.pallas_call(cross_kernel, in_specs=[pl.BlockSpec(memory_space=pltpu.SM...  7.92 us
    all_to_all x1, starting transfers between devices, local(): lax.all_to_all(packed, 'sta', split_axis=0, concat_axis=0, tiled=True)  7.48 us
    pallas_call x1, Pallas kernels, lags(): pl.pallas_call(functools.partial(lag_kernel, scale), grid=(lag_count // t...  7.02 us
  transfers between devices with their start and end apart: 1, of which 1 were waited for; matrix products, arithmetic and copies ran while one was open for 0% of the time, Pallas kernels for 0%

profile of v1, /device:TPU:1, one launch (start us, length us, event | category | flops | bytes accessed | tf_op | source)
XLA Modules:
  0.0 111.8 jit_solution(245886400619353576)
XLA Ops:
  0.0 0.0 copy-start.2
  0.0 1.6 %copy-done.2 = bf16[2,4,16,4,2048]{4,3,2,1,0:T(4,128)(2,1)S(1)} copy-done((bf16[2,4,16,4,2048]{4,3,2,1,0:T(4,128)(2,1)S(1)}, bf16[2,4,16,4,2048]{4,3,2,1,0:T(4,128)(2,1)}, u32[]{:S(2)}) %copy-start.2) | copy-done | bytes 2097176
  1.6 0.0 copy-start.3
  1.6 0.8 copy-done.3
  2.4 0.0 copy-start.5
  2.4 0.7 copy-done.5
  3.0 1.9 %pack.1 = bf16[16,2,4,4,16,128]{5,4,3,2,1,0:T(8,128)(2,1)S(1)} custom-call(s32[16]{0:T(128)S(1)} %copy-done.5, s32[4,16,16]{2,1,0:T(8,128)S(1)} %copy-done.3, bf16[2,4,16,4,2048]{4,3,2,1,0:T(4,128)(2,1)S(1)} %copy-done.2), custom_call_target="tpu_custom_call" | custom-call | tf_op jit(solution)/shard_map/pack/pallas_call | solution.py:53
  4.9 0.0 copy-start.1
  4.9 1.3 %copy-done.1 = bf16[16,2,4,4,16,128]{5,4,3,2,1,0:T(8,128)(2,1)} copy-done((bf16[16,2,4,4,16,128]{5,4,3,2,1,0:T(8,128)(2,1)}, bf16[16,2,4,4,16,128]{5,4,3,2,1,0:T(8,128)(2,1)S(1)}, u32[]{:S(2)}) %copy-start.1) | copy-done | bytes 2097176
  6.2 0.0 copy-start.4
  6.2 0.0 copy-start.6
  6.2 7.5 %all-to-all-start = ((bf16[16,2,4,4,16,128]{5,4,3,2,1,0:T(8,128)(2,1)}), bf16[16,2,4,4,16,128]{5,4,3,2,1,0:T(8,128)(2,1)S(1)}, u32[]{:S(2)}, u32[]{:S(2)}) async-start(bf16[16,2,4,4,16,128]{5,4,3,2,1,0:T(8,128)(2,1)} %copy-done.1), calls=%async_computation | async-start | bytes 4194304 | tf_op jit(solution)/shard_map/all_to_all | solution.py:184
  13.7 0.0 copy-done.4
  13.7 0.2 fusion
  13.9 0.1 reshape.6.inverse_ref
  14.0 0.0 copy-done.6
  14.0 0.1 copy.7.pairs_ref
  14.1 41.1 %all-to-all-done.blocks_ref = bf16[16,2,4,4,16,128]{5,4,3,2,1,0:T(8,128)(2,1)S(1)} async-done(((bf16[16,2,4,4,16,128]{5,4,3,2,1,0:T(8,128)(2,1)}), bf16[16,2,4,4,16,128]{5,4,3,2,1,0:T(8,128)(2,1)S(1)}, u32[]{:S(2)}, u32[]{:S(2)}) %all-to-all-start) | async-done | bytes 2097184 | tf_op jit(solution)/shard_map/all_to_all | solution.py:184
  55.2 7.9 %cross.1 = bf16[16,2,128,128]{3,2,1,0:T(8,128)(2,1)S(1)} custom-call(s32[4,8,2]{2,1,0:T(8,128)S(1)} %copy.7.pairs_ref, f32[1024]{0:T(1024)S(1)} %reshape.6.inverse_ref, bf16[16,2,4,4,16,128]{5,4,3,2,1,0:T(8,128)(2,1)S(1)} %all-to-all-done.blocks_ref), custom_call_target="tpu_custom_call" | custom-call | tf_op jit(solution)/shard_map/cross/pallas_call | solution.py:128
  63.1 35.9 %all_to_all.10.stacked_ref = bf16[16,2,128,128]{3,2,1,0:T(8,128)(2,1)S(1)} all-to-all(bf16[16,2,128,128]{3,2,1,0:T(8,128)(2,1)S(1)} %cross.1), channel_id=1, replica_groups=mesh['grp'=2,'sta'=16] {'sta'}, dimensions={0} | all-to-all | bytes 2097152 | tf_op jit(solution)/shard_map/all_to_all | solution.py:189
  99.0 0.0 copy-start
  99.0 5.8 %copy-done = bf16[4096,2048]{1,0:T(8,128)(2,1)S(1)} copy-done((bf16[4096,2048]{1,0:T(8,128)(2,1)S(1)}, bf16[4096,2048]{1,0:T(8,128)(2,1)}, u32[]{:S(2)}) %copy-start) | copy-done | bytes 16777240
  104.7 7.0 %lags.1 = f32[128,2048]{1,0:T(8,128)} custom-call(bf16[16,2,128,128]{3,2,1,0:T(8,128)(2,1)S(1)} %all_to_all.10.stacked_ref, bf16[4096,2048]{1,0:T(8,128)(2,1)S(1)} %copy-done), custom_call_target="tpu_custom_call" | custom-call | tf_op jit(solution)/shard_map/lags/pallas_call | solution.py:163
Async XLA Ops:
  0.0 1.6 %copy-start.2 = (bf16[2,4,16,4,2048]{4,3,2,1,0:T(4,128)(2,1)S(1)}, bf16[2,4,16,4,2048]{4,3,2,1,0:T(4,128)(2,1)}, u32[]{:S(2)}) copy-start(bf16[2,4,16,4,2048]{4,3,2,1,0:T(4,128)(2,1)} %spectra_ref.1) | copy-start | bytes 6291460
  1.6 0.8 copy-start.3
  2.4 0.7 copy-start.5
  4.9 1.3 %copy-start.1 = (bf16[16,2,4,4,16,128]{5,4,3,2,1,0:T(8,128)(2,1)}, bf16[16,2,4,4,16,128]{5,4,3,2,1,0:T(8,128)(2,1)S(1)}, u32[]{:S(2)}) copy-start(bf16[16,2,4,4,16,128]{5,4,3,2,1,0:T(8,128)(2,1)S(1)} %pack.1) | copy-start | bytes 6291460
  6.2 7.5 %copy-start.4 = (s32[4,16,16]{2,1,0:T(8,128)S(1)}, s32[4,16,16]{2,1,0:T(8,128)}, u32[]{:S(2)}) copy-start(s32[4,16,16]{2,1,0:T(8,128)} %masks_ref.1) | copy-start | bytes 12292
  6.2 7.8 %copy-start.6 = (s32[4,8,2]{1,2,0:T(2,128)S(1)}, s32[4,8,2]{1,2,0:T(2,128)}, u32[]{:S(2)}) copy-start(s32[4,8,2]{1,2,0:T(2,128)} %param.8) | copy-start | bytes 772
  6.2 48.9 %all-to-all-start = ((bf16[16,2,4,4,16,128]{5,4,3,2,1,0:T(8,128)(2,1)}), bf16[16,2,4,4,16,128]{5,4,3,2,1,0:T(8,128)(2,1)S(1)}, u32[]{:S(2)}, u32[]{:S(2)}) async-start(bf16[16,2,4,4,16,128]{5,4,3,2,1,0:T(8,128)(2,1)} %copy-done.1), calls=%async_computation | async-start | bytes 4194304 | tf_op jit(solution)/shard_map/all_to_all | solution.py:184
  99.0 5.8 %copy-start = (bf16[4096,2048]{1,0:T(8,128)(2,1)S(1)}, bf16[4096,2048]{1,0:T(8,128)(2,1)}, u32[]{:S(2)}) copy-start(bf16[4096,2048]{1,0:T(8,128)(2,1)} %constant.4.clone.table_ref) | copy-start | bytes 50331652

commit v2 on v1

v2 whole, which is shorter than its diff:
```python
import functools
import math

import jax
import jax.numpy as jnp
import ml_dtypes
import numpy as np
from jax import lax
from jax.experimental import pallas as pl
from jax.experimental.pallas import tpu as pltpu
from jax.sharding import PartitionSpec as P

LAGS = 2048
MIB = 1 << 20


def phase_tiles(freq_count, lag_count, tile):
    freqs = np.arange(freq_count, dtype=np.int64)
    shifts = np.arange(lag_count // 2, dtype=np.int64)
    phases = np.mod(freqs[:, None] * shifts[None, :], 2 * freq_count)
    angles = np.arange(2 * freq_count) * (math.pi / freq_count)
    cosines = np.cos(angles).astype(np.float32).astype(ml_dtypes.bfloat16)[phases]
    sines = (-np.sin(angles)).astype(np.float32).astype(ml_dtypes.bfloat16)[phases]
    both = np.stack([cosines, sines]).reshape(2, freq_count, -1, tile)
    return np.ascontiguousarray(both.transpose(2, 0, 1, 3))


def pack_kernel(
    devices, counts_ref, masks_ref, spectra_ref, out_ref, raw_ref, rows_ref, ready_ref, in_sems, out_sems
):
    me = lax.axis_index("sta")
    parts, days, windows, slots, _ = spectra_ref.shape
    bins = out_ref.shape[-1]
    count = counts_ref[me]

    def load(step):
        c, d = step // days, step % days
        return pltpu.make_async_copy(spectra_ref.at[c, d], raw_ref.at[c, d], in_sems.at[step])

    def store(step):
        c, d = step // days, step % days
        return pltpu.make_async_copy(ready_ref.at[:, c, d], out_ref.at[:, c, d], out_sems.at[step])

    for step in range(parts * days):
        load(step).start()
    lane = lax.broadcasted_iota(jnp.int32, masks_ref.shape[1:], 1)

    def one(step, carry):
        c, d = step // days, step % days
        mine = jnp.where(lane == me, masks_ref[d], 0)
        keep = (jnp.sum(mine, axis=1, keepdims=True) > 0).astype(jnp.float32)
        load(step).wait()
        for owner in range(devices):
            for w in range(windows):
                rows_ref[owner, w * slots : (w + 1) * slots, :] = raw_ref[
                    c, d, w, :, owner * bins : (owner + 1) * bins
                ].astype(jnp.float32)
        for slot in range(slots):
            live = keep * jnp.where(slot < count, 1.0, 0.0)
            wide = jnp.broadcast_to(live, (windows, bins))
            for owner in range(devices):
                picked = rows_ref[owner, pl.ds(slot, windows, stride=slots), :]
                ready_ref[owner, c, d, slot] = (picked * wide).astype(jnp.bfloat16)
        store(step).start()
        return carry

    lax.fori_loop(0, parts * days, one, 0)
    for step in range(parts * days):
        store(step).wait()


def pack(spectra, block_counts, window_masks, devices):
    parts, days, windows, slots, total = spectra.shape
    bins = total // devices
    packed = (devices, parts, days, slots, windows, bins)
    return pl.pallas_call(
        functools.partial(pack_kernel, devices),
        in_specs=[
            pl.BlockSpec(memory_space=pltpu.SMEM),
            pl.BlockSpec(memory_space=pltpu.VMEM),
            pl.BlockSpec(memory_space=pl.ANY),
        ],
        out_specs=pl.BlockSpec(memory_space=pl.ANY),
        out_shape=jax.ShapeDtypeStruct(packed, jnp.bfloat16),
        scratch_shapes=[
            pltpu.VMEM(spectra.shape, jnp.bfloat16),
            pltpu.VMEM((devices, windows * slots, bins), jnp.float32),
            pltpu.VMEM(packed, jnp.bfloat16),
            pltpu.SemaphoreType.DMA((parts * days,)),
            pltpu.SemaphoreType.DMA((parts * days,)),
        ],
        compiler_params=pltpu.CompilerParams(vmem_limit_bytes=60 * MIB),
        name="pack",
    )(block_counts, window_masks, spectra)


def window_sums(terms, rows):
    for step in (1, 2, 4):
        own = (rows & step) == 0
        terms = [
            jnp.where(own, first, second) + pltpu.roll(jnp.where(own, second, first), 8 - step, 0)
            for first, second in zip(terms[::2], terms[1::2])
        ]
    return terms[0]


def pair_stack(a, b, inverse_ref, blocks_ref, rows):
    block_count, _, days, slots = blocks_ref.shape[:4]
    total = None
    stacked = []
    for d in range(days):
        scale = inverse_ref[(d * block_count + a) * block_count + b]
        right = [[blocks_ref[b, c, d, s].astype(jnp.float32) for s in range(slots)] for c in range(2)]
        right_sum = [x + y for x, y in zip(right[0], right[1])]
        right_gap = [y - x for x, y in zip(right[0], right[1])]
        real, imag = [], []
        for i in range(slots):
            left_real = blocks_ref[a, 0, d, i].astype(jnp.float32)
            left_imag = blocks_ref[a, 1, d, i].astype(jnp.float32)
            left_sum = left_real + left_imag
            for j in range(slots):
                shared = left_sum * right[0][j]
                gain = left_imag * right_gap[j]
                loss = left_real * right_sum[j]
                both = shared[:8] + shared[8:]
                real.append(both + (gain[:8] + gain[8:]))
                imag.append(both - (loss[:8] + loss[8:]))
        fresh = [
            [window_sums(part[k : k + 8], rows) * scale for k in range(0, slots * slots, 8)]
            for part in (real, imag)
        ]
        if total is None:
            total = fresh
        else:
            total = [[t + n for t, n in zip(ts, ns)] for ts, ns in zip(total, fresh)]
        stacked.append([jnp.concatenate(part, axis=0).astype(jnp.bfloat16) for part in total])
    return stacked


def cross_kernel(pairs_ref, inverse_ref, blocks_ref, out_ref):
    block_count, _, days, slots, _, bins = blocks_ref.shape
    rounds, pairs = pairs_ref.shape[0], pairs_ref.shape[1]
    rows = lax.broadcasted_iota(jnp.int32, (8, bins), 0)
    held = days * pairs // block_count

    def one_pair(index, carry):
        r, p = index // pairs, index % pairs
        stacked = pair_stack(pairs_ref[r, p, 0], pairs_ref[r, p, 1], inverse_ref, blocks_ref, rows)
        for d in range(days):
            row = pl.multiple_of((r * held + d % held) * slots * slots, 16)
            for c in range(2):
                out_ref[(p * days + d) // held, c, pl.ds(row, slots * slots), :] = stacked[d][c]
        return carry

    lax.fori_loop(0, rounds * pairs, one_pair, 0)


def cross(blocks, inverse, pair_table):
    devices, parts, days, slots, windows, bins = blocks.shape
    rounds, pairs, _ = pair_table.shape
    held = days * pairs // devices
    return pl.pallas_call(
        cross_kernel,
        in_specs=[
            pl.BlockSpec(memory_space=pltpu.SMEM),
            pl.BlockSpec(memory_space=pltpu.SMEM),
            pl.BlockSpec(memory_space=pltpu.VMEM),
        ],
        out_specs=pl.BlockSpec(memory_space=pltpu.VMEM),
        out_shape=jax.ShapeDtypeStruct(
            (devices, parts, rounds * held * slots * slots, bins), jnp.bfloat16
        ),
        compiler_params=pltpu.CompilerParams(vmem_limit_bytes=16 * MIB),
        name="cross",
    )(pair_table, inverse, blocks)


def lag_kernel(
    scale, stacked_ref, table_ref, out_ref, left_ref, held_ref, lagged_ref, in_sems, out_sems
):
    tiles, _, depth, tile = table_ref.shape
    parts, rows, _ = left_ref.shape
    half = tiles * tile
    loads = [
        pltpu.make_async_copy(table_ref.at[t], held_ref.at[t], in_sems.at[t]) for t in range(tiles)
    ]
    for t in reversed(range(tiles)):
        loads[t].start()
    devices, _, _, bins = stacked_ref.shape
    for c in range(parts):
        for src in range(devices):
            left_ref[c, :, src * bins : (src + 1) * bins] = stacked_ref[src, c]

    turn = lax.broadcasted_iota(jnp.int32, (depth, 128), 0) % 4
    cosine = jnp.where(turn == 0, 1.0, jnp.where(turn == 2, -1.0, 0.0)).astype(jnp.bfloat16)
    sine = jnp.where(turn == 1, 1.0, jnp.where(turn == 3, -1.0, 0.0)).astype(jnp.bfloat16)
    before = jnp.dot(left_ref[0], cosine, preferred_element_type=jnp.float32)
    before = (before + jnp.dot(left_ref[1], sine, preferred_element_type=jnp.float32)) * scale

    lane = lax.broadcasted_iota(jnp.int32, (rows, 128), 1)
    flip = (128 - lane) % 128
    stores = []
    for t in reversed(range(tiles)):
        loads[t].wait()
        even = jnp.dot(left_ref[0], held_ref[t, 0], preferred_element_type=jnp.float32) * scale
        odd = jnp.dot(left_ref[1], held_ref[t, 1], preferred_element_type=jnp.float32) * scale
        lagged_ref[:, half + t * tile : half + (t + 1) * tile] = even + odd
        gap = even - odd
        for sub in reversed(range(tile // 128)):
            turned = jnp.take_along_axis(gap[:, sub * 128 : (sub + 1) * 128], flip, axis=1)
            at = half - t * tile - (sub + 1) * 128
            lagged_ref[:, at : at + 128] = jnp.where(lane == 0, before, turned)
            before = turned
        for k, at in enumerate((half + t * tile, half - (t + 1) * tile)):
            stores.append(
                pltpu.make_async_copy(
                    lagged_ref.at[:, at : at + tile],
                    out_ref.at[:, at : at + tile],
                    out_sems.at[2 * t + k],
                )
            )
            stores[-1].start()
    for store in stores:
        store.wait()


def lags(stacked, table, scale):
    devices, parts, rows, bins = stacked.shape
    tiles, _, depth, tile = table.shape
    lag_count = 2 * tiles * tile
    return pl.pallas_call(
        functools.partial(lag_kernel, scale),
        in_specs=[
            pl.BlockSpec(memory_space=pltpu.VMEM),
            pl.BlockSpec(memory_space=pl.ANY),
        ],
        out_specs=pl.BlockSpec(memory_space=pl.ANY),
        out_shape=jax.ShapeDtypeStruct((rows, lag_count), jnp.float32),
        scratch_shapes=[
            pltpu.VMEM((parts, rows, depth), jnp.bfloat16),
            pltpu.VMEM(table.shape, jnp.bfloat16),
            pltpu.VMEM((rows, lag_count), jnp.float32),
            pltpu.SemaphoreType.DMA((tiles,)),
            pltpu.SemaphoreType.DMA((2 * tiles,)),
        ],
        compiler_params=pltpu.CompilerParams(vmem_limit_bytes=48 * MIB),
        name="lags",
    )(stacked, table)


def local(table, spectra, block_counts, window_masks, pair_table):
    devices = lax.axis_size("sta")
    parts, days, windows, slots, total = spectra.shape
    rounds, pairs, _ = pair_table.shape
    held = days * pairs // devices
    packed = pack(spectra, block_counts, window_masks, devices)
    blocks = lax.all_to_all(packed, "sta", split_axis=0, concat_axis=0, tiled=True)
    weights = window_masks.astype(jnp.float32)
    joint = jnp.einsum("dwa,dwb->dab", weights, weights)
    inverse = (1.0 / jnp.maximum(joint, 1.0)).reshape(-1)
    stacked = cross(blocks, inverse, pair_table)
    received = lax.all_to_all(stacked, "sta", split_axis=0, concat_axis=0, tiled=True)
    lagged = lags(received, table, 1.0 / math.sqrt(total))
    return lagged.reshape(rounds, held, slots * slots, LAGS)


def solution(mesh):
    placed = (P(None, "grp", None, "sta", None), P(), P("grp", None, None), P())

    def run(spectra, block_counts, window_masks, pair_table):
        table = phase_tiles(spectra.shape[-1], LAGS, 256)
        return jax.shard_map(
            functools.partial(local, table),
            mesh=mesh,
            in_specs=placed,
            out_specs=P("grp", "sta", None, None),
            check_vma=False,
        )(spectra, block_counts, window_masks, pair_table)

    return run
```

time: 112 us -> 102 us (0.911)
  local copies, waits for them, and re-layouts: 10.3 us -> 0.19 us
    unnamed x15 -> x5, local copies, waits for them, and re-layouts: 10.2 us -> 0.11 us
where the time goes in v2:
time: 102 us
  waiting for transfers between devices  41.1 us (40%)
  blocking collectives  35.9 us (35%)
  Pallas kernels  17.1 us (17%)
  starting transfers between devices  7.36 us (7%)
    all_to_all x1, waiting for transfers between devices, local(): lax.all_to_all(packed, 'sta', split_axis=0, concat_axis=0, tiled=True)  41.1 us
    all_to_all x1, blocking collectives, local(): lax.all_to_all(stacked, 'sta', split_axis=0, concat_axis=0, tiled=True)  35.9 us
    pallas_call x1, Pallas kernels, cross(): pl.pallas_call(cross_kernel, in_specs=[pl.BlockSpec(memory_space=pltpu.SM...  7.67 us
    all_to_all x1, starting transfers between devices, local(): lax.all_to_all(packed, 'sta', split_axis=0, concat_axis=0, tiled=True)  7.36 us
    pallas_call x1, Pallas kernels, lags(): pl.pallas_call(functools.partial(lag_kernel, scale), in_specs=[pl.BlockSp...  5.39 us
    pallas_call x1, Pallas kernels, pack(): pl.pallas_call(functools.partial(pack_kernel, devices), in_specs=[pl.Bloc...  4.08 us
  transfers between devices with their start and end apart: 1, of which 1 were waited for; matrix products, arithmetic and copies ran while one was open for 0% of the time, Pallas kernels for 0%

profile of v2, /device:TPU:1, one launch (start us, length us, event | category | flops | bytes accessed | tf_op | source)
XLA Modules:
  0.0 101.9 jit_solution(12351729240940821393)
XLA Ops:
  0.0 4.1 %pack.1 = bf16[16,2,4,4,16,128]{5,4,3,2,1,0:T(8,128)(2,1)} custom-call(s32[16]{0:T(128)} %counts_ref.1, s32[4,16,16]{2,1,0:T(8,128)} %masks_ref.1, bf16[2,4,16,4,2048]{4,3,2,1,0:T(4,128)(2,1)} %spectra_ref.1), custom_call_target="tpu_custom_call" | custom-call | tf_op jit(solution)/shard_map/pack/pallas_call | solution.py:76
  4.1 0.0 copy-start
  4.1 0.0 copy-start.1
  4.1 7.4 %all-to-all-start = ((bf16[16,2,4,4,16,128]{5,4,3,2,1,0:T(8,128)(2,1)}), bf16[16,2,4,4,16,128]{5,4,3,2,1,0:T(8,128)(2,1)S(1)}, u32[]{:S(2)}, u32[]{:S(2)}) async-start(bf16[16,2,4,4,16,128]{5,4,3,2,1,0:T(8,128)(2,1)} %pack.1), calls=%async_computation | async-start | bytes 4194304 | tf_op jit(solution)/shard_map/all_to_all | solution.py:257
  11.5 0.0 copy-done
  11.5 0.2 fusion
  11.7 0.1 reshape.6.inverse_ref
  11.8 0.0 copy-done.1
  11.8 0.1 copy.7.pairs_ref
  11.9 41.1 %all-to-all-done.blocks_ref = bf16[16,2,4,4,16,128]{5,4,3,2,1,0:T(8,128)(2,1)S(1)} async-done(((bf16[16,2,4,4,16,128]{5,4,3,2,1,0:T(8,128)(2,1)}), bf16[16,2,4,4,16,128]{5,4,3,2,1,0:T(8,128)(2,1)S(1)}, u32[]{:S(2)}, u32[]{:S(2)}) %all-to-all-start) | async-done | bytes 2097184 | tf_op jit(solution)/shard_map/all_to_all | solution.py:257
  52.9 7.7 %cross.1 = bf16[16,2,128,128]{3,2,1,0:T(8,128)(2,1)S(1)} custom-call(s32[4,8,2]{2,1,0:T(8,128)S(1)} %copy.7.pairs_ref, f32[1024]{0:T(1024)S(1)} %reshape.6.inverse_ref, bf16[16,2,4,4,16,128]{5,4,3,2,1,0:T(8,128)(2,1)S(1)} %all-to-all-done.blocks_ref), custom_call_target="tpu_custom_call" | custom-call | tf_op jit(solution)/shard_map/cross/pallas_call | solution.py:162
  60.6 35.9 %all_to_all.10.stacked_ref = bf16[16,2,128,128]{3,2,1,0:T(8,128)(2,1)S(1)} all-to-all(bf16[16,2,128,128]{3,2,1,0:T(8,128)(2,1)S(1)} %cross.1), channel_id=1, replica_groups=mesh['grp'=2,'sta'=16] {'sta'}, dimensions={0} | all-to-all | bytes 2097152 | tf_op jit(solution)/shard_map/all_to_all | solution.py:262
  96.5 5.4 %lags.1 = f32[128,2048]{1,0:T(8,128)} custom-call(bf16[16,2,128,128]{3,2,1,0:T(8,128)(2,1)S(1)} %all_to_all.10.stacked_ref, bf16[4,2,2048,256]{3,2,1,0:T(8,128)(2,1)} %constant.4.clone.table_ref), custom_call_target="tpu_custom_call" | custom-call | tf_op jit(solution)/shard_map/lags/pallas_call | solution.py:231
Async XLA Ops:
  4.1 7.4 %copy-start = (s32[4,16,16]{2,1,0:T(8,128)S(1)}, s32[4,16,16]{2,1,0:T(8,128)}, u32[]{:S(2)}) copy-start(s32[4,16,16]{2,1,0:T(8,128)} %masks_ref.1) | copy-start | bytes 12292
  4.1 7.7 %copy-start.1 = (s32[4,8,2]{1,2,0:T(2,128)S(1)}, s32[4,8,2]{1,2,0:T(2,128)}, u32[]{:S(2)}) copy-start(s32[4,8,2]{1,2,0:T(2,128)} %param.8) | copy-start | bytes 772
  4.1 48.8 %all-to-all-start = ((bf16[16,2,4,4,16,128]{5,4,3,2,1,0:T(8,128)(2,1)}), bf16[16,2,4,4,16,128]{5,4,3,2,1,0:T(8,128)(2,1)S(1)}, u32[]{:S(2)}, u32[]{:S(2)}) async-start(bf16[16,2,4,4,16,128]{5,4,3,2,1,0:T(8,128)(2,1)} %pack.1), calls=%async_computation | async-start | bytes 4194304 | tf_op jit(solution)/shard_map/all_to_all | solution.py:257

commit v3 on v2

--- a/solution.py
+++ b/solution.py
@@ -12,6 +12,8 @@
 
 LAGS = 2048
 MIB = 1 << 20
+ORDER = (12, 1, 13, 2, 14, 3, 15, 4, 8, 5, 9, 6, 10, 7, 11)
+FIRST = 5
 
 
 def phase_tiles(freq_count, lag_count, tile):
@@ -67,6 +69,65 @@
     lax.fori_loop(0, parts * days, one, 0)
     for step in range(parts * days):
         store(step).wait()
+
+
+def piece_kernel(aways, counts_ref, masks_ref, spectra_ref, *refs):
+    out_refs, raw_ref, rows_ref, sems = refs[: len(aways)], refs[-3], refs[-2], refs[-1]
+    me = lax.axis_index("sta")
+    parts, days, windows, slots, bins = raw_ref.shape[1:]
+    count = counts_ref[me]
+    loads = []
+    for n, away in enumerate(aways):
+        columns = pl.ds(pl.multiple_of((me ^ away) * bins, 128), bins)
+        loads.append(
+            pltpu.make_async_copy(spectra_ref.at[:, :, :, :, columns], raw_ref.at[n], sems.at[n])
+        )
+        loads[n].start()
+    lane = lax.broadcasted_iota(jnp.int32, masks_ref.shape[1:], 1)
+    wide = []
+    for d in range(days):
+        mine = jnp.where(lane == me, masks_ref[d], 0)
+        keep = (jnp.sum(mine, axis=1, keepdims=True) > 0).astype(jnp.float32)
+        wide.append(jnp.broadcast_to(keep, (windows, bins)))
+    live = [jnp.where(slot < count, 1.0, 0.0) for slot in range(slots)]
+    for n, out_ref in enumerate(out_refs):
+        loads[n].wait()
+
+        def one(c, carry):
+            for d in range(days):
+                for w in range(windows):
+                    rows_ref[d, w * slots : (w + 1) * slots, :] = raw_ref[n, c, d, w].astype(
+                        jnp.float32
+                    )
+                for slot in range(slots):
+                    picked = rows_ref[d, pl.ds(slot, windows, stride=slots), :]
+                    out_ref[c, d, slot] = (picked * (wide[d] * live[slot])).astype(jnp.bfloat16)
+            return carry
+
+        lax.fori_loop(0, parts, one, 0)
+
+
+def pieces(spectra, block_counts, window_masks, devices, aways, name):
+    parts, days, windows, slots, total = spectra.shape
+    bins = total // devices
+    share = jax.ShapeDtypeStruct((parts, days, slots, windows, bins), jnp.bfloat16)
+    return pl.pallas_call(
+        functools.partial(piece_kernel, aways),
+        in_specs=[
+            pl.BlockSpec(memory_space=pltpu.SMEM),
+            pl.BlockSpec(memory_space=pltpu.VMEM),
+            pl.BlockSpec(memory_space=pl.ANY),
+        ],
+        out_specs=[pl.BlockSpec(memory_space=pltpu.VMEM)] * len(aways),
+        out_shape=[share] * len(aways),
+        scratch_shapes=[
+            pltpu.VMEM((len(aways), parts, days, windows, slots, bins), jnp.bfloat16),
+            pltpu.VMEM((days, windows * slots, bins), jnp.float32),
+            pltpu.SemaphoreType.DMA((len(aways),)),
+        ],
+        compiler_params=pltpu.CompilerParams(vmem_limit_bytes=60 * MIB),
+        name=name,
+    )(block_counts, window_masks, spectra)
 
 
 def pack(spectra, block_counts, window_masks, devices):
@@ -137,11 +198,23 @@
     return stacked
 
 
-def cross_kernel(pairs_ref, inverse_ref, blocks_ref, out_ref):
+def cross_kernel(sources, pairs_ref, inverse_ref, *refs):
+    block_refs, out_ref, blocks_ref = refs[: len(sources)], refs[-2], refs[-1]
     block_count, _, days, slots, _, bins = blocks_ref.shape
     rounds, pairs = pairs_ref.shape[0], pairs_ref.shape[1]
     rows = lax.broadcasted_iota(jnp.int32, (8, bins), 0)
     held = days * pairs // block_count
+    me = lax.axis_index("sta")
+    for ref, source in zip(block_refs, sources):
+        if source is None:
+
+            def widen(n, carry):
+                blocks_ref[n] = ref[n].astype(jnp.float32)
+                return carry
+
+            lax.fori_loop(0, block_count, widen, 0)
+        else:
+            blocks_ref[me ^ source] = ref[...].astype(jnp.float32)
 
     def one_pair(index, carry):
         r, p = index // pairs, index % pairs
@@ -152,27 +225,25 @@
                 out_ref[(p * days + d) // held, c, pl.ds(row, slots * slots), :] = stacked[d][c]
         return carry
 
-    lax.fori_loop(0, rounds * pairs, one_pair, 0)
-
-
-def cross(blocks, inverse, pair_table):
-    devices, parts, days, slots, windows, bins = blocks.shape
+    lax.fori_loop(0, rounds * pairs, one_pair, 0, unroll=2)
+
+
+def cross(blocks, sources, inverse, pair_table, devices):
+    parts, days, slots, windows, bins = blocks[0].shape[-5:]
     rounds, pairs, _ = pair_table.shape
     held = days * pairs // devices
     return pl.pallas_call(
-        cross_kernel,
-        in_specs=[
-            pl.BlockSpec(memory_space=pltpu.SMEM),
-            pl.BlockSpec(memory_space=pltpu.SMEM),
-            pl.BlockSpec(memory_space=pltpu.VMEM),
-        ],
+        functools.partial(cross_kernel, sources),
+        in_specs=[pl.BlockSpec(memory_space=pltpu.SMEM)] * 2
+        + [pl.BlockSpec(memory_space=pltpu.VMEM)] * len(blocks),
         out_specs=pl.BlockSpec(memory_space=pltpu.VMEM),
         out_shape=jax.ShapeDtypeStruct(
             (devices, parts, rounds * held * slots * slots, bins), jnp.bfloat16
         ),
-        compiler_params=pltpu.CompilerParams(vmem_limit_bytes=16 * MIB),
+        scratch_shapes=[pltpu.VMEM((devices, parts, days, slots, windows, bins), jnp.float32)],
+        compiler_params=pltpu.CompilerParams(vmem_limit_bytes=40 * MIB),
         name="cross",
-    )(pair_table, inverse, blocks)
+    )(pair_table, inverse, *blocks)
 
 
 def lag_kernel(
@@ -253,12 +324,22 @@
     parts, days, windows, slots, total = spectra.shape
     rounds, pairs, _ = pair_table.shape
     held = days * pairs // devices
-    packed = pack(spectra, block_counts, window_masks, devices)
-    blocks = lax.all_to_all(packed, "sta", split_axis=0, concat_axis=0, tiled=True)
+    if devices == len(ORDER) + 1 and total % (128 * devices) == 0:
+        sources = ORDER + (0,)
+        shares = pieces(spectra, block_counts, window_masks, devices, sources[:FIRST], "pack_first")
+        shares += pieces(spectra, block_counts, window_masks, devices, sources[FIRST:], "pack_rest")
+        blocks = [
+            lax.ppermute(share, "sta", [(n, n ^ away) for n in range(devices)]) if away else share
+            for share, away in zip(shares, sources)
+        ]
+    else:
+        packed = pack(spectra, block_counts, window_masks, devices)
+        sources = (None,)
+        blocks = [lax.all_to_all(packed, "sta", split_axis=0, concat_axis=0, tiled=True)]
     weights = window_masks.astype(jnp.float32)
     joint = jnp.einsum("dwa,dwb->dab", weights, weights)
     inverse = (1.0 / jnp.maximum(joint, 1.0)).reshape(-1)
-    stacked = cross(blocks, inverse, pair_table)
+    stacked = cross(blocks, sources, inverse, pair_table, devices)
     received = lax.all_to_all(stacked, "sta", split_axis=0, concat_axis=0, tiled=True)
     lagged = lags(received, table, 1.0 / math.sqrt(total))
     return lagged.reshape(rounds, held, slots * slots, LAGS)

time: 102 us -> 96.2 us (0.943)
  waiting for transfers between devices: 41.1 us -> 12.6 us
  starting transfers between devices: 7.36 us -> 32.4 us
  blocking collectives: 35.9 us -> 29.2 us
  Pallas kernels: 17.1 us -> 18.7 us
  local copies, waits for them, and re-layouts: 0.19 us -> 1.76 us
    all_to_all x1 -> x0, waiting for transfers between devices: 41.1 us -> none  [local(): lax.all_to_all(packed, 'sta', split_axis=0, concat_axis=0, tiled=True)]
    ppermute x0 -> x15, starting transfers between devices: none -> 32.4 us  [local(): lax.ppermute(share, 'sta', [(n, n ^ away) for n in range(devices)])]
    ppermute x0 -> x15, waiting for transfers between devices: none -> 12.6 us  [local(): lax.ppermute(share, 'sta', [(n, n ^ away) for n in range(devices)])]
    all_to_all x1 -> x0, starting transfers between devices: 7.36 us -> none  [local(): lax.all_to_all(packed, 'sta', split_axis=0, concat_axis=0, tiled=True)]
    all_to_all x1, blocking collectives: 35.9 us -> 29.2 us  [local(): lax.all_to_all(stacked, 'sta', split_axis=0, concat_axis=0, tiled=True)]
    unnamed x5 -> x3, local copies, waits for them, and re-layouts: 0.11 us -> 1.68 us
    pallas_call x2 -> x3, Pallas kernels: 11.7 us -> 13.3 us  [the longest x1 6.91 us: cross(): pl.pallas_call(functools.partial(cross_kernel, sources), in_specs=[pl.Blo...]
  transfers between devices with their start and end apart: 1 -> 15, of which waited for: 1 -> 4; matrix products, arithmetic and copies ran while one was open for 0% -> 2% of each run, Pallas kernels for 0% -> 4%
where the time goes in v3:
time: 96.2 us; the launch traced here: 95.8 us
  starting transfers between devices  32.4 us (34%)
  blocking collectives  29.2 us (30%)
  Pallas kernels  18.7 us (19%)
  waiting for transfers between devices  12.6 us (13%)
  local copies, waits for them, and re-layouts  1.76 us (2%)
  matrix products  1.03 us (1%)
    ppermute x15, starting transfers between devices, local(): lax.ppermute(share, 'sta', [(n, n ^ away) for n in range(devices)])  32.4 us
    all_to_all x1, blocking collectives, local(): lax.all_to_all(stacked, 'sta', split_axis=0, concat_axis=0, tiled=True)  29.2 us
    ppermute x15, waiting for transfers between devices, local(): lax.ppermute(share, 'sta', [(n, n ^ away) for n in range(devices)])  12.6 us
    pallas_call x1, Pallas kernels, cross(): pl.pallas_call(functools.partial(cross_kernel, sources), in_specs=[pl.Blo...  6.91 us
    pallas_call x2, Pallas kernels, pieces(): pl.pallas_call(functools.partial(piece_kernel, aways), in_specs=[pl.Block...  6.39 us
    pallas_call x1, Pallas kernels, lags(): pl.pallas_call(functools.partial(lag_kernel, scale), in_specs=[pl.BlockSp...  5.39 us
  transfers between devices with their start and end apart: 15, of which 4 were waited for; matrix products, arithmetic and copies ran while one was open for 2% of the time, Pallas kernels for 4%

profile of v3, /device:TPU:1, one launch (start us, length us, event | category | flops | bytes accessed | tf_op | source)
XLA Modules:
  0.0 95.8 jit_solution(3942607781628790094)
XLA Ops:
  0.0 2.9 %pack_first.1 = (bf16[2,4,4,16,128]{4,3,2,1,0:T(8,128)(2,1)}, bf16[2,4,4,16,128]{4,3,2,1,0:T(8,128)(2,1)}, bf16[2,4,4,16,128]{4,3,2,1,0:T(8,128)(2,1)}, bf16[2,4...) custom-call(s32[16]{0:T(128)} %counts_ref.3, s32[4,16,16]{2,1,0:T(8,128)} %masks_ref.3, ...), custom_call_target="tpu_custom_call" | custom-call | tf_op jit(solution)/shard_map/pack_first/pallas_call | solution.py:114
  2.9 4.2 %collective-permute-start = (bf16[2,4,4,16,128]{4,3,2,1,0:T(8,128)(2,1)}, bf16[2,4,4,16,128]{4,3,2,1,0:T(8,128)(2,1)S(1)}, u32[]{:S(2)}, u32[]{:S(2)}) collective-permute-start(bf16[2,4,4,16,128]{4,3,2,1,0:T(8,128)(2,1)} %get-tuple-element.21), channel_id=1, source_target_pairs={{0,12},{1,13},{2,14},{3,15},{4,8},{5,9},{6,10},{7,11},{8,4},{9,5},... | collective-permute-start | bytes 393224 | tf_op jit(solution)/shard_map/ppermute | solution.py:332
  7.1 1.0 collective-permute-start.1
  8.0 1.2 %collective-permute-start.3 = (bf16[2,4,4,16,128]{4,3,2,1,0:T(8,128)(2,1)}, bf16[2,4,4,16,128]{4,3,2,1,0:T(8,128)(2,1)S(1)}, u32[]{:S(2)}, u32[]{:S(2)}) collective-permute-start(bf16[2,4,4,16,128]{4,3,2,1,0:T(8,128)(2,1)} %get-tuple-element.24), channel_id=1, source_target_pairs={{0,2},{1,3},{2,0},{3,1},{4,6},{5,7},{6,4},{7,5},{8,10},{9,11},{10,... | collective-permute-start | bytes 393224 | tf_op jit(solution)/shard_map/ppermute | solution.py:332
  9.3 3.1 %collective-permute-start.4 = (bf16[2,4,4,16,128]{4,3,2,1,0:T(8,128)(2,1)}, bf16[2,4,4,16,128]{4,3,2,1,0:T(8,128)(2,1)S(1)}, u32[]{:S(2)}, u32[]{:S(2)}) collective-permute-start(bf16[2,4,4,16,128]{4,3,2,1,0:T(8,128)(2,1)} %get-tuple-element.25), channel_id=1, source_target_pairs={{0,14},{1,15},{2,12},{3,13},{4,10},{5,11},{6,8},{7,9},{8,6},{9,7},... | collective-permute-start | bytes 393224 | tf_op jit(solution)/shard_map/ppermute | solution.py:332
  12.4 3.5 %pack_rest.1 = (bf16[2,4,4,16,128]{4,3,2,1,0:T(8,128)(2,1)}, bf16[2,4,4,16,128]{4,3,2,1,0:T(8,128)(2,1)}, bf16[2,4,4,16,128]{4,3,2,1,0:T(8,128)(2,1)}, bf16[2,4,...) custom-call(s32[16]{0:T(128)} %counts_ref.3, ...), custom_call_target="tpu_custom_call" | custom-call | tf_op jit(solution)/shard_map/pack_rest/pallas_call | solution.py:114
  15.9 2.3 %collective-permute-start.5 = (bf16[2,4,4,16,128]{4,3,2,1,0:T(8,128)(2,1)}, bf16[2,4,4,16,128]{4,3,2,1,0:T(8,128)(2,1)S(1)}, u32[]{:S(2)}, u32[]{:S(2)}) collective-permute-start(bf16[2,4,4,16,128]{4,3,2,1,0:T(8,128)(2,1)} %get-tuple-element.26), channel_id=1, source_target_pairs={{0,3},{1,2},{2,1},{3,0},{4,7},{5,6},{6,5},{7,4},{8,11},{9,10},{10,... | collective-permute-start | bytes 393224 | tf_op jit(solution)/shard_map/ppermute | solution.py:332
  18.2 4.7 %collective-permute-start.7 = (bf16[2,4,4,16,128]{4,3,2,1,0:T(8,128)(2,1)}, bf16[2,4,4,16,128]{4,3,2,1,0:T(8,128)(2,1)S(1)}, u32[]{:S(2)}, u32[]{:S(2)}) collective-permute-start(bf16[2,4,4,16,128]{4,3,2,1,0:T(8,128)(2,1)} %get-tuple-element.28), channel_id=1, source_target_pairs={{0,4},{1,5},{2,6},{3,7},{4,0},{5,1},{6,2},{7,3},{8,12},{9,13},{10,... | collective-permute-start | bytes 393224 | tf_op jit(solution)/shard_map/ppermute | solution.py:332
  22.9 4.1 %collective-permute-start.8 = (bf16[2,4,4,16,128]{4,3,2,1,0:T(8,128)(2,1)}, bf16[2,4,4,16,128]{4,3,2,1,0:T(8,128)(2,1)S(1)}, u32[]{:S(2)}, u32[]{:S(2)}) collective-permute-start(bf16[2,4,4,16,128]{4,3,2,1,0:T(8,128)(2,1)} %get-tuple-element.29), channel_id=1, source_target_pairs={{0,8},{1,9},{2,10},{3,11},{4,12},{5,13},{6,14},{7,15},{8,0},{9,1},... | collective-permute-start | bytes 393224 | tf_op jit(solution)/shard_map/ppermute | solution.py:332
  27.0 2.8 %collective-permute-start.9 = (bf16[2,4,4,16,128]{4,3,2,1,0:T(8,128)(2,1)}, bf16[2,4,4,16,128]{4,3,2,1,0:T(8,128)(2,1)S(1)}, u32[]{:S(2)}, u32[]{:S(2)}) collective-permute-start(bf16[2,4,4,16,128]{4,3,2,1,0:T(8,128)(2,1)} %get-tuple-element.30), channel_id=1, source_target_pairs={{0,5},{1,4},{2,7},{3,6},{4,1},{5,0},{6,3},{7,2},{8,13},{9,12},{10,... | collective-permute-start | bytes 393224 | tf_op jit(solution)/shard_map/ppermute | solution.py:332
  29.8 0.8 copy.7.pairs_ref
  30.6 2.6 %collective-permute-start.10 = (bf16[2,4,4,16,128]{4,3,2,1,0:T(8,128)(2,1)}, bf16[2,4,4,16,128]{4,3,2,1,0:T(8,128)(2,1)S(1)}, u32[]{:S(2)}, u32[]{:S(2)}) collective-permute-start(bf16[2,4,4,16,128]{4,3,2,1,0:T(8,128)(2,1)} %get-tuple-element.31), channel_id=1, source_target_pairs={{0,9},{1,8},{2,11},{3,10},{4,13},{5,12},{6,15},{7,14},{8,1},{9,0},... | collective-permute-start | bytes 393224 | tf_op jit(solution)/shard_map/ppermute | solution.py:332
  33.6 2.1 %collective-permute-start.12 = (bf16[2,4,4,16,128]{4,3,2,1,0:T(8,128)(2,1)}, bf16[2,4,4,16,128]{4,3,2,1,0:T(8,128)(2,1)S(1)}, u32[]{:S(2)}, u32[]{:S(2)}) collective-permute-start(bf16[2,4,4,16,128]{4,3,2,1,0:T(8,128)(2,1)} %get-tuple-element.33), channel_id=1, source_target_pairs={{0,10},{1,11},{2,8},{3,9},{4,14},{5,15},{6,12},{7,13},{8,2},{9,3},... | collective-permute-start | bytes 393224 | tf_op jit(solution)/shard_map/ppermute | solution.py:332
  35.7 1.2 %collective-permute-start.13 = (bf16[2,4,4,16,128]{4,3,2,1,0:T(8,128)(2,1)}, bf16[2,4,4,16,128]{4,3,2,1,0:T(8,128)(2,1)S(1)}, u32[]{:S(2)}, u32[]{:S(2)}) collective-permute-start(bf16[2,4,4,16,128]{4,3,2,1,0:T(8,128)(2,1)} %get-tuple-element.34), channel_id=1, source_target_pairs={{0,7},{1,6},{2,5},{3,4},{4,3},{5,2},{6,1},{7,0},{8,15},{9,14},{10,... | collective-permute-start | bytes 393224 | tf_op jit(solution)/shard_map/ppermute | solution.py:332
  36.9 2.7 %collective-permute-start.14 = (bf16[2,4,4,16,128]{4,3,2,1,0:T(8,128)(2,1)}, bf16[2,4,4,16,128]{4,3,2,1,0:T(8,128)(2,1)S(1)}, u32[]{:S(2)}, u32[]{:S(2)}) collective-permute-start(bf16[2,4,4,16,128]{4,3,2,1,0:T(8,128)(2,1)} %get-tuple-element.35), channel_id=1, source_target_pairs={{0,11},{1,10},{2,9},{3,8},{4,15},{5,14},{6,13},{7,12},{8,3},{9,2},... | collective-permute-start | bytes 393224 | tf_op jit(solution)/shard_map/ppermute | solution.py:332
  39.6 1.0 %fusion = f32[4,16,16]{2,1,0:T(8,128)S(1)} fusion(s32[4,16,16]{2,1,0:T(8,128)} %masks_ref.3), kind=kOutput, calls=%fused_computation.1 | convolution fusion | flops 35840 | bytes 8192 | tf_op jit(solution)/shard_map/dwa,dwb->dab/dot_general | solution.py:340
  40.7 2.9 %collective-permute-done.10.refs_10_ = bf16[2,4,4,16,128]{4,3,2,1,0:T(8,128)(2,1)S(1)} collective-permute-done((bf16[2,4,4,16,128]{4,3,2,1,0:T(8,128)(2,1)}, bf16[2,4,4,16,128]{4,3,2,1,0:T(8,128)(2,1)S(1)}, u32[]{:S(2)}, u32[]{:S(2)}) %collective-permute-start.10) | collective-permute-done | bytes 131104 | tf_op jit(solution)/shard_map/ppermute | solution.py:332
  43.7 3.9 %collective-permute-done.12.refs_12_ = bf16[2,4,4,16,128]{4,3,2,1,0:T(8,128)(2,1)S(1)} collective-permute-done((bf16[2,4,4,16,128]{4,3,2,1,0:T(8,128)(2,1)}, bf16[2,4,4,16,128]{4,3,2,1,0:T(8,128)(2,1)S(1)}, u32[]{:S(2)}, u32[]{:S(2)}) %collective-permute-start.12) | collective-permute-done | bytes 131104 | tf_op jit(solution)/shard_map/ppermute | solution.py:332
  47.6 0.7 collective-permute-done.13.refs_13_
  48.3 5.0 %collective-permute-done.14.refs_14_ = bf16[2,4,4,16,128]{4,3,2,1,0:T(8,128)(2,1)S(1)} collective-permute-done((bf16[2,4,4,16,128]{4,3,2,1,0:T(8,128)(2,1)}, bf16[2,4,4,16,128]{4,3,2,1,0:T(8,128)(2,1)S(1)}, u32[]{:S(2)}, u32[]{:S(2)}) %collective-permute-start.14) | collective-permute-done | bytes 131104 | tf_op jit(solution)/shard_map/ppermute | solution.py:332
  53.3 0.9 copy-done
  54.2 6.9 %cross.1 = bf16[16,2,128,128]{3,2,1,0:T(8,128)(2,1)S(1)} custom-call(s32[4,8,2]{2,1,0:T(8,128)S(1)} %copy.7.pairs_ref, f32[1024]{0:T(1024)S(1)} %reshape.6.inverse_ref, bf16[2,4,4,16,128]{4,3,2,1,0:T(8,128)(2,1)S(1)} %collective-permute-done.refs_0_, bf16[2,4,4,16,128]{4,3,2,1,0:T(8,128)(2,1)S(1)} %collective-permute-done.1.refs_1_, ...), custom_call_target="tpu_custom_call" | custom-call | tf_op jit(solution)/shard_map/cross/pallas_call | solution.py:235
  61.1 29.2 %all_to_all.5.stacked_ref = bf16[16,2,128,128]{3,2,1,0:T(8,128)(2,1)S(1)} all-to-all(bf16[16,2,128,128]{3,2,1,0:T(8,128)(2,1)S(1)} %cross.1), channel_id=1, replica_groups=mesh['grp'=2,'sta'=16] {'sta'}, dimensions={0} | all-to-all | bytes 2097152 | tf_op jit(solution)/shard_map/all_to_all | solution.py:343
  90.4 5.4 %lags.1 = f32[128,2048]{1,0:T(8,128)} custom-call(bf16[16,2,128,128]{3,2,1,0:T(8,128)(2,1)S(1)} %all_to_all.5.stacked_ref, bf16[4,2,2048,256]{3,2,1,0:T(8,128)(2,1)} %constant.4.clone.table_ref), custom_call_target="tpu_custom_call" | custom-call | tf_op jit(solution)/shard_map/lags/pallas_call | solution.py:302
  (16 shorter events, 0.5 us)
Async XLA Ops:
  2.9 13.1 %collective-permute-start = (bf16[2,4,4,16,128]{4,3,2,1,0:T(8,128)(2,1)}, bf16[2,4,4,16,128]{4,3,2,1,0:T(8,128)(2,1)S(1)}, u32[]{:S(2)}, u32[]{:S(2)}) collective-permute-start(bf16[2,4,4,16,128]{4,3,2,1,0:T(8,128)(2,1)} %get-tuple-element.21), channel_id=1, source_target_pairs={{0,12},{1,13},{2,14},{3,15},{4,8},{5,9},{6,10},{7,11},{8,4},{9,5},... | collective-permute-start | bytes 393224 | tf_op jit(solution)/shard_map/ppermute | solution.py:332
  7.1 11.1 %collective-permute-start.1 = (bf16[2,4,4,16,128]{4,3,2,1,0:T(8,128)(2,1)}, bf16[2,4,4,16,128]{4,3,2,1,0:T(8,128)(2,1)S(1)}, u32[]{:S(2)}, u32[]{:S(2)}) collective-permute-start(bf16[2,4,4,16,128]{4,3,2,1,0:T(8,128)(2,1)} %get-tuple-element.22), channel_id=1, source_target_pairs={{0,1},{1,0},{2,3},{3,2},{4,5},{5,4},{6,7},{7,6},{8,9},{9,8},{10,11... | collective-permute-start | bytes 393224 | tf_op jit(solution)/shard_map/ppermute | solution.py:332
  8.0 10.2 %collective-permute-start.2 = (bf16[2,4,4,16,128]{4,3,2,1,0:T(8,128)(2,1)}, bf16[2,4,4,16,128]{4,3,2,1,0:T(8,128)(2,1)S(1)}, u32[]{:S(2)}, u32[]{:S(2)}) collective-permute-start(bf16[2,4,4,16,128]{4,3,2,1,0:T(8,128)(2,1)} %get-tuple-element.23), channel_id=1, source_target_pairs={{0,13},{1,12},{2,15},{3,14},{4,9},{5,8},{6,11},{7,10},{8,5},{9,4},... | collective-permute-start | bytes 393224 | tf_op jit(solution)/shard_map/ppermute | solution.py:332
  8.0 14.9 %collective-permute-start.3 = (bf16[2,4,4,16,128]{4,3,2,1,0:T(8,128)(2,1)}, bf16[2,4,4,16,128]{4,3,2,1,0:T(8,128)(2,1)S(1)}, u32[]{:S(2)}, u32[]{:S(2)}) collective-permute-start(bf16[2,4,4,16,128]{4,3,2,1,0:T(8,128)(2,1)} %get-tuple-element.24), channel_id=1, source_target_pairs={{0,2},{1,3},{2,0},{3,1},{4,6},{5,7},{6,4},{7,5},{8,10},{9,11},{10,... | collective-permute-start | bytes 393224 | tf_op jit(solution)/shard_map/ppermute | solution.py:332
  9.3 17.7 %collective-permute-start.4 = (bf16[2,4,4,16,128]{4,3,2,1,0:T(8,128)(2,1)}, bf16[2,4,4,16,128]{4,3,2,1,0:T(8,128)(2,1)S(1)}, u32[]{:S(2)}, u32[]{:S(2)}) collective-permute-start(bf16[2,4,4,16,128]{4,3,2,1,0:T(8,128)(2,1)} %get-tuple-element.25), channel_id=1, source_target_pairs={{0,14},{1,15},{2,12},{3,13},{4,10},{5,11},{6,8},{7,9},{8,6},{9,7},... | collective-permute-start | bytes 393224 | tf_op jit(solution)/shard_map/ppermute | solution.py:332
  15.9 14.7 %collective-permute-start.5 = (bf16[2,4,4,16,128]{4,3,2,1,0:T(8,128)(2,1)}, bf16[2,4,4,16,128]{4,3,2,1,0:T(8,128)(2,1)S(1)}, u32[]{:S(2)}, u32[]{:S(2)}) collective-permute-start(bf16[2,4,4,16,128]{4,3,2,1,0:T(8,128)(2,1)} %get-tuple-element.26), channel_id=1, source_target_pairs={{0,3},{1,2},{2,1},{3,0},{4,7},{5,6},{6,5},{7,4},{8,11},{9,10},{10,... | collective-permute-start | bytes 393224 | tf_op jit(solution)/shard_map/ppermute | solution.py:332
  18.2 15.0 %collective-permute-start.6 = (bf16[2,4,4,16,128]{4,3,2,1,0:T(8,128)(2,1)}, bf16[2,4,4,16,128]{4,3,2,1,0:T(8,128)(2,1)S(1)}, u32[]{:S(2)}, u32[]{:S(2)}) collective-permute-start(bf16[2,4,4,16,128]{4,3,2,1,0:T(8,128)(2,1)} %get-tuple-element.27), channel_id=1, source_target_pairs={{0,15},{1,14},{2,13},{3,12},{4,11},{5,10},{6,9},{7,8},{8,7},{9,6},... | collective-permute-start | bytes 393224 | tf_op jit(solution)/shard_map/ppermute | solution.py:332
  18.2 15.4 %collective-permute-start.7 = (bf16[2,4,4,16,128]{4,3,2,1,0:T(8,128)(2,1)}, bf16[2,4,4,16,128]{4,3,2,1,0:T(8,128)(2,1)S(1)}, u32[]{:S(2)}, u32[]{:S(2)}) collective-permute-start(bf16[2,4,4,16,128]{4,3,2,1,0:T(8,128)(2,1)} %get-tuple-element.28), channel_id=1, source_target_pairs={{0,4},{1,5},{2,6},{3,7},{4,0},{5,1},{6,2},{7,3},{8,12},{9,13},{10,... | collective-permute-start | bytes 393224 | tf_op jit(solution)/shard_map/ppermute | solution.py:332
  22.9 12.8 %collective-permute-start.8 = (bf16[2,4,4,16,128]{4,3,2,1,0:T(8,128)(2,1)}, bf16[2,4,4,16,128]{4,3,2,1,0:T(8,128)(2,1)S(1)}, u32[]{:S(2)}, u32[]{:S(2)}) collective-permute-start(bf16[2,4,4,16,128]{4,3,2,1,0:T(8,128)(2,1)} %get-tuple-element.29), channel_id=1, source_target_pairs={{0,8},{1,9},{2,10},{3,11},{4,12},{5,13},{6,14},{7,15},{8,0},{9,1},... | collective-permute-start | bytes 393224 | tf_op jit(solution)/shard_map/ppermute | solution.py:332
  27.0 9.9 %collective-permute-start.9 = (bf16[2,4,4,16,128]{4,3,2,1,0:T(8,128)(2,1)}, bf16[2,4,4,16,128]{4,3,2,1,0:T(8,128)(2,1)S(1)}, u32[]{:S(2)}, u32[]{:S(2)}) collective-permute-start(bf16[2,4,4,16,128]{4,3,2,1,0:T(8,128)(2,1)} %get-tuple-element.30), channel_id=1, source_target_pairs={{0,5},{1,4},{2,7},{3,6},{4,1},{5,0},{6,3},{7,2},{8,13},{9,12},{10,... | collective-permute-start | bytes 393224 | tf_op jit(solution)/shard_map/ppermute | solution.py:332
  30.6 13.0 %collective-permute-start.10 = (bf16[2,4,4,16,128]{4,3,2,1,0:T(8,128)(2,1)}, bf16[2,4,4,16,128]{4,3,2,1,0:T(8,128)(2,1)S(1)}, u32[]{:S(2)}, u32[]{:S(2)}) collective-permute-start(bf16[2,4,4,16,128]{4,3,2,1,0:T(8,128)(2,1)} %get-tuple-element.31), channel_id=1, source_target_pairs={{0,9},{1,8},{2,11},{3,10},{4,13},{5,12},{6,15},{7,14},{8,1},{9,0},... | collective-permute-start | bytes 393224 | tf_op jit(solution)/shard_map/ppermute | solution.py:332
  33.2 10.5 %collective-permute-start.11 = (bf16[2,4,4,16,128]{4,3,2,1,0:T(8,128)(2,1)}, bf16[2,4,4,16,128]{4,3,2,1,0:T(8,128)(2,1)S(1)}, u32[]{:S(2)}, u32[]{:S(2)}) collective-permute-start(bf16[2,4,4,16,128]{4,3,2,1,0:T(8,128)(2,1)} %get-tuple-element.32), channel_id=1, source_target_pairs={{0,6},{1,7},{2,4},{3,5},{4,2},{5,3},{6,0},{7,1},{8,14},{9,15},{10,... | collective-permute-start | bytes 393224 | tf_op jit(solution)/shard_map/ppermute | solution.py:332
  33.6 14.0 %collective-permute-start.12 = (bf16[2,4,4,16,128]{4,3,2,1,0:T(8,128)(2,1)}, bf16[2,4,4,16,128]{4,3,2,1,0:T(8,128)(2,1)S(1)}, u32[]{:S(2)}, u32[]{:S(2)}) collective-permute-start(bf16[2,4,4,16,128]{4,3,2,1,0:T(8,128)(2,1)} %get-tuple-element.33), channel_id=1, source_target_pairs={{0,10},{1,11},{2,8},{3,9},{4,14},{5,15},{6,12},{7,13},{8,2},{9,3},... | collective-permute-start | bytes 393224 | tf_op jit(solution)/shard_map/ppermute | solution.py:332
  35.7 12.5 %collective-permute-start.13 = (bf16[2,4,4,16,128]{4,3,2,1,0:T(8,128)(2,1)}, bf16[2,4,4,16,128]{4,3,2,1,0:T(8,128)(2,1)S(1)}, u32[]{:S(2)}, u32[]{:S(2)}) collective-permute-start(bf16[2,4,4,16,128]{4,3,2,1,0:T(8,128)(2,1)} %get-tuple-element.34), channel_id=1, source_target_pairs={{0,7},{1,6},{2,5},{3,4},{4,3},{5,2},{6,1},{7,0},{8,15},{9,14},{10,... | collective-permute-start | bytes 393224 | tf_op jit(solution)/shard_map/ppermute | solution.py:332
  36.9 16.3 %collective-permute-start.14 = (bf16[2,4,4,16,128]{4,3,2,1,0:T(8,128)(2,1)}, bf16[2,4,4,16,128]{4,3,2,1,0:T(8,128)(2,1)S(1)}, u32[]{:S(2)}, u32[]{:S(2)}) collective-permute-start(bf16[2,4,4,16,128]{4,3,2,1,0:T(8,128)(2,1)} %get-tuple-element.35), channel_id=1, source_target_pairs={{0,11},{1,10},{2,9},{3,8},{4,15},{5,14},{6,13},{7,12},{8,3},{9,2},... | collective-permute-start | bytes 393224 | tf_op jit(solution)/shard_map/ppermute | solution.py:332
  53.3 0.9 copy-start

commit v4 on v3

--- a/solution.py
+++ b/solution.py
@@ -14,6 +14,7 @@
 MIB = 1 << 20
 ORDER = (12, 1, 13, 2, 14, 3, 15, 4, 8, 5, 9, 6, 10, 7, 11)
 FIRST = 5
+LATE = 3
 
 
 def phase_tiles(freq_count, lag_count, tile):
@@ -198,8 +199,9 @@
     return stacked
 
 
-def cross_kernel(sources, pairs_ref, inverse_ref, *refs):
-    block_refs, out_ref, blocks_ref = refs[: len(sources)], refs[-2], refs[-1]
+def cross_kernel(sources, late, aliased, pairs_ref, inverse_ref, *refs):
+    block_refs = refs[: len(sources)]
+    out_ref, blocks_ref = refs[len(sources) + aliased :]
     block_count, _, days, slots, _, bins = blocks_ref.shape
     rounds, pairs = pairs_ref.shape[0], pairs_ref.shape[1]
     rows = lax.broadcasted_iota(jnp.int32, (8, bins), 0)
@@ -218,32 +220,50 @@
 
     def one_pair(index, carry):
         r, p = index // pairs, index % pairs
-        stacked = pair_stack(pairs_ref[r, p, 0], pairs_ref[r, p, 1], inverse_ref, blocks_ref, rows)
-        for d in range(days):
-            row = pl.multiple_of((r * held + d % held) * slots * slots, 16)
-            for c in range(2):
-                out_ref[(p * days + d) // held, c, pl.ds(row, slots * slots), :] = stacked[d][c]
+        a, b = pairs_ref[r, p, 0], pairs_ref[r, p, 1]
+
+        def work():
+            stacked = pair_stack(a, b, inverse_ref, blocks_ref, rows)
+            for d in range(days):
+                row = pl.multiple_of((r * held + d % held) * slots * slots, 16)
+                for c in range(2):
+                    out_ref[(p * days + d) // held, c, pl.ds(row, slots * slots), :] = stacked[d][c]
+
+        if len(late) == 0 and aliased == 0:
+            work()
+        else:
+            waits = [(x ^ me) == away for x in (a, b) for away in late or sources]
+            waits = functools.reduce(jnp.logical_or, waits)
+            pl.when(jnp.logical_not(waits) if late else waits)(work)
         return carry
 
-    lax.fori_loop(0, rounds * pairs, one_pair, 0, unroll=2)
-
-
-def cross(blocks, sources, inverse, pair_table, devices):
+    lax.fori_loop(0, rounds * pairs, one_pair, 0)
+
+
+def cross(blocks, sources, inverse, pair_table, devices, late=(), started=()):
     parts, days, slots, windows, bins = blocks[0].shape[-5:]
     rounds, pairs, _ = pair_table.shape
     held = days * pairs // devices
+    share = len(sources) / devices
+    work = int(rounds * pairs * days * slots * slots * windows * bins * share)
     return pl.pallas_call(
-        functools.partial(cross_kernel, sources),
+        functools.partial(cross_kernel, sources, late, len(started)),
         in_specs=[pl.BlockSpec(memory_space=pltpu.SMEM)] * 2
-        + [pl.BlockSpec(memory_space=pltpu.VMEM)] * len(blocks),
-        out_specs=pl.BlockSpec(memory_space=pltpu.VMEM),
-        out_shape=jax.ShapeDtypeStruct(
-            (devices, parts, rounds * held * slots * slots, bins), jnp.bfloat16
+        + [pl.BlockSpec(memory_space=pltpu.VMEM)] * (len(blocks) + len(started)),
+        out_specs=[pl.BlockSpec(memory_space=pltpu.VMEM)] * 2,
+        out_shape=[
+            jax.ShapeDtypeStruct(
+                (devices, parts, rounds * held * slots * slots, bins), jnp.bfloat16
+            ),
+            jax.ShapeDtypeStruct((devices, parts, days, slots, windows, bins), jnp.float32),
+        ],
+        input_output_aliases={2 + len(blocks) + n: n for n in range(len(started))},
+        compiler_params=pltpu.CompilerParams(vmem_limit_bytes=40 * MIB),
+        cost_estimate=pl.CostEstimate(
+            flops=16 * work, bytes_accessed=4 << 20, transcendentals=0
         ),
-        scratch_shapes=[pltpu.VMEM((devices, parts, days, slots, windows, bins), jnp.float32)],
-        compiler_params=pltpu.CompilerParams(vmem_limit_bytes=40 * MIB),
-        name="cross",
-    )(pair_table, inverse, *blocks)
+        name="cross_rest" if started else "cross",
+    )(pair_table, inverse, *blocks, *started)
 
 
 def lag_kernel(
@@ -328,10 +348,13 @@
         sources = ORDER + (0,)
         shares = pieces(spectra, block_counts, window_masks, devices, sources[:FIRST], "pack_first")
         shares += pieces(spectra, block_counts, window_masks, devices, sources[FIRST:], "pack_rest")
-        blocks = [
-            lax.ppermute(share, "sta", [(n, n ^ away) for n in range(devices)]) if away else share
-            for share, away in zip(shares, sources)
-        ]
+        blocks = []
+        for n, (share, away) in enumerate(zip(shares, sources)):
+            if 5 <= n < len(ORDER):
+                share, _ = lax.optimization_barrier((share, blocks[n - 5]))
+            if away:
+                share = lax.ppermute(share, "sta", [(m, m ^ away) for m in range(devices)])
+            blocks.append(share)
     else:
         packed = pack(spectra, block_counts, window_masks, devices)
         sources = (None,)
@@ -339,7 +362,22 @@
     weights = window_masks.astype(jnp.float32)
     joint = jnp.einsum("dwa,dwb->dab", weights, weights)
     inverse = (1.0 / jnp.maximum(joint, 1.0)).reshape(-1)
-    stacked = cross(blocks, sources, inverse, pair_table, devices)
+    if len(sources) > 1:
+        late = sources[-1 - LATE : -1]
+        soon = [n for n, away in enumerate(sources) if away not in late]
+        started = cross(
+            [blocks[n] for n in soon],
+            tuple(sources[n] for n in soon),
+            inverse,
+            pair_table,
+            devices,
+            late,
+        )
+        stacked, _ = cross(
+            blocks[-1 - LATE : -1], late, inverse, pair_table, devices, (), tuple(started)
+        )
+    else:
+        stacked, _ = cross(blocks, sources, inverse, pair_table, devices)
     received = lax.all_to_all(stacked, "sta", split_axis=0, concat_axis=0, tiled=True)
     lagged = lags(received, table, 1.0 / math.sqrt(total))
     return lagged.reshape(rounds, held, slots * slots, LAGS)

time: 96.2 us -> 93.1 us (0.968)
  waiting for transfers between devices: 12.6 us -> 7.95 us
  Pallas kernels: 18.7 us -> 21.1 us
    ppermute x15, waiting for transfers between devices: 12.6 us -> 7.95 us  [local(): share = lax.ppermute(share, 'sta', [(m, m ^ away) for m in range(devices)])]
    pallas_call x1 -> x2, Pallas kernels: 6.91 us -> 9.25 us  [cross(): pl.pallas_call(functools.partial(cross_kernel, sources, late, len(started...]
  transfers between devices with their start and end apart: 15 -> 15, of which waited for: 4 -> 3; matrix products, arithmetic and copies ran while one was open for 2% -> 0% of each run, Pallas kernels for 4% -> 10%
where the time goes in v4:
time: 93.1 us; the launch traced here: 92.7 us
  starting transfers between devices  32.8 us (35%)
  blocking collectives  29.5 us (32%)
  Pallas kernels  21.1 us (23%)
  waiting for transfers between devices  7.95 us (9%)
  local copies, waits for them, and re-layouts  1.09 us (1%)
    ppermute x15, starting transfers between devices, local(): share = lax.ppermute(share, 'sta', [(m, m ^ away) for m in range(devices)])  32.8 us
    all_to_all x1, blocking collectives, local(): lax.all_to_all(stacked, 'sta', split_axis=0, concat_axis=0, tiled=True)  29.5 us
    pallas_call x2, Pallas kernels, cross(): pl.pallas_call(functools.partial(cross_kernel, sources, late, len(started...  9.25 us
    ppermute x15, waiting for transfers between devices, local(): share = lax.ppermute(share, 'sta', [(m, m ^ away) for m in range(devices)])  7.95 us
    pallas_call x2, Pallas kernels, pieces(): pl.pallas_call(functools.partial(piece_kernel, aways), in_specs=[pl.Block...  6.43 us
    pallas_call x1, Pallas kernels, lags(): pl.pallas_call(functools.partial(lag_kernel, scale), in_specs=[pl.BlockSp...  5.39 us
  transfers between devices with their start and end apart: 15, of which 3 were waited for; matrix products, arithmetic and copies ran while one was open for 0% of the time, Pallas kernels for 10%

profile of v4, /device:TPU:1, one launch (start us, length us, event | category | flops | bytes accessed | tf_op | source)
XLA Modules:
  0.0 92.7 jit_solution(8343666799885384027)
XLA Ops:
  0.0 3.0 %pack_first.1 = (bf16[2,4,4,16,128]{4,3,2,1,0:T(8,128)(2,1)}, bf16[2,4,4,16,128]{4,3,2,1,0:T(8,128)(2,1)}, bf16[2,4,4,16,128]{4,3,2,1,0:T(8,128)(2,1)}, bf16[2,4...) custom-call(s32[16]{0:T(128)} %counts_ref.3, s32[4,16,16]{2,1,0:T(8,128)} %masks_ref.3, ...), custom_call_target="tpu_custom_call" | custom-call | tf_op jit(solution)/shard_map/pack_first/pallas_call | solution.py:115
  3.1 4.8 %collective-permute-start.9 = (bf16[2,4,4,16,128]{4,3,2,1,0:T(8,128)(2,1)}, bf16[2,4,4,16,128]{4,3,2,1,0:T(8,128)(2,1)S(1)}, u32[]{:S(2)}, u32[]{:S(2)}) collective-permute-start(bf16[2,4,4,16,128]{4,3,2,1,0:T(8,128)(2,1)} %get-tuple-element.49), channel_id=1, source_target_pairs={{0,12},{1,13},{2,14},{3,15},{4,8},{5,9},{6,10},{7,11},{8,4},{9,5},... | collective-permute-start | bytes 393224 | tf_op jit(solution)/shard_map/ppermute | solution.py:356
  7.9 0.9 %collective-permute-start.6 = (bf16[2,4,4,16,128]{4,3,2,1,0:T(8,128)(2,1)}, bf16[2,4,4,16,128]{4,3,2,1,0:T(8,128)(2,1)S(1)}, u32[]{:S(2)}, u32[]{:S(2)}) collective-permute-start(bf16[2,4,4,16,128]{4,3,2,1,0:T(8,128)(2,1)} %get-tuple-element.46), channel_id=1, source_target_pairs={{0,14},{1,15},{2,12},{3,13},{4,10},{5,11},{6,8},{7,9},{8,6},{9,7},... | collective-permute-start | bytes 393224 | tf_op jit(solution)/shard_map/ppermute | solution.py:356
  8.8 0.3 collective-permute-start.3
  9.1 4.0 %collective-permute-start = (bf16[2,4,4,16,128]{4,3,2,1,0:T(8,128)(2,1)}, bf16[2,4,4,16,128]{4,3,2,1,0:T(8,128)(2,1)S(1)}, u32[]{:S(2)}, u32[]{:S(2)}) collective-permute-start(bf16[2,4,4,16,128]{4,3,2,1,0:T(8,128)(2,1)} %get-tuple-element.36), channel_id=1, source_target_pairs={{0,13},{1,12},{2,15},{3,14},{4,9},{5,8},{6,11},{7,10},{8,5},{9,4},... | collective-permute-start | bytes 393224 | tf_op jit(solution)/shard_map/ppermute | solution.py:356
  13.1 3.5 %pack_rest.1 = (bf16[2,4,4,16,128]{4,3,2,1,0:T(8,128)(2,1)}, bf16[2,4,4,16,128]{4,3,2,1,0:T(8,128)(2,1)}, bf16[2,4,4,16,128]{4,3,2,1,0:T(8,128)(2,1)}, bf16[2,4,...) custom-call(s32[16]{0:T(128)} %counts_ref.3, ...), custom_call_target="tpu_custom_call" | custom-call | tf_op jit(solution)/shard_map/pack_rest/pallas_call | solution.py:115
  16.6 1.0 %collective-permute-start.12 = (bf16[2,4,4,16,128]{4,3,2,1,0:T(8,128)(2,1)}, bf16[2,4,4,16,128]{4,3,2,1,0:T(8,128)(2,1)S(1)}, u32[]{:S(2)}, u32[]{:S(2)}) collective-permute-start(bf16[2,4,4,16,128]{4,3,2,1,0:T(8,128)(2,1)} %get-tuple-element.54), channel_id=1, source_target_pairs={{0,15},{1,14},{2,13},{3,12},{4,11},{5,10},{6,9},{7,8},{8,7},{9,6},... | collective-permute-start | bytes 393224 | tf_op jit(solution)/shard_map/ppermute | solution.py:356
  17.6 0.3 collective-permute-start.11
  18.0 9.4 %collective-permute-start.7 = (bf16[2,4,4,16,128]{4,3,2,1,0:T(8,128)(2,1)}, bf16[2,4,4,16,128]{4,3,2,1,0:T(8,128)(2,1)S(1)}, u32[]{:S(2)}, u32[]{:S(2)}) collective-permute-start(bf16[2,4,4,16,128]{4,3,2,1,0:T(8,128)(2,1)} %get-tuple-element.47), channel_id=1, source_target_pairs={{0,5},{1,4},{2,7},{3,6},{4,1},{5,0},{6,3},{7,2},{8,13},{9,12},{10,... | collective-permute-start | bytes 393224 | tf_op jit(solution)/shard_map/ppermute | solution.py:356
  27.3 2.4 %collective-permute-start.1 = (bf16[2,4,4,16,128]{4,3,2,1,0:T(8,128)(2,1)}, bf16[2,4,4,16,128]{4,3,2,1,0:T(8,128)(2,1)S(1)}, u32[]{:S(2)}, u32[]{:S(2)}) collective-permute-start(bf16[2,4,4,16,128]{4,3,2,1,0:T(8,128)(2,1)} %get-tuple-element.37), channel_id=1, source_target_pairs={{0,4},{1,5},{2,6},{3,7},{4,0},{5,1},{6,2},{7,3},{8,12},{9,13},{10,... | collective-permute-start | bytes 393224 | tf_op jit(solution)/shard_map/ppermute | solution.py:356
  29.9 1.9 %collective-permute-start.14 = (bf16[2,4,4,16,128]{4,3,2,1,0:T(8,128)(2,1)}, bf16[2,4,4,16,128]{4,3,2,1,0:T(8,128)(2,1)S(1)}, u32[]{:S(2)}, u32[]{:S(2)}) collective-permute-start(bf16[2,4,4,16,128]{4,3,2,1,0:T(8,128)(2,1)} %get-tuple-element.58), channel_id=1, source_target_pairs={{0,6},{1,7},{2,4},{3,5},{4,2},{5,3},{6,0},{7,1},{8,14},{9,15},{10,... | collective-permute-start | bytes 393224 | tf_op jit(solution)/shard_map/ppermute | solution.py:356
  31.8 1.2 %collective-permute-start.13 = (bf16[2,4,4,16,128]{4,3,2,1,0:T(8,128)(2,1)}, bf16[2,4,4,16,128]{4,3,2,1,0:T(8,128)(2,1)S(1)}, u32[]{:S(2)}, u32[]{:S(2)}) collective-permute-start(bf16[2,4,4,16,128]{4,3,2,1,0:T(8,128)(2,1)} %get-tuple-element.56), channel_id=1, source_target_pairs={{0,9},{1,8},{2,11},{3,10},{4,13},{5,12},{6,15},{7,14},{8,1},{9,0},... | collective-permute-start | bytes 393224 | tf_op jit(solution)/shard_map/ppermute | solution.py:356
  33.1 2.8 %collective-permute-start.8 = (bf16[2,4,4,16,128]{4,3,2,1,0:T(8,128)(2,1)}, bf16[2,4,4,16,128]{4,3,2,1,0:T(8,128)(2,1)S(1)}, u32[]{:S(2)}, u32[]{:S(2)}) collective-permute-start(bf16[2,4,4,16,128]{4,3,2,1,0:T(8,128)(2,1)} %get-tuple-element.48), channel_id=1, source_target_pairs={{0,11},{1,10},{2,9},{3,8},{4,15},{5,14},{6,13},{7,12},{8,3},{9,2},... | collective-permute-start | bytes 393224 | tf_op jit(solution)/shard_map/ppermute | solution.py:356
  35.9 0.7 collective-permute-done.4.refs_8_
  36.7 2.0 %collective-permute-start.5 = (bf16[2,4,4,16,128]{4,3,2,1,0:T(8,128)(2,1)}, bf16[2,4,4,16,128]{4,3,2,1,0:T(8,128)(2,1)S(1)}, u32[]{:S(2)}, u32[]{:S(2)}) collective-permute-start(bf16[2,4,4,16,128]{4,3,2,1,0:T(8,128)(2,1)} %get-tuple-element.43), channel_id=1, source_target_pairs={{0,7},{1,6},{2,5},{3,4},{4,3},{5,2},{6,1},{7,0},{8,15},{9,14},{10,... | collective-permute-start | bytes 393224 | tf_op jit(solution)/shard_map/ppermute | solution.py:356
  38.7 1.5 %collective-permute-start.2 = (bf16[2,4,4,16,128]{4,3,2,1,0:T(8,128)(2,1)}, bf16[2,4,4,16,128]{4,3,2,1,0:T(8,128)(2,1)S(1)}, u32[]{:S(2)}, u32[]{:S(2)}) collective-permute-start(bf16[2,4,4,16,128]{4,3,2,1,0:T(8,128)(2,1)} %get-tuple-element.38), channel_id=1, source_target_pairs={{0,10},{1,11},{2,8},{3,9},{4,14},{5,15},{6,12},{7,13},{8,2},{9,3},... | collective-permute-start | bytes 393224 | tf_op jit(solution)/shard_map/ppermute | solution.py:356
  40.2 0.2 fusion
  40.5 2.9 %collective-permute-done.14.refs_11_ = bf16[2,4,4,16,128]{4,3,2,1,0:T(8,128)(2,1)S(1)} collective-permute-done((bf16[2,4,4,16,128]{4,3,2,1,0:T(8,128)(2,1)}, bf16[2,4,4,16,128]{4,3,2,1,0:T(8,128)(2,1)S(1)}, u32[]{:S(2)}, u32[]{:S(2)}) %collective-permute-start.14) | collective-permute-done | bytes 131104 | tf_op jit(solution)/shard_map/ppermute | solution.py:356
  43.4 0.9 copy-done
  44.3 5.6 %cross.1 = (bf16[16,2,128,128]{3,2,1,0:T(8,128)(2,1)S(1)}, f32[16,2,4,4,16,128]{5,4,3,2,1,0:T(8,128)S(1)}) custom-call(s32[4,8,2]{2,1,0:T(8,128)S(1)} %copy.10.pairs_ref, f32[1024]{0:T(1024)S(1)} %reshape.6.inverse_ref, bf16[2,4,4,16,128]{4,3,2,1,0:T(8,128)(2,1)S(1)} %collective-permute-done.9.refs_0_, ...), custom_call_target="tpu_custom_call" | custom-call | flops 54525952 | bytes 4194304 | tf_op jit(solution)/shard_map/cross/pallas_call | solution.py:249
  49.9 4.2 %collective-permute-done.2.refs_0_ = bf16[2,4,4,16,128]{4,3,2,1,0:T(8,128)(2,1)S(1)} collective-permute-done((bf16[2,4,4,16,128]{4,3,2,1,0:T(8,128)(2,1)}, bf16[2,4,4,16,128]{4,3,2,1,0:T(8,128)(2,1)S(1)}, u32[]{:S(2)}, u32[]{:S(2)}) %collective-permute-start.2) | collective-permute-done | bytes 131104 | tf_op jit(solution)/shard_map/ppermute | solution.py:356
  54.2 3.7 %cross_rest.1 = (bf16[16,2,128,128]{3,2,1,0:T(8,128)(2,1)S(1)}, f32[16,2,4,4,16,128]{5,4,3,2,1,0:T(8,128)S(1)}) custom-call(s32[4,8,2]{2,1,0:T(8,128)S(1)} %copy.10.pairs_ref, f32[1024]{0:T(1024)S(1)} %reshape.6.inverse_ref, bf16[2,4,4,16,128]{4,3,2,1,0:T(8,128)(2,1)S(1)} %collective-permute-done.2.refs_0_, ...), custom_call_target="tpu_custom_call", output_to_operand_aliasing={{0}: (5, {}), {1}: (6, {})} | custom-call | flops 12582912 | bytes 4194304 | tf_op jit(solution)/shard_map/cross_rest/pallas_call | solution.py:249
  57.8 29.5 %all_to_all.5.stacked_ref = bf16[16,2,128,128]{3,2,1,0:T(8,128)(2,1)S(1)} all-to-all(bf16[16,2,128,128]{3,2,1,0:T(8,128)(2,1)S(1)} %get-tuple-element.62), channel_id=1, replica_groups=mesh['grp'=2,'sta'=16] {'sta'}, dimensions={0} | all-to-all | bytes 2097152 | tf_op jit(solution)/shard_map/all_to_all | solution.py:381
  87.3 5.4 %lags.1 = f32[128,2048]{1,0:T(8,128)} custom-call(bf16[16,2,128,128]{3,2,1,0:T(8,128)(2,1)S(1)} %all_to_all.5.stacked_ref, bf16[4,2,2048,256]{3,2,1,0:T(8,128)(2,1)} %constant.4.clone.table_ref), custom_call_target="tpu_custom_call" | custom-call | tf_op jit(solution)/shard_map/lags/pallas_call | solution.py:322
  (21 shorter events, 0.3 us)
Async XLA Ops:
  0.0 40.2 %copy-start.1 = (s32[4,16,16]{2,1,0:T(8,128)S(1)}, s32[4,16,16]{2,1,0:T(8,128)}, u32[]{:S(2)}) copy-start(s32[4,16,16]{2,1,0:T(8,128)} %masks_ref.3) | copy-start | bytes 12292
  0.0 29.8 %copy-start.2 = (s32[4,8,2]{1,2,0:T(2,128)S(1)}, s32[4,8,2]{1,2,0:T(2,128)}, u32[]{:S(2)}) copy-start(s32[4,8,2]{1,2,0:T(2,128)} %param.8) | copy-start | bytes 772
  3.0 13.6 %collective-permute-start.10 = (bf16[2,4,4,16,128]{4,3,2,1,0:T(8,128)(2,1)}, bf16[2,4,4,16,128]{4,3,2,1,0:T(8,128)(2,1)S(1)}, u32[]{:S(2)}, u32[]{:S(2)}) collective-permute-start(bf16[2,4,4,16,128]{4,3,2,1,0:T(8,128)(2,1)} %get-tuple-element.50), channel_id=1, source_target_pairs={{0,1},{1,0},{2,3},{3,2},{4,5},{5,4},{6,7},{7,6},{8,9},{9,8},{10,11... | collective-permute-start | bytes 393224 | tf_op jit(solution)/shard_map/ppermute | solution.py:356
  3.1 14.5 %collective-permute-start.9 = (bf16[2,4,4,16,128]{4,3,2,1,0:T(8,128)(2,1)}, bf16[2,4,4,16,128]{4,3,2,1,0:T(8,128)(2,1)S(1)}, u32[]{:S(2)}, u32[]{:S(2)}) collective-permute-start(bf16[2,4,4,16,128]{4,3,2,1,0:T(8,128)(2,1)} %get-tuple-element.49), channel_id=1, source_target_pairs={{0,12},{1,13},{2,14},{3,15},{4,8},{5,9},{6,10},{7,11},{8,4},{9,5},... | collective-permute-start | bytes 393224 | tf_op jit(solution)/shard_map/ppermute | solution.py:356
  7.9 10.1 %collective-permute-start.6 = (bf16[2,4,4,16,128]{4,3,2,1,0:T(8,128)(2,1)}, bf16[2,4,4,16,128]{4,3,2,1,0:T(8,128)(2,1)S(1)}, u32[]{:S(2)}, u32[]{:S(2)}) collective-permute-start(bf16[2,4,4,16,128]{4,3,2,1,0:T(8,128)(2,1)} %get-tuple-element.46), channel_id=1, source_target_pairs={{0,14},{1,15},{2,12},{3,13},{4,10},{5,11},{6,8},{7,9},{8,6},{9,7},... | collective-permute-start | bytes 393224 | tf_op jit(solution)/shard_map/ppermute | solution.py:356
  8.8 18.5 %collective-permute-start.3 = (bf16[2,4,4,16,128]{4,3,2,1,0:T(8,128)(2,1)}, bf16[2,4,4,16,128]{4,3,2,1,0:T(8,128)(2,1)S(1)}, u32[]{:S(2)}, u32[]{:S(2)}) collective-permute-start(bf16[2,4,4,16,128]{4,3,2,1,0:T(8,128)(2,1)} %get-tuple-element.41), channel_id=1, source_target_pairs={{0,2},{1,3},{2,0},{3,1},{4,6},{5,7},{6,4},{7,5},{8,10},{9,11},{10,... | collective-permute-start | bytes 393224 | tf_op jit(solution)/shard_map/ppermute | solution.py:356
  9.1 18.2 %collective-permute-start = (bf16[2,4,4,16,128]{4,3,2,1,0:T(8,128)(2,1)}, bf16[2,4,4,16,128]{4,3,2,1,0:T(8,128)(2,1)S(1)}, u32[]{:S(2)}, u32[]{:S(2)}) collective-permute-start(bf16[2,4,4,16,128]{4,3,2,1,0:T(8,128)(2,1)} %get-tuple-element.36), channel_id=1, source_target_pairs={{0,13},{1,12},{2,15},{3,14},{4,9},{5,8},{6,11},{7,10},{8,5},{9,4},... | collective-permute-start | bytes 393224 | tf_op jit(solution)/shard_map/ppermute | solution.py:356
  16.6 13.3 %collective-permute-start.12 = (bf16[2,4,4,16,128]{4,3,2,1,0:T(8,128)(2,1)}, bf16[2,4,4,16,128]{4,3,2,1,0:T(8,128)(2,1)S(1)}, u32[]{:S(2)}, u32[]{:S(2)}) collective-permute-start(bf16[2,4,4,16,128]{4,3,2,1,0:T(8,128)(2,1)} %get-tuple-element.54), channel_id=1, source_target_pairs={{0,15},{1,14},{2,13},{3,12},{4,11},{5,10},{6,9},{7,8},{8,7},{9,6},... | collective-permute-start | bytes 393224 | tf_op jit(solution)/shard_map/ppermute | solution.py:356
  17.6 14.2 %collective-permute-start.11 = (bf16[2,4,4,16,128]{4,3,2,1,0:T(8,128)(2,1)}, bf16[2,4,4,16,128]{4,3,2,1,0:T(8,128)(2,1)S(1)}, u32[]{:S(2)}, u32[]{:S(2)}) collective-permute-start(bf16[2,4,4,16,128]{4,3,2,1,0:T(8,128)(2,1)} %get-tuple-element.52), channel_id=1, source_target_pairs={{0,3},{1,2},{2,1},{3,0},{4,7},{5,6},{6,5},{7,4},{8,11},{9,10},{10,... | collective-permute-start | bytes 393224 | tf_op jit(solution)/shard_map/ppermute | solution.py:356
  18.0 15.1 %collective-permute-start.7 = (bf16[2,4,4,16,128]{4,3,2,1,0:T(8,128)(2,1)}, bf16[2,4,4,16,128]{4,3,2,1,0:T(8,128)(2,1)S(1)}, u32[]{:S(2)}, u32[]{:S(2)}) collective-permute-start(bf16[2,4,4,16,128]{4,3,2,1,0:T(8,128)(2,1)} %get-tuple-element.47), channel_id=1, source_target_pairs={{0,5},{1,4},{2,7},{3,6},{4,1},{5,0},{6,3},{7,2},{8,13},{9,12},{10,... | collective-permute-start | bytes 393224 | tf_op jit(solution)/shard_map/ppermute | solution.py:356
  27.3 9.3 %collective-permute-start.4 = (bf16[2,4,4,16,128]{4,3,2,1,0:T(8,128)(2,1)}, bf16[2,4,4,16,128]{4,3,2,1,0:T(8,128)(2,1)S(1)}, u32[]{:S(2)}, u32[]{:S(2)}) collective-permute-start(bf16[2,4,4,16,128]{4,3,2,1,0:T(8,128)(2,1)} %get-tuple-element.42), channel_id=1, source_target_pairs={{0,8},{1,9},{2,10},{3,11},{4,12},{5,13},{6,14},{7,15},{8,0},{9,1},... | collective-permute-start | bytes 393224 | tf_op jit(solution)/shard_map/ppermute | solution.py:356
  27.3 11.3 %collective-permute-start.1 = (bf16[2,4,4,16,128]{4,3,2,1,0:T(8,128)(2,1)}, bf16[2,4,4,16,128]{4,3,2,1,0:T(8,128)(2,1)S(1)}, u32[]{:S(2)}, u32[]{:S(2)}) collective-permute-start(bf16[2,4,4,16,128]{4,3,2,1,0:T(8,128)(2,1)} %get-tuple-element.37), channel_id=1, source_target_pairs={{0,4},{1,5},{2,6},{3,7},{4,0},{5,1},{6,2},{7,3},{8,12},{9,13},{10,... | collective-permute-start | bytes 393224 | tf_op jit(solution)/shard_map/ppermute | solution.py:356
  29.9 13.5 %collective-permute-start.14 = (bf16[2,4,4,16,128]{4,3,2,1,0:T(8,128)(2,1)}, bf16[2,4,4,16,128]{4,3,2,1,0:T(8,128)(2,1)S(1)}, u32[]{:S(2)}, u32[]{:S(2)}) collective-permute-start(bf16[2,4,4,16,128]{4,3,2,1,0:T(8,128)(2,1)} %get-tuple-element.58), channel_id=1, source_target_pairs={{0,6},{1,7},{2,4},{3,5},{4,2},{5,3},{6,0},{7,1},{8,14},{9,15},{10,... | collective-permute-start | bytes 393224 | tf_op jit(solution)/shard_map/ppermute | solution.py:356
  31.8 11.6 %collective-permute-start.13 = (bf16[2,4,4,16,128]{4,3,2,1,0:T(8,128)(2,1)}, bf16[2,4,4,16,128]{4,3,2,1,0:T(8,128)(2,1)S(1)}, u32[]{:S(2)}, u32[]{:S(2)}) collective-permute-start(bf16[2,4,4,16,128]{4,3,2,1,0:T(8,128)(2,1)} %get-tuple-element.56), channel_id=1, source_target_pairs={{0,9},{1,8},{2,11},{3,10},{4,13},{5,12},{6,15},{7,14},{8,1},{9,0},... | collective-permute-start | bytes 393224 | tf_op jit(solution)/shard_map/ppermute | solution.py:356
  33.1 16.8 %collective-permute-start.8 = (bf16[2,4,4,16,128]{4,3,2,1,0:T(8,128)(2,1)}, bf16[2,4,4,16,128]{4,3,2,1,0:T(8,128)(2,1)S(1)}, u32[]{:S(2)}, u32[]{:S(2)}) collective-permute-start(bf16[2,4,4,16,128]{4,3,2,1,0:T(8,128)(2,1)} %get-tuple-element.48), channel_id=1, source_target_pairs={{0,11},{1,10},{2,9},{3,8},{4,15},{5,14},{6,13},{7,12},{8,3},{9,2},... | collective-permute-start | bytes 393224 | tf_op jit(solution)/shard_map/ppermute | solution.py:356
  36.7 13.2 %collective-permute-start.5 = (bf16[2,4,4,16,128]{4,3,2,1,0:T(8,128)(2,1)}, bf16[2,4,4,16,128]{4,3,2,1,0:T(8,128)(2,1)S(1)}, u32[]{:S(2)}, u32[]{:S(2)}) collective-permute-start(bf16[2,4,4,16,128]{4,3,2,1,0:T(8,128)(2,1)} %get-tuple-element.43), channel_id=1, source_target_pairs={{0,7},{1,6},{2,5},{3,4},{4,3},{5,2},{6,1},{7,0},{8,15},{9,14},{10,... | collective-permute-start | bytes 393224 | tf_op jit(solution)/shard_map/ppermute | solution.py:356
  38.7 15.5 %collective-permute-start.2 = (bf16[2,4,4,16,128]{4,3,2,1,0:T(8,128)(2,1)}, bf16[2,4,4,16,128]{4,3,2,1,0:T(8,128)(2,1)S(1)}, u32[]{:S(2)}, u32[]{:S(2)}) collective-permute-start(bf16[2,4,4,16,128]{4,3,2,1,0:T(8,128)(2,1)} %get-tuple-element.38), channel_id=1, source_target_pairs={{0,10},{1,11},{2,8},{3,9},{4,14},{5,15},{6,12},{7,13},{8,2},{9,3},... | collective-permute-start | bytes 393224 | tf_op jit(solution)/shard_map/ppermute | solution.py:356
  43.4 0.9 copy-start

commit v5 on v4

--- a/solution.py
+++ b/solution.py
@@ -200,8 +200,14 @@
 
 
 def cross_kernel(sources, late, aliased, pairs_ref, inverse_ref, *refs):
-    block_refs = refs[: len(sources)]
-    out_ref, blocks_ref = refs[len(sources) + aliased :]
+    block_refs, refs = refs[: len(sources)], refs[len(sources) + aliased :]
+    if late:
+        table_ref, out_ref, blocks_ref, held_ref, sem = refs
+        share_refs = ()
+        fetch = pltpu.make_async_copy(table_ref, held_ref, sem)
+        fetch.start()
+    else:
+        out_ref, blocks_ref, *share_refs = refs
     block_count, _, days, slots, _, bins = blocks_ref.shape
     rounds, pairs = pairs_ref.shape[0], pairs_ref.shape[1]
     rows = lax.broadcasted_iota(jnp.int32, (8, bins), 0)
@@ -238,49 +244,60 @@
         return carry
 
     lax.fori_loop(0, rounds * pairs, one_pair, 0)
-
-
-def cross(blocks, sources, inverse, pair_table, devices, late=(), started=()):
+    for share_ref, away in zip(share_refs, (0,) + ORDER):
+        share_ref[...] = out_ref[me ^ away]
+    if late:
+        fetch.wait()
+
+
+def cross(blocks, sources, inverse, pair_table, devices, late=(), started=(), table=None):
     parts, days, slots, windows, bins = blocks[0].shape[-5:]
     rounds, pairs, _ = pair_table.shape
     held = days * pairs // devices
     share = len(sources) / devices
+    stack = rounds * held * slots * slots
+    spread = devices if started else 0
+    tables = [] if table is None else [table]
+    wide = 4 * devices * parts * days * slots * windows * max(bins, 128)
     work = int(rounds * pairs * days * slots * slots * windows * bins * share)
     return pl.pallas_call(
         functools.partial(cross_kernel, sources, late, len(started)),
         in_specs=[pl.BlockSpec(memory_space=pltpu.SMEM)] * 2
-        + [pl.BlockSpec(memory_space=pltpu.VMEM)] * (len(blocks) + len(started)),
-        out_specs=[pl.BlockSpec(memory_space=pltpu.VMEM)] * 2,
+        + [pl.BlockSpec(memory_space=pltpu.VMEM)] * (len(blocks) + len(started))
+        + [pl.BlockSpec(memory_space=pl.ANY)] * len(tables),
+        out_specs=[pl.BlockSpec(memory_space=pltpu.VMEM)] * (2 + spread + len(tables)),
         out_shape=[
-            jax.ShapeDtypeStruct(
-                (devices, parts, rounds * held * slots * slots, bins), jnp.bfloat16
-            ),
+            jax.ShapeDtypeStruct((devices, parts, stack, bins), jnp.bfloat16),
             jax.ShapeDtypeStruct((devices, parts, days, slots, windows, bins), jnp.float32),
-        ],
+        ]
+        + [jax.ShapeDtypeStruct((parts, stack, bins), jnp.bfloat16)] * spread
+        + [jax.ShapeDtypeStruct(table.shape, table.dtype) for table in tables],
+        scratch_shapes=[pltpu.SemaphoreType.DMA] * len(tables),
         input_output_aliases={2 + len(blocks) + n: n for n in range(len(started))},
-        compiler_params=pltpu.CompilerParams(vmem_limit_bytes=40 * MIB),
+        compiler_params=pltpu.CompilerParams(vmem_limit_bytes=38 * MIB if late else wide + 20 * MIB),
         cost_estimate=pl.CostEstimate(
             flops=16 * work, bytes_accessed=4 << 20, transcendentals=0
         ),
         name="cross_rest" if started else "cross",
-    )(pair_table, inverse, *blocks, *started)
-
-
-def lag_kernel(
-    scale, stacked_ref, table_ref, out_ref, left_ref, held_ref, lagged_ref, in_sems, out_sems
-):
+    )(pair_table, inverse, *blocks, *started, *tables)
+
+
+def lag_kernel(scale, sources, *refs):
+    stacked_refs, refs = refs[: len(sources)], refs[len(sources) :]
+    table_ref, out_ref, left_ref, lagged_ref, out_sems = refs
     tiles, _, depth, tile = table_ref.shape
     parts, rows, _ = left_ref.shape
     half = tiles * tile
-    loads = [
-        pltpu.make_async_copy(table_ref.at[t], held_ref.at[t], in_sems.at[t]) for t in range(tiles)
-    ]
-    for t in reversed(range(tiles)):
-        loads[t].start()
-    devices, _, _, bins = stacked_ref.shape
-    for c in range(parts):
-        for src in range(devices):
-            left_ref[c, :, src * bins : (src + 1) * bins] = stacked_ref[src, c]
+    for stacked_ref, source in zip(stacked_refs, sources):
+        bins = stacked_ref.shape[-1]
+        if source is None:
+            for src in range(stacked_ref.shape[0]):
+                for c in range(parts):
+                    left_ref[c, :, src * bins : (src + 1) * bins] = stacked_ref[src, c]
+        else:
+            at = pl.multiple_of((lax.axis_index("sta") ^ source) * bins, 128)
+            for c in range(parts):
+                left_ref[c, :, pl.ds(at, bins)] = stacked_ref[c]
 
     turn = lax.broadcasted_iota(jnp.int32, (depth, 128), 0) % 4
     cosine = jnp.where(turn == 0, 1.0, jnp.where(turn == 2, -1.0, 0.0)).astype(jnp.bfloat16)
@@ -292,9 +309,8 @@
     flip = (128 - lane) % 128
     stores = []
     for t in reversed(range(tiles)):
-        loads[t].wait()
-        even = jnp.dot(left_ref[0], held_ref[t, 0], preferred_element_type=jnp.float32) * scale
-        odd = jnp.dot(left_ref[1], held_ref[t, 1], preferred_element_type=jnp.float32) * scale
+        even = jnp.dot(left_ref[0], table_ref[t, 0], preferred_element_type=jnp.float32) * scale
+        odd = jnp.dot(left_ref[1], table_ref[t, 1], preferred_element_type=jnp.float32) * scale
         lagged_ref[:, half + t * tile : half + (t + 1) * tile] = even + odd
         gap = even - odd
         for sub in reversed(range(tile // 128)):
@@ -315,28 +331,36 @@
         store.wait()
 
 
-def lags(stacked, table, scale):
-    devices, parts, rows, bins = stacked.shape
+def lags(stacked, sources, table, scale):
+    parts, rows, _ = stacked[0].shape[-3:]
     tiles, _, depth, tile = table.shape
     lag_count = 2 * tiles * tile
     return pl.pallas_call(
-        functools.partial(lag_kernel, scale),
-        in_specs=[
-            pl.BlockSpec(memory_space=pltpu.VMEM),
-            pl.BlockSpec(memory_space=pl.ANY),
-        ],
+        functools.partial(lag_kernel, scale, sources),
+        in_specs=[pl.BlockSpec(memory_space=pltpu.VMEM)] * (len(stacked) + 1),
         out_specs=pl.BlockSpec(memory_space=pl.ANY),
         out_shape=jax.ShapeDtypeStruct((rows, lag_count), jnp.float32),
         scratch_shapes=[
             pltpu.VMEM((parts, rows, depth), jnp.bfloat16),
-            pltpu.VMEM(table.shape, jnp.bfloat16),
             pltpu.VMEM((rows, lag_count), jnp.float32),
-            pltpu.SemaphoreType.DMA((tiles,)),
             pltpu.SemaphoreType.DMA((2 * tiles,)),
         ],
-        compiler_params=pltpu.CompilerParams(vmem_limit_bytes=48 * MIB),
+        compiler_params=pltpu.CompilerParams(vmem_limit_bytes=20 * MIB),
         name="lags",
-    )(stacked, table)
+    )(*stacked, table)
+
+
+def swap(shares, sources, devices):
+    received = []
+    sent = []
+    for share, away in zip(shares, sources):
+        if away:
+            if len(sent) >= 5:
+                share, _ = lax.optimization_barrier((share, sent[-5]))
+            share = lax.ppermute(share, "sta", [(n, n ^ away) for n in range(devices)])
+            sent.append(share)
+        received.append(share)
+    return received
 
 
 def local(table, spectra, block_counts, window_masks, pair_table):
@@ -348,13 +372,7 @@
         sources = ORDER + (0,)
         shares = pieces(spectra, block_counts, window_masks, devices, sources[:FIRST], "pack_first")
         shares += pieces(spectra, block_counts, window_masks, devices, sources[FIRST:], "pack_rest")
-        blocks = []
-        for n, (share, away) in enumerate(zip(shares, sources)):
-            if 5 <= n < len(ORDER):
-                share, _ = lax.optimization_barrier((share, blocks[n - 5]))
-            if away:
-                share = lax.ppermute(share, "sta", [(m, m ^ away) for m in range(devices)])
-            blocks.append(share)
+        blocks = swap(shares, sources, devices)
     else:
         packed = pack(spectra, block_counts, window_masks, devices)
         sources = (None,)
@@ -365,21 +383,24 @@
     if len(sources) > 1:
         late = sources[-1 - LATE : -1]
         soon = [n for n, away in enumerate(sources) if away not in late]
-        started = cross(
+        *started, table = cross(
             [blocks[n] for n in soon],
             tuple(sources[n] for n in soon),
             inverse,
             pair_table,
             devices,
             late,
+            table=table,
         )
-        stacked, _ = cross(
+        shares = cross(
             blocks[-1 - LATE : -1], late, inverse, pair_table, devices, (), tuple(started)
-        )
+        )[2:]
+        sources = (0,) + ORDER
+        received = swap(shares, sources, devices)
     else:
         stacked, _ = cross(blocks, sources, inverse, pair_table, devices)
-    received = lax.all_to_all(stacked, "sta", split_axis=0, concat_axis=0, tiled=True)
-    lagged = lags(received, table, 1.0 / math.sqrt(total))
+        received = [lax.all_to_all(stacked, "sta", split_axis=0, concat_axis=0, tiled=True)]
+    lagged = lags(received, sources, table, 1.0 / math.sqrt(total))
     return lagged.reshape(rounds, held, slots * slots, LAGS)
 
 

time: 93.1 us -> 88.4 us (0.950)
  blocking collectives: 29.5 us -> 0 us
  starting transfers between devices: 32.8 us -> 52.7 us
  waiting for transfers between devices: 7.95 us -> 15.3 us
  Pallas kernels: 21.1 us -> 18.7 us
    all_to_all x1 -> x0, blocking collectives: 29.5 us -> none  [local(): lax.all_to_all(stacked, 'sta', split_axis=0, concat_axis=0, tiled=True)]
    ppermute x15 -> x30, starting transfers between devices: 32.8 us -> 52.7 us  [swap(): share = lax.ppermute(share, 'sta', [(n, n ^ away) for n in range(devices)])]
    ppermute x15 -> x30, waiting for transfers between devices: 7.95 us -> 15.3 us  [swap(): share = lax.ppermute(share, 'sta', [(n, n ^ away) for n in range(devices)])]
    pallas_call x1, Pallas kernels: 5.39 us -> 2.91 us  [lags(): pl.pallas_call(functools.partial(lag_kernel, scale, sources), in_specs=[p...]
  transfers between devices with their start and end apart: 15 -> 30, of which waited for: 3 -> 7; matrix products, arithmetic and copies ran while one was open for 0% -> 0% of each run, Pallas kernels for 10% -> 10%
where the time goes in v5:
time: 88.4 us; the launch traced here: 88.1 us
  starting transfers between devices  52.7 us (60%)
  Pallas kernels  18.7 us (21%)
  waiting for transfers between devices  15.3 us (17%)
  local copies, waits for them, and re-layouts  1.09 us (1%)
    ppermute x30, starting transfers between devices, swap(): share = lax.ppermute(share, 'sta', [(n, n ^ away) for n in range(devices)])  52.7 us
    ppermute x30, waiting for transfers between devices, swap(): share = lax.ppermute(share, 'sta', [(n, n ^ away) for n in range(devices)])  15.3 us
    pallas_call x2, Pallas kernels, cross(): pl.pallas_call(functools.partial(cross_kernel, sources, late, len(started...  9.38 us
    pallas_call x2, Pallas kernels, pieces(): pl.pallas_call(functools.partial(piece_kernel, aways), in_specs=[pl.Block...  6.44 us
    pallas_call x1, Pallas kernels, lags(): pl.pallas_call(functools.partial(lag_kernel, scale, sources), in_specs=[p...  2.91 us
  transfers between devices with their start and end apart: 30, of which 7 were waited for; matrix products, arithmetic and copies ran while one was open for 0% of the time, Pallas kernels for 10%

profile of v5, /device:TPU:1, one launch (start us, length us, event | category | flops | bytes accessed | tf_op | source)
XLA Modules:
  0.0 88.1 jit_solution(14847775917503892638)
XLA Ops:
  0.0 3.0 %pack_first.1 = (bf16[2,4,4,16,128]{4,3,2,1,0:T(8,128)(2,1)}, bf16[2,4,4,16,128]{4,3,2,1,0:T(8,128)(2,1)}, bf16[2,4,4,16,128]{4,3,2,1,0:T(8,128)(2,1)}, bf16[2,4...) custom-call(s32[16]{0:T(128)} %counts_ref.3, s32[4,16,16]{2,1,0:T(8,128)} %masks_ref.3, ...), custom_call_target="tpu_custom_call" | custom-call | tf_op jit(solution)/shard_map/pack_first/pallas_call | solution.py:115
  3.1 4.8 %collective-permute-start.9 = (bf16[2,4,4,16,128]{4,3,2,1,0:T(8,128)(2,1)}, bf16[2,4,4,16,128]{4,3,2,1,0:T(8,128)(2,1)S(1)}, u32[]{:S(2)}, u32[]{:S(2)}) collective-permute-start(bf16[2,4,4,16,128]{4,3,2,1,0:T(8,128)(2,1)} %get-tuple-element.75), channel_id=1, source_target_pairs={{0,12},{1,13},{2,14},{3,15},{4,8},{5,9},{6,10},{7,11},{8,4},{9,5},... | collective-permute-start | bytes 393224 | tf_op jit(solution)/shard_map/ppermute | solution.py:360
  9.1 4.0 %collective-permute-start = (bf16[2,4,4,16,128]{4,3,2,1,0:T(8,128)(2,1)}, bf16[2,4,4,16,128]{4,3,2,1,0:T(8,128)(2,1)S(1)}, u32[]{:S(2)}, u32[]{:S(2)}) collective-permute-start(bf16[2,4,4,16,128]{4,3,2,1,0:T(8,128)(2,1)} %get-tuple-element.62), channel_id=1, source_target_pairs={{0,13},{1,12},{2,15},{3,14},{4,9},{5,8},{6,11},{7,10},{8,5},{9,4},... | collective-permute-start | bytes 393224 | tf_op jit(solution)/shard_map/ppermute | solution.py:360
  13.1 3.5 %pack_rest.1 = (bf16[2,4,4,16,128]{4,3,2,1,0:T(8,128)(2,1)}, bf16[2,4,4,16,128]{4,3,2,1,0:T(8,128)(2,1)}, bf16[2,4,4,16,128]{4,3,2,1,0:T(8,128)(2,1)}, bf16[2,4,...) custom-call(s32[16]{0:T(128)} %counts_ref.3, ...), custom_call_target="tpu_custom_call" | custom-call | tf_op jit(solution)/shard_map/pack_rest/pallas_call | solution.py:115
  18.0 9.4 %collective-permute-start.7 = (bf16[2,4,4,16,128]{4,3,2,1,0:T(8,128)(2,1)}, bf16[2,4,4,16,128]{4,3,2,1,0:T(8,128)(2,1)S(1)}, u32[]{:S(2)}, u32[]{:S(2)}) collective-permute-start(bf16[2,4,4,16,128]{4,3,2,1,0:T(8,128)(2,1)} %get-tuple-element.73), channel_id=1, source_target_pairs={{0,5},{1,4},{2,7},{3,6},{4,1},{5,0},{6,3},{7,2},{8,13},{9,12},{10,... | collective-permute-start | bytes 393224 | tf_op jit(solution)/shard_map/ppermute | solution.py:360
  27.3 2.5 %collective-permute-start.1 = (bf16[2,4,4,16,128]{4,3,2,1,0:T(8,128)(2,1)}, bf16[2,4,4,16,128]{4,3,2,1,0:T(8,128)(2,1)S(1)}, u32[]{:S(2)}, u32[]{:S(2)}) collective-permute-start(bf16[2,4,4,16,128]{4,3,2,1,0:T(8,128)(2,1)} %get-tuple-element.63), channel_id=1, source_target_pairs={{0,4},{1,5},{2,6},{3,7},{4,0},{5,1},{6,2},{7,3},{8,12},{9,13},{10,... | collective-permute-start | bytes 393224 | tf_op jit(solution)/shard_map/ppermute | solution.py:360
  29.9 1.9 %collective-permute-start.14 = (bf16[2,4,4,16,128]{4,3,2,1,0:T(8,128)(2,1)}, bf16[2,4,4,16,128]{4,3,2,1,0:T(8,128)(2,1)S(1)}, u32[]{:S(2)}, u32[]{:S(2)}) collective-permute-start(bf16[2,4,4,16,128]{4,3,2,1,0:T(8,128)(2,1)} %get-tuple-element.84), channel_id=1, source_target_pairs={{0,6},{1,7},{2,4},{3,5},{4,2},{5,3},{6,0},{7,1},{8,14},{9,15},{10,... | collective-permute-start | bytes 393224 | tf_op jit(solution)/shard_map/ppermute | solution.py:360
  33.1 2.8 %collective-permute-start.8 = (bf16[2,4,4,16,128]{4,3,2,1,0:T(8,128)(2,1)}, bf16[2,4,4,16,128]{4,3,2,1,0:T(8,128)(2,1)S(1)}, u32[]{:S(2)}, u32[]{:S(2)}) collective-permute-start(bf16[2,4,4,16,128]{4,3,2,1,0:T(8,128)(2,1)} %get-tuple-element.74), channel_id=1, source_target_pairs={{0,11},{1,10},{2,9},{3,8},{4,15},{5,14},{6,13},{7,12},{8,3},{9,2},... | collective-permute-start | bytes 393224 | tf_op jit(solution)/shard_map/ppermute | solution.py:360
  36.7 2.0 %collective-permute-start.5 = (bf16[2,4,4,16,128]{4,3,2,1,0:T(8,128)(2,1)}, bf16[2,4,4,16,128]{4,3,2,1,0:T(8,128)(2,1)S(1)}, u32[]{:S(2)}, u32[]{:S(2)}) collective-permute-start(bf16[2,4,4,16,128]{4,3,2,1,0:T(8,128)(2,1)} %get-tuple-element.69), channel_id=1, source_target_pairs={{0,7},{1,6},{2,5},{3,4},{4,3},{5,2},{6,1},{7,0},{8,15},{9,14},{10,... | collective-permute-start | bytes 393224 | tf_op jit(solution)/shard_map/ppermute | solution.py:360
  38.7 1.5 %collective-permute-start.2 = (bf16[2,4,4,16,128]{4,3,2,1,0:T(8,128)(2,1)}, bf16[2,4,4,16,128]{4,3,2,1,0:T(8,128)(2,1)S(1)}, u32[]{:S(2)}, u32[]{:S(2)}) collective-permute-start(bf16[2,4,4,16,128]{4,3,2,1,0:T(8,128)(2,1)} %get-tuple-element.64), channel_id=1, source_target_pairs={{0,10},{1,11},{2,8},{3,9},{4,14},{5,15},{6,12},{7,13},{8,2},{9,3},... | collective-permute-start | bytes 393224 | tf_op jit(solution)/shard_map/ppermute | solution.py:360
  40.5 2.9 %collective-permute-done.14.refs_11_ = bf16[2,4,4,16,128]{4,3,2,1,0:T(8,128)(2,1)S(1)} collective-permute-done((bf16[2,4,4,16,128]{4,3,2,1,0:T(8,128)(2,1)}, bf16[2,4,4,16,128]{4,3,2,1,0:T(8,128)(2,1)S(1)}, u32[]{:S(2)}, u32[]{:S(2)}) %collective-permute-start.14) | collective-permute-done | bytes 131104 | tf_op jit(solution)/shard_map/ppermute | solution.py:360
  44.3 5.6 %cross.1 = (bf16[16,2,128,128]{3,2,1,0:T(8,128)(2,1)S(1)}, f32[16,2,4,4,16,128]{5,4,3,2,1,0:T(8,128)S(1)}, bf16[4,2,2048,256]{3,2,1,0:T(8,128)(2,1)S(1)}) custom-call(s32[4,8,2]{2,1,0:T(8,128)S(1)} %copy.10.pairs_ref, f32[1024]{0:T(1024)S(1)} %reshape.6.inverse_ref, bf16[2,4,4,16,128]{4,3,2,1,0:T(8,128)(2,1)S(1)} %collective-permute-done.9.refs_0_, ...), custom_call_target="tpu_custom_call" | custom-call | flops 54525952 | bytes 4194304 | tf_op jit(solution)/shard_map/cross/pallas_call | solution.py:263
  49.9 4.2 %collective-permute-done.2.refs_0_ = bf16[2,4,4,16,128]{4,3,2,1,0:T(8,128)(2,1)S(1)} collective-permute-done((bf16[2,4,4,16,128]{4,3,2,1,0:T(8,128)(2,1)}, bf16[2,4,4,16,128]{4,3,2,1,0:T(8,128)(2,1)S(1)}, u32[]{:S(2)}, u32[]{:S(2)}) %collective-permute-start.2) | collective-permute-done | bytes 131104 | tf_op jit(solution)/shard_map/ppermute | solution.py:360
  54.1 3.8 %cross_rest.1 = (bf16[16,2,128,128]{3,2,1,0:T(8,128)(2,1)S(1)}, f32[16,2,4,4,16,128]{5,4,3,2,1,0:T(8,128)S(1)}, bf16[2,128,128]{2,1,0:T(8,128)(2,1)S(1)}, bf16[2...) custom-call(s32[4,8,2]{2,1,0:T(8,128)S(1)} %copy.10.pairs_ref, ...), custom_call_target="tpu_custom_call", output_to_operand_aliasing={{0}: (5, {}), {1}: (6, {})} | custom-call | flops 12582912 | bytes 4194304 | tf_op jit(solution)/shard_map/cross_rest/pallas_call | solution.py:263
  58.8 2.4 %collective-permute-start.16 = (bf16[2,128,128]{2,1,0:T(8,128)(2,1)S(1)}, bf16[2,128,128]{2,1,0:T(8,128)(2,1)S(1)}, u32[]{:S(2)}, u32[]{:S(2)}) collective-permute-start(bf16[2,128,128]{2,1,0:T(8,128)(2,1)S(1)} %get-tuple-element.90), channel_id=1, source_target_pairs={{0,1},{1,0},{2,3},{3,2},{4,5},{5,4},{6,7},{7,6},{8,9},{9,8},{10,11... | collective-permute-start | bytes 196616 | tf_op jit(solution)/shard_map/ppermute | solution.py:360
  61.9 3.6 %collective-permute-start.19 = (bf16[2,128,128]{2,1,0:T(8,128)(2,1)S(1)}, bf16[2,128,128]{2,1,0:T(8,128)(2,1)S(1)}, u32[]{:S(2)}, u32[]{:S(2)}) collective-permute-start(bf16[2,128,128]{2,1,0:T(8,128)(2,1)S(1)} %get-tuple-element.93), channel_id=1, source_target_pairs={{0,14},{1,15},{2,12},{3,13},{4,10},{5,11},{6,8},{7,9},{8,6},{9,7},... | collective-permute-start | bytes 196616 | tf_op jit(solution)/shard_map/ppermute | solution.py:360
  67.6 2.9 %collective-permute-start.23 = (bf16[2,128,128]{2,1,0:T(8,128)(2,1)S(1)}, bf16[2,128,128]{2,1,0:T(8,128)(2,1)S(1)}, u32[]{:S(2)}, u32[]{:S(2)}) collective-permute-start(bf16[2,128,128]{2,1,0:T(8,128)(2,1)S(1)} %get-tuple-element.101), channel_id=1, source_target_pairs={{0,8},{1,9},{2,10},{3,11},{4,12},{5,13},{6,14},{7,15},{8,0},{9,1},... | collective-permute-start | bytes 196616 | tf_op jit(solution)/shard_map/ppermute | solution.py:360
  71.9 1.9 %collective-permute-done.21.refs_7_ = bf16[2,128,128]{2,1,0:T(8,128)(2,1)S(1)} collective-permute-done((bf16[2,128,128]{2,1,0:T(8,128)(2,1)S(1)}, bf16[2,128,128]{2,1,0:T(8,128)(2,1)S(1)}, u32[]{:S(2)}, u32[]{:S(2)}) %collective-permute-start.21) | collective-permute-done | bytes 65568 | tf_op jit(solution)/shard_map/ppermute | solution.py:360
  73.8 1.9 %collective-permute-start.27 = (bf16[2,128,128]{2,1,0:T(8,128)(2,1)S(1)}, bf16[2,128,128]{2,1,0:T(8,128)(2,1)S(1)}, u32[]{:S(2)}, u32[]{:S(2)}) collective-permute-start(bf16[2,128,128]{2,1,0:T(8,128)(2,1)S(1)} %get-tuple-element.109), channel_id=1, source_target_pairs={{0,10},{1,11},{2,8},{3,9},{4,14},{5,15},{6,12},{7,13},{8,2},{9,3},... | collective-permute-start | bytes 196616 | tf_op jit(solution)/shard_map/ppermute | solution.py:360
  75.8 2.6 %collective-permute-start.28 = (bf16[2,128,128]{2,1,0:T(8,128)(2,1)S(1)}, bf16[2,128,128]{2,1,0:T(8,128)(2,1)S(1)}, u32[]{:S(2)}, u32[]{:S(2)}) collective-permute-start(bf16[2,128,128]{2,1,0:T(8,128)(2,1)S(1)} %get-tuple-element.111), channel_id=1, source_target_pairs={{0,7},{1,6},{2,5},{3,4},{4,3},{5,2},{6,1},{7,0},{8,15},{9,14},{10,... | collective-permute-start | bytes 196616 | tf_op jit(solution)/shard_map/ppermute | solution.py:360
  78.4 1.4 %collective-permute-start.29 = (bf16[2,128,128]{2,1,0:T(8,128)(2,1)S(1)}, bf16[2,128,128]{2,1,0:T(8,128)(2,1)S(1)}, u32[]{:S(2)}, u32[]{:S(2)}) collective-permute-start(bf16[2,128,128]{2,1,0:T(8,128)(2,1)S(1)} %get-tuple-element.113), channel_id=1, source_target_pairs={{0,11},{1,10},{2,9},{3,8},{4,15},{5,14},{6,13},{7,12},{8,3},{9,2},... | collective-permute-start | bytes 196616 | tf_op jit(solution)/shard_map/ppermute | solution.py:360
  80.8 1.3 %collective-permute-done.28.refs_14_ = bf16[2,128,128]{2,1,0:T(8,128)(2,1)S(1)} collective-permute-done((bf16[2,128,128]{2,1,0:T(8,128)(2,1)S(1)}, bf16[2,128,128]{2,1,0:T(8,128)(2,1)S(1)}, u32[]{:S(2)}, u32[]{:S(2)}) %collective-permute-start.28) | collective-permute-done | bytes 65568 | tf_op jit(solution)/shard_map/ppermute | solution.py:360
  82.2 3.0 %collective-permute-done.29.refs_15_ = bf16[2,128,128]{2,1,0:T(8,128)(2,1)S(1)} collective-permute-done((bf16[2,128,128]{2,1,0:T(8,128)(2,1)S(1)}, bf16[2,128,128]{2,1,0:T(8,128)(2,1)S(1)}, u32[]{:S(2)}, u32[]{:S(2)}) %collective-permute-start.29) | collective-permute-done | bytes 65568 | tf_op jit(solution)/shard_map/ppermute | solution.py:360
  85.2 2.9 %lags.1 = f32[128,2048]{1,0:T(8,128)} custom-call(bf16[2,128,128]{2,1,0:T(8,128)(2,1)S(1)} %get-tuple-element.88.refs_0_, bf16[2,128,128]{2,1,0:T(8,128)(2,1)S(1)} %collective-permute-done.15.refs_1_, bf16[2,128,128]{2,1,0:T(8,128)(2,1)S(1)} %collective-permute-done.16.refs_2_, bf16[2,128,128]{2,1,0:T(8,128)(2,1)S(1)} %collective-permute-done.17.refs_3_, ...), custom_call_target="tpu_custom_call" | custom-call | tf_op jit(solution)/shard_map/lags/pallas_call | solution.py:338
  (50 shorter events, 12.2 us)
Async XLA Ops:
  3.0 13.6 %collective-permute-start.10 = (bf16[2,4,4,16,128]{4,3,2,1,0:T(8,128)(2,1)}, bf16[2,4,4,16,128]{4,3,2,1,0:T(8,128)(2,1)S(1)}, u32[]{:S(2)}, u32[]{:S(2)}) collective-permute-start(bf16[2,4,4,16,128]{4,3,2,1,0:T(8,128)(2,1)} %get-tuple-element.76), channel_id=1, source_target_pairs={{0,1},{1,0},{2,3},{3,2},{4,5},{5,4},{6,7},{7,6},{8,9},{9,8},{10,11... | collective-permute-start | bytes 393224 | tf_op jit(solution)/shard_map/ppermute | solution.py:360
  3.1 14.6 %collective-permute-start.9 = (bf16[2,4,4,16,128]{4,3,2,1,0:T(8,128)(2,1)}, bf16[2,4,4,16,128]{4,3,2,1,0:T(8,128)(2,1)S(1)}, u32[]{:S(2)}, u32[]{:S(2)}) collective-permute-start(bf16[2,4,4,16,128]{4,3,2,1,0:T(8,128)(2,1)} %get-tuple-element.75), channel_id=1, source_target_pairs={{0,12},{1,13},{2,14},{3,15},{4,8},{5,9},{6,10},{7,11},{8,4},{9,5},... | collective-permute-start | bytes 393224 | tf_op jit(solution)/shard_map/ppermute | solution.py:360
  7.9 10.1 %collective-permute-start.6 = (bf16[2,4,4,16,128]{4,3,2,1,0:T(8,128)(2,1)}, bf16[2,4,4,16,128]{4,3,2,1,0:T(8,128)(2,1)S(1)}, u32[]{:S(2)}, u32[]{:S(2)}) collective-permute-start(bf16[2,4,4,16,128]{4,3,2,1,0:T(8,128)(2,1)} %get-tuple-element.72), channel_id=1, source_target_pairs={{0,14},{1,15},{2,12},{3,13},{4,10},{5,11},{6,8},{7,9},{8,6},{9,7},... | collective-permute-start | bytes 393224 | tf_op jit(solution)/shard_map/ppermute | solution.py:360
  8.8 18.5 %collective-permute-start.3 = (bf16[2,4,4,16,128]{4,3,2,1,0:T(8,128)(2,1)}, bf16[2,4,4,16,128]{4,3,2,1,0:T(8,128)(2,1)S(1)}, u32[]{:S(2)}, u32[]{:S(2)}) collective-permute-start(bf16[2,4,4,16,128]{4,3,2,1,0:T(8,128)(2,1)} %get-tuple-element.67), channel_id=1, source_target_pairs={{0,2},{1,3},{2,0},{3,1},{4,6},{5,7},{6,4},{7,5},{8,10},{9,11},{10,... | collective-permute-start | bytes 393224 | tf_op jit(solution)/shard_map/ppermute | solution.py:360
  9.1 18.2 %collective-permute-start = (bf16[2,4,4,16,128]{4,3,2,1,0:T(8,128)(2,1)}, bf16[2,4,4,16,128]{4,3,2,1,0:T(8,128)(2,1)S(1)}, u32[]{:S(2)}, u32[]{:S(2)}) collective-permute-start(bf16[2,4,4,16,128]{4,3,2,1,0:T(8,128)(2,1)} %get-tuple-element.62), channel_id=1, source_target_pairs={{0,13},{1,12},{2,15},{3,14},{4,9},{5,8},{6,11},{7,10},{8,5},{9,4},... | collective-permute-start | bytes 393224 | tf_op jit(solution)/shard_map/ppermute | solution.py:360
  16.6 13.3 %collective-permute-start.12 = (bf16[2,4,4,16,128]{4,3,2,1,0:T(8,128)(2,1)}, bf16[2,4,4,16,128]{4,3,2,1,0:T(8,128)(2,1)S(1)}, u32[]{:S(2)}, u32[]{:S(2)}) collective-permute-start(bf16[2,4,4,16,128]{4,3,2,1,0:T(8,128)(2,1)} %get-tuple-element.80), channel_id=1, source_target_pairs={{0,15},{1,14},{2,13},{3,12},{4,11},{5,10},{6,9},{7,8},{8,7},{9,6},... | collective-permute-start | bytes 393224 | tf_op jit(solution)/shard_map/ppermute | solution.py:360
  17.6 14.2 %collective-permute-start.11 = (bf16[2,4,4,16,128]{4,3,2,1,0:T(8,128)(2,1)}, bf16[2,4,4,16,128]{4,3,2,1,0:T(8,128)(2,1)S(1)}, u32[]{:S(2)}, u32[]{:S(2)}) collective-permute-start(bf16[2,4,4,16,128]{4,3,2,1,0:T(8,128)(2,1)} %get-tuple-element.78), channel_id=1, source_target_pairs={{0,3},{1,2},{2,1},{3,0},{4,7},{5,6},{6,5},{7,4},{8,11},{9,10},{10,... | collective-permute-start | bytes 393224 | tf_op jit(solution)/shard_map/ppermute | solution.py:360
  18.0 15.1 %collective-permute-start.7 = (bf16[2,4,4,16,128]{4,3,2,1,0:T(8,128)(2,1)}, bf16[2,4,4,16,128]{4,3,2,1,0:T(8,128)(2,1)S(1)}, u32[]{:S(2)}, u32[]{:S(2)}) collective-permute-start(bf16[2,4,4,16,128]{4,3,2,1,0:T(8,128)(2,1)} %get-tuple-element.73), channel_id=1, source_target_pairs={{0,5},{1,4},{2,7},{3,6},{4,1},{5,0},{6,3},{7,2},{8,13},{9,12},{10,... | collective-permute-start | bytes 393224 | tf_op jit(solution)/shard_map/ppermute | solution.py:360
  27.3 9.3 %collective-permute-start.4 = (bf16[2,4,4,16,128]{4,3,2,1,0:T(8,128)(2,1)}, bf16[2,4,4,16,128]{4,3,2,1,0:T(8,128)(2,1)S(1)}, u32[]{:S(2)}, u32[]{:S(2)}) collective-permute-start(bf16[2,4,4,16,128]{4,3,2,1,0:T(8,128)(2,1)} %get-tuple-element.68), channel_id=1, source_target_pairs={{0,8},{1,9},{2,10},{3,11},{4,12},{5,13},{6,14},{7,15},{8,0},{9,1},... | collective-permute-start | bytes 393224 | tf_op jit(solution)/shard_map/ppermute | solution.py:360
  27.3 11.4 %collective-permute-start.1 = (bf16[2,4,4,16,128]{4,3,2,1,0:T(8,128)(2,1)}, bf16[2,4,4,16,128]{4,3,2,1,0:T(8,128)(2,1)S(1)}, u32[]{:S(2)}, u32[]{:S(2)}) collective-permute-start(bf16[2,4,4,16,128]{4,3,2,1,0:T(8,128)(2,1)} %get-tuple-element.63), channel_id=1, source_target_pairs={{0,4},{1,5},{2,6},{3,7},{4,0},{5,1},{6,2},{7,3},{8,12},{9,13},{10,... | collective-permute-start | bytes 393224 | tf_op jit(solution)/shard_map/ppermute | solution.py:360
  29.9 13.5 %collective-permute-start.14 = (bf16[2,4,4,16,128]{4,3,2,1,0:T(8,128)(2,1)}, bf16[2,4,4,16,128]{4,3,2,1,0:T(8,128)(2,1)S(1)}, u32[]{:S(2)}, u32[]{:S(2)}) collective-permute-start(bf16[2,4,4,16,128]{4,3,2,1,0:T(8,128)(2,1)} %get-tuple-element.84), channel_id=1, source_target_pairs={{0,6},{1,7},{2,4},{3,5},{4,2},{5,3},{6,0},{7,1},{8,14},{9,15},{10,... | collective-permute-start | bytes 393224 | tf_op jit(solution)/shard_map/ppermute | solution.py:360
  31.8 11.6 %collective-permute-start.13 = (bf16[2,4,4,16,128]{4,3,2,1,0:T(8,128)(2,1)}, bf16[2,4,4,16,128]{4,3,2,1,0:T(8,128)(2,1)S(1)}, u32[]{:S(2)}, u32[]{:S(2)}) collective-permute-start(bf16[2,4,4,16,128]{4,3,2,1,0:T(8,128)(2,1)} %get-tuple-element.82), channel_id=1, source_target_pairs={{0,9},{1,8},{2,11},{3,10},{4,13},{5,12},{6,15},{7,14},{8,1},{9,0},... | collective-permute-start | bytes 393224 | tf_op jit(solution)/shard_map/ppermute | solution.py:360
  33.1 16.8 %collective-permute-start.8 = (bf16[2,4,4,16,128]{4,3,2,1,0:T(8,128)(2,1)}, bf16[2,4,4,16,128]{4,3,2,1,0:T(8,128)(2,1)S(1)}, u32[]{:S(2)}, u32[]{:S(2)}) collective-permute-start(bf16[2,4,4,16,128]{4,3,2,1,0:T(8,128)(2,1)} %get-tuple-element.74), channel_id=1, source_target_pairs={{0,11},{1,10},{2,9},{3,8},{4,15},{5,14},{6,13},{7,12},{8,3},{9,2},... | collective-permute-start | bytes 393224 | tf_op jit(solution)/shard_map/ppermute | solution.py:360
  36.7 13.3 %collective-permute-start.5 = (bf16[2,4,4,16,128]{4,3,2,1,0:T(8,128)(2,1)}, bf16[2,4,4,16,128]{4,3,2,1,0:T(8,128)(2,1)S(1)}, u32[]{:S(2)}, u32[]{:S(2)}) collective-permute-start(bf16[2,4,4,16,128]{4,3,2,1,0:T(8,128)(2,1)} %get-tuple-element.69), channel_id=1, source_target_pairs={{0,7},{1,6},{2,5},{3,4},{4,3},{5,2},{6,1},{7,0},{8,15},{9,14},{10,... | collective-permute-start | bytes 393224 | tf_op jit(solution)/shard_map/ppermute | solution.py:360
  38.7 15.5 %collective-permute-start.2 = (bf16[2,4,4,16,128]{4,3,2,1,0:T(8,128)(2,1)}, bf16[2,4,4,16,128]{4,3,2,1,0:T(8,128)(2,1)S(1)}, u32[]{:S(2)}, u32[]{:S(2)}) collective-permute-start(bf16[2,4,4,16,128]{4,3,2,1,0:T(8,128)(2,1)} %get-tuple-element.64), channel_id=1, source_target_pairs={{0,10},{1,11},{2,8},{3,9},{4,14},{5,15},{6,12},{7,13},{8,2},{9,3},... | collective-permute-start | bytes 393224 | tf_op jit(solution)/shard_map/ppermute | solution.py:360
  57.9 7.6 %collective-permute-start.15 = (bf16[2,128,128]{2,1,0:T(8,128)(2,1)S(1)}, bf16[2,128,128]{2,1,0:T(8,128)(2,1)S(1)}, u32[]{:S(2)}, u32[]{:S(2)}) collective-permute-start(bf16[2,128,128]{2,1,0:T(8,128)(2,1)S(1)} %get-tuple-element.89), channel_id=1, source_target_pairs={{0,12},{1,13},{2,14},{3,15},{4,8},{5,9},{6,10},{7,11},{8,4},{9,5},... | collective-permute-start | bytes 196616 | tf_op jit(solution)/shard_map/ppermute | solution.py:360
  58.8 7.9 %collective-permute-start.16 = (bf16[2,128,128]{2,1,0:T(8,128)(2,1)S(1)}, bf16[2,128,128]{2,1,0:T(8,128)(2,1)S(1)}, u32[]{:S(2)}, u32[]{:S(2)}) collective-permute-start(bf16[2,128,128]{2,1,0:T(8,128)(2,1)S(1)} %get-tuple-element.90), channel_id=1, source_target_pairs={{0,1},{1,0},{2,3},{3,2},{4,5},{5,4},{6,7},{7,6},{8,9},{9,8},{10,11... | collective-permute-start | bytes 196616 | tf_op jit(solution)/shard_map/ppermute | solution.py:360
  61.9 8.6 %collective-permute-start.19 = (bf16[2,128,128]{2,1,0:T(8,128)(2,1)S(1)}, bf16[2,128,128]{2,1,0:T(8,128)(2,1)S(1)}, u32[]{:S(2)}, u32[]{:S(2)}) collective-permute-start(bf16[2,128,128]{2,1,0:T(8,128)(2,1)S(1)} %get-tuple-element.93), channel_id=1, source_target_pairs={{0,14},{1,15},{2,12},{3,13},{4,10},{5,11},{6,8},{7,9},{8,6},{9,7},... | collective-permute-start | bytes 196616 | tf_op jit(solution)/shard_map/ppermute | solution.py:360
  66.7 7.1 %collective-permute-start.21 = (bf16[2,128,128]{2,1,0:T(8,128)(2,1)S(1)}, bf16[2,128,128]{2,1,0:T(8,128)(2,1)S(1)}, u32[]{:S(2)}, u32[]{:S(2)}) collective-permute-start(bf16[2,128,128]{2,1,0:T(8,128)(2,1)S(1)} %get-tuple-element.97), channel_id=1, source_target_pairs={{0,15},{1,14},{2,13},{3,12},{4,11},{5,10},{6,9},{7,8},{8,7},{9,6},... | collective-permute-start | bytes 196616 | tf_op jit(solution)/shard_map/ppermute | solution.py:360
  67.6 8.2 %collective-permute-start.23 = (bf16[2,128,128]{2,1,0:T(8,128)(2,1)S(1)}, bf16[2,128,128]{2,1,0:T(8,128)(2,1)S(1)}, u32[]{:S(2)}, u32[]{:S(2)}) collective-permute-start(bf16[2,128,128]{2,1,0:T(8,128)(2,1)S(1)} %get-tuple-element.101), channel_id=1, source_target_pairs={{0,8},{1,9},{2,10},{3,11},{4,12},{5,13},{6,14},{7,15},{8,0},{9,1},... | collective-permute-start | bytes 196616 | tf_op jit(solution)/shard_map/ppermute | solution.py:360
  70.5 7.9 %collective-permute-start.24 = (bf16[2,128,128]{2,1,0:T(8,128)(2,1)S(1)}, bf16[2,128,128]{2,1,0:T(8,128)(2,1)S(1)}, u32[]{:S(2)}, u32[]{:S(2)}) collective-permute-start(bf16[2,128,128]{2,1,0:T(8,128)(2,1)S(1)} %get-tuple-element.103), channel_id=1, source_target_pairs={{0,5},{1,4},{2,7},{3,6},{4,1},{5,0},{6,3},{7,2},{8,13},{9,12},{10,... | collective-permute-start | bytes 196616 | tf_op jit(solution)/shard_map/ppermute | solution.py:360
  71.8 7.9 %collective-permute-start.25 = (bf16[2,128,128]{2,1,0:T(8,128)(2,1)S(1)}, bf16[2,128,128]{2,1,0:T(8,128)(2,1)S(1)}, u32[]{:S(2)}, u32[]{:S(2)}) collective-permute-start(bf16[2,128,128]{2,1,0:T(8,128)(2,1)S(1)} %get-tuple-element.105), channel_id=1, source_target_pairs={{0,9},{1,8},{2,11},{3,10},{4,13},{5,12},{6,15},{7,14},{8,1},{9,0},... | collective-permute-start | bytes 196616 | tf_op jit(solution)/shard_map/ppermute | solution.py:360
  73.8 7.0 %collective-permute-start.26 = (bf16[2,128,128]{2,1,0:T(8,128)(2,1)S(1)}, bf16[2,128,128]{2,1,0:T(8,128)(2,1)S(1)}, u32[]{:S(2)}, u32[]{:S(2)}) collective-permute-start(bf16[2,128,128]{2,1,0:T(8,128)(2,1)S(1)} %get-tuple-element.107), channel_id=1, source_target_pairs={{0,6},{1,7},{2,4},{3,5},{4,2},{5,3},{6,0},{7,1},{8,14},{9,15},{10,... | collective-permute-start | bytes 196616 | tf_op jit(solution)/shard_map/ppermute | solution.py:360
  73.8 7.0 %collective-permute-start.27 = (bf16[2,128,128]{2,1,0:T(8,128)(2,1)S(1)}, bf16[2,128,128]{2,1,0:T(8,128)(2,1)S(1)}, u32[]{:S(2)}, u32[]{:S(2)}) collective-permute-start(bf16[2,128,128]{2,1,0:T(8,128)(2,1)S(1)} %get-tuple-element.109), channel_id=1, source_target_pairs={{0,10},{1,11},{2,8},{3,9},{4,14},{5,15},{6,12},{7,13},{8,2},{9,3},... | collective-permute-start | bytes 196616 | tf_op jit(solution)/shard_map/ppermute | solution.py:360
  (9 other events, 109.0 us)

commit v6 on v5

--- a/solution.py
+++ b/solution.py
@@ -13,7 +13,7 @@
 LAGS = 2048
 MIB = 1 << 20
 ORDER = (12, 1, 13, 2, 14, 3, 15, 4, 8, 5, 9, 6, 10, 7, 11)
-FIRST = 5
+FIRST = 3
 LATE = 3
 
 
@@ -282,35 +282,29 @@
     )(pair_table, inverse, *blocks, *started, *tables)
 
 
-def lag_kernel(scale, sources, *refs):
-    stacked_refs, refs = refs[: len(sources)], refs[len(sources) :]
-    table_ref, out_ref, left_ref, lagged_ref, out_sems = refs
-    tiles, _, depth, tile = table_ref.shape
-    parts, rows, _ = left_ref.shape
-    half = tiles * tile
-    for stacked_ref, source in zip(stacked_refs, sources):
-        bins = stacked_ref.shape[-1]
-        if source is None:
-            for src in range(stacked_ref.shape[0]):
-                for c in range(parts):
-                    left_ref[c, :, src * bins : (src + 1) * bins] = stacked_ref[src, c]
-        else:
-            at = pl.multiple_of((lax.axis_index("sta") ^ source) * bins, 128)
-            for c in range(parts):
-                left_ref[c, :, pl.ds(at, bins)] = stacked_ref[c]
-
+def quarter_turns(depth):
     turn = lax.broadcasted_iota(jnp.int32, (depth, 128), 0) % 4
-    cosine = jnp.where(turn == 0, 1.0, jnp.where(turn == 2, -1.0, 0.0)).astype(jnp.bfloat16)
-    sine = jnp.where(turn == 1, 1.0, jnp.where(turn == 3, -1.0, 0.0)).astype(jnp.bfloat16)
-    before = jnp.dot(left_ref[0], cosine, preferred_element_type=jnp.float32)
-    before = (before + jnp.dot(left_ref[1], sine, preferred_element_type=jnp.float32)) * scale
-
+    cosine = jnp.where(turn == 0, 1.0, jnp.where(turn == 2, -1.0, 0.0))
+    sine = jnp.where(turn == 1, 1.0, jnp.where(turn == 3, -1.0, 0.0))
+    return cosine.astype(jnp.bfloat16), sine.astype(jnp.bfloat16)
+
+
+def product(left, right):
+    return jnp.dot(left, right, preferred_element_type=jnp.float32)
+
+
+def write_lags(scale, sums, before, out_ref, lagged_ref, out_sems):
+    rows, lag_count = lagged_ref.shape
+    tiles = out_sems.shape[0] // 2
+    half = lag_count // 2
+    tile = half // tiles
     lane = lax.broadcasted_iota(jnp.int32, (rows, 128), 1)
     flip = (128 - lane) % 128
+    before = before * scale
     stores = []
     for t in reversed(range(tiles)):
-        even = jnp.dot(left_ref[0], table_ref[t, 0], preferred_element_type=jnp.float32) * scale
-        odd = jnp.dot(left_ref[1], table_ref[t, 1], preferred_element_type=jnp.float32) * scale
+        even, odd = sums(t)
+        even, odd = even * scale, odd * scale
         lagged_ref[:, half + t * tile : half + (t + 1) * tile] = even + odd
         gap = even - odd
         for sub in reversed(range(tile // 128)):
@@ -331,23 +325,100 @@
         store.wait()
 
 
-def lags(stacked, sources, table, scale):
+def place(source, bins):
+    return pl.ds(pl.multiple_of((lax.axis_index("sta") ^ source) * bins, 128), bins)
+
+
+def lag_kernel(scale, sources, late, *refs):
+    stacked_refs, table_ref, refs = refs[: len(sources)], refs[len(sources)], refs[len(sources) + 1 :]
+    tiles, parts, depth, tile = table_ref.shape
+    left_ref = refs[2]
+    rows = left_ref.shape[1]
+    for stacked_ref, source in zip(stacked_refs, sources):
+        bins = stacked_ref.shape[-1]
+        for c in range(parts):
+            if source is None:
+                for src in range(stacked_ref.shape[0]):
+                    left_ref[c, :, src * bins : (src + 1) * bins] = stacked_ref[src, c]
+            else:
+                left_ref[c, :, place(source, bins)] = stacked_ref[c]
+    for source in late:
+        for c in range(parts):
+            left_ref[c, :, place(source, bins)] = jnp.zeros((rows, bins), jnp.bfloat16)
+
+    cosine, sine = quarter_turns(depth)
+    before = product(left_ref[0], cosine) + product(left_ref[1], sine)
+
+    def sums(t):
+        return product(left_ref[0], table_ref[t, 0]), product(left_ref[1], table_ref[t, 1])
+
+    if late:
+        sums_ref, before_ref, _ = refs
+        before_ref[...] = before
+        for t in range(tiles):
+            sums_ref[t, 0], sums_ref[t, 1] = sums(t)
+    else:
+        out_ref, lagged_ref, _, out_sems = refs
+        write_lags(scale, sums, before, out_ref, lagged_ref, out_sems)
+
+
+def rest_kernel(scale, sources, *refs):
+    stacked_refs, refs = refs[: len(sources)], refs[len(sources) :]
+    table_ref, sums_ref, before_ref, out_ref, lagged_ref, out_sems = refs
+    bins = stacked_refs[0].shape[-1]
+    cosine, sine = quarter_turns(bins)
+    before = before_ref[...]
+    for ref in stacked_refs:
+        before = before + (product(ref[0], cosine) + product(ref[1], sine))
+
+    def sums(t):
+        totals = []
+        for c in range(2):
+            total = sums_ref[t, c]
+            for ref, source in zip(stacked_refs, sources):
+                total = total + product(ref[c], table_ref[t, c, place(source, bins), :])
+            totals.append(total)
+        return totals
+
+    write_lags(scale, sums, before, out_ref, lagged_ref, out_sems)
+
+
+def lags(stacked, sources, table, scale, late=(), started=()):
     parts, rows, _ = stacked[0].shape[-3:]
     tiles, _, depth, tile = table.shape
     lag_count = 2 * tiles * tile
+    vmem = pl.BlockSpec(memory_space=pltpu.VMEM)
+    left = pltpu.VMEM((parts, rows, depth), jnp.bfloat16)
+    if late:
+        body = functools.partial(lag_kernel, scale, sources, late)
+        out_specs = [vmem] * 2
+        out_shape = [
+            jax.ShapeDtypeStruct((tiles, parts, rows, tile), jnp.float32),
+            jax.ShapeDtypeStruct((rows, 128), jnp.float32),
+        ]
+        scratch = [left]
+    else:
+        out_specs = pl.BlockSpec(memory_space=pl.ANY)
+        out_shape = jax.ShapeDtypeStruct((rows, lag_count), jnp.float32)
+        scratch = [pltpu.VMEM((rows, lag_count), jnp.float32)]
+        if started:
+            body = functools.partial(rest_kernel, scale, sources)
+        else:
+            body = functools.partial(lag_kernel, scale, sources, late)
+            scratch.append(left)
+        scratch.append(pltpu.SemaphoreType.DMA((2 * tiles,)))
     return pl.pallas_call(
-        functools.partial(lag_kernel, scale, sources),
-        in_specs=[pl.BlockSpec(memory_space=pltpu.VMEM)] * (len(stacked) + 1),
-        out_specs=pl.BlockSpec(memory_space=pl.ANY),
-        out_shape=jax.ShapeDtypeStruct((rows, lag_count), jnp.float32),
-        scratch_shapes=[
-            pltpu.VMEM((parts, rows, depth), jnp.bfloat16),
-            pltpu.VMEM((rows, lag_count), jnp.float32),
-            pltpu.SemaphoreType.DMA((2 * tiles,)),
-        ],
+        body,
+        in_specs=[vmem] * (len(stacked) + 1 + len(started)),
+        out_specs=out_specs,
+        out_shape=out_shape,
+        scratch_shapes=scratch,
         compiler_params=pltpu.CompilerParams(vmem_limit_bytes=20 * MIB),
-        name="lags",
-    )(*stacked, table)
+        cost_estimate=pl.CostEstimate(
+            flops=2 * rows * depth * lag_count, bytes_accessed=4 << 20, transcendentals=0
+        ),
+        name="lags_first" if late else "lags",
+    )(*stacked, table, *started)
 
 
 def swap(shares, sources, devices):
@@ -400,7 +471,13 @@
     else:
         stacked, _ = cross(blocks, sources, inverse, pair_table, devices)
         received = [lax.all_to_all(stacked, "sta", split_axis=0, concat_axis=0, tiled=True)]
-    lagged = lags(received, sources, table, 1.0 / math.sqrt(total))
+    scale = 1.0 / math.sqrt(total)
+    if len(sources) > 1:
+        kept = len(sources) - LATE
+        started = lags(received[:kept], sources[:kept], table, scale, sources[kept:])
+        lagged = lags(received[kept:], sources[kept:], table, scale, (), tuple(started))
+    else:
+        lagged = lags(received, sources, table, scale)
     return lagged.reshape(rounds, held, slots * slots, LAGS)
 
 

time: 88.4 us -> 86.4 us (0.977)
  starting transfers between devices: 52.7 us -> 50.9 us
  waiting for transfers between devices: 15.3 us -> 14.4 us
    ppermute x30, starting transfers between devices: 52.7 us -> 50.9 us  [swap(): share = lax.ppermute(share, 'sta', [(n, n ^ away) for n in range(devices)])]
    ppermute x30, waiting for transfers between devices: 15.3 us -> 14.4 us  [swap(): share = lax.ppermute(share, 'sta', [(n, n ^ away) for n in range(devices)])]
    pallas_call x1 -> x2, Pallas kernels: 2.91 us -> 3.65 us  [lags(): pl.pallas_call(body, in_specs=[vmem] * (len(stacked) + 1 + len(started)),...]
  transfers between devices with their start and end apart: 30 -> 30, of which waited for: 7 -> 6; matrix products, arithmetic and copies ran while one was open for 0% -> 0% of each run, Pallas kernels for 10% -> 13%
where the time goes in v6:
time: 86.4 us; the launch traced here: 86.1 us
  starting transfers between devices  50.9 us (59%)
  Pallas kernels  19.4 us (22%)
  waiting for transfers between devices  14.4 us (17%)
  local copies, waits for them, and re-layouts  1.09 us (1%)
    ppermute x30, starting transfers between devices, swap(): share = lax.ppermute(share, 'sta', [(n, n ^ away) for n in range(devices)])  50.9 us
    ppermute x30, waiting for transfers between devices, swap(): share = lax.ppermute(share, 'sta', [(n, n ^ away) for n in range(devices)])  14.4 us
    pallas_call x2, Pallas kernels, cross(): pl.pallas_call(functools.partial(cross_kernel, sources, late, len(started...  9.38 us
    pallas_call x2, Pallas kernels, pieces(): pl.pallas_call(functools.partial(piece_kernel, aways), in_specs=[pl.Block...  6.39 us
    pallas_call x2, Pallas kernels, lags(): pl.pallas_call(body, in_specs=[vmem] * (len(stacked) + 1 + len(started)),...  3.65 us
  transfers between devices with their start and end apart: 30, of which 6 were waited for; matrix products, arithmetic and copies ran while one was open for 0% of the time, Pallas kernels for 13%

profile of v6, /device:TPU:1, one launch (start us, length us, event | category | flops | bytes accessed | tf_op | source)
XLA Modules:
  0.0 86.1 jit_solution(3117849972137361418)
XLA Ops:
  0.0 2.7 %pack_first.1 = (bf16[2,4,4,16,128]{4,3,2,1,0:T(8,128)(2,1)}, bf16[2,4,4,16,128]{4,3,2,1,0:T(8,128)(2,1)}, bf16[2,4,4,16,128]{4,3,2,1,0:T(8,128)(2,1)}) custom-call(s32[16]{0:T(128)} %counts_ref.3, s32[4,16,16]{2,1,0:T(8,128)} %masks_ref.3, bf16[2,4,16,4,2048]{4,3,2,1,0:T(4,128)(2,1)} %spectra_ref.3), custom_call_target="tpu_custom_call" | custom-call | tf_op jit(solution)/shard_map/pack_first/pallas_call | solution.py:115
  2.8 4.8 %collective-permute-start.9 = (bf16[2,4,4,16,128]{4,3,2,1,0:T(8,128)(2,1)}, bf16[2,4,4,16,128]{4,3,2,1,0:T(8,128)(2,1)S(1)}, u32[]{:S(2)}, u32[]{:S(2)}) collective-permute-start(bf16[2,4,4,16,128]{4,3,2,1,0:T(8,128)(2,1)} %get-tuple-element.77), channel_id=1, source_target_pairs={{0,12},{1,13},{2,14},{3,15},{4,8},{5,9},{6,10},{7,11},{8,4},{9,5},... | collective-permute-start | bytes 393224 | tf_op jit(solution)/shard_map/ppermute | solution.py:431
  7.6 3.7 %pack_rest.1 = (bf16[2,4,4,16,128]{4,3,2,1,0:T(8,128)(2,1)}, bf16[2,4,4,16,128]{4,3,2,1,0:T(8,128)(2,1)}, bf16[2,4,4,16,128]{4,3,2,1,0:T(8,128)(2,1)}, bf16[2,4,...) custom-call(s32[16]{0:T(128)} %counts_ref.3, ...), custom_call_target="tpu_custom_call" | custom-call | tf_op jit(solution)/shard_map/pack_rest/pallas_call | solution.py:115
  11.4 1.4 %collective-permute-start.3 = (bf16[2,4,4,16,128]{4,3,2,1,0:T(8,128)(2,1)}, bf16[2,4,4,16,128]{4,3,2,1,0:T(8,128)(2,1)S(1)}, u32[]{:S(2)}, u32[]{:S(2)}) collective-permute-start(bf16[2,4,4,16,128]{4,3,2,1,0:T(8,128)(2,1)} %get-tuple-element.69), channel_id=1, source_target_pairs={{0,2},{1,3},{2,0},{3,1},{4,6},{5,7},{6,4},{7,5},{8,10},{9,11},{10,... | collective-permute-start | bytes 393224 | tf_op jit(solution)/shard_map/ppermute | solution.py:431
  12.8 3.3 %collective-permute-start.6 = (bf16[2,4,4,16,128]{4,3,2,1,0:T(8,128)(2,1)}, bf16[2,4,4,16,128]{4,3,2,1,0:T(8,128)(2,1)S(1)}, u32[]{:S(2)}, u32[]{:S(2)}) collective-permute-start(bf16[2,4,4,16,128]{4,3,2,1,0:T(8,128)(2,1)} %get-tuple-element.74), channel_id=1, source_target_pairs={{0,14},{1,15},{2,12},{3,13},{4,10},{5,11},{6,8},{7,9},{8,6},{9,7},... | collective-permute-start | bytes 393224 | tf_op jit(solution)/shard_map/ppermute | solution.py:431
  16.1 1.6 %collective-permute-start.12 = (bf16[2,4,4,16,128]{4,3,2,1,0:T(8,128)(2,1)}, bf16[2,4,4,16,128]{4,3,2,1,0:T(8,128)(2,1)S(1)}, u32[]{:S(2)}, u32[]{:S(2)}) collective-permute-start(bf16[2,4,4,16,128]{4,3,2,1,0:T(8,128)(2,1)} %get-tuple-element.82), channel_id=1, source_target_pairs={{0,15},{1,14},{2,13},{3,12},{4,11},{5,10},{6,9},{7,8},{8,7},{9,6},... | collective-permute-start | bytes 393224 | tf_op jit(solution)/shard_map/ppermute | solution.py:431
  18.0 7.5 %collective-permute-start.1 = (bf16[2,4,4,16,128]{4,3,2,1,0:T(8,128)(2,1)}, bf16[2,4,4,16,128]{4,3,2,1,0:T(8,128)(2,1)S(1)}, u32[]{:S(2)}, u32[]{:S(2)}) collective-permute-start(bf16[2,4,4,16,128]{4,3,2,1,0:T(8,128)(2,1)} %get-tuple-element.65), channel_id=1, source_target_pairs={{0,4},{1,5},{2,6},{3,7},{4,0},{5,1},{6,2},{7,3},{8,12},{9,13},{10,... | collective-permute-start | bytes 393224 | tf_op jit(solution)/shard_map/ppermute | solution.py:431
  26.5 3.3 %collective-permute-start.7 = (bf16[2,4,4,16,128]{4,3,2,1,0:T(8,128)(2,1)}, bf16[2,4,4,16,128]{4,3,2,1,0:T(8,128)(2,1)S(1)}, u32[]{:S(2)}, u32[]{:S(2)}) collective-permute-start(bf16[2,4,4,16,128]{4,3,2,1,0:T(8,128)(2,1)} %get-tuple-element.75), channel_id=1, source_target_pairs={{0,5},{1,4},{2,7},{3,6},{4,1},{5,0},{6,3},{7,2},{8,13},{9,12},{10,... | collective-permute-start | bytes 393224 | tf_op jit(solution)/shard_map/ppermute | solution.py:431
  30.0 2.1 %collective-permute-start.14 = (bf16[2,4,4,16,128]{4,3,2,1,0:T(8,128)(2,1)}, bf16[2,4,4,16,128]{4,3,2,1,0:T(8,128)(2,1)S(1)}, u32[]{:S(2)}, u32[]{:S(2)}) collective-permute-start(bf16[2,4,4,16,128]{4,3,2,1,0:T(8,128)(2,1)} %get-tuple-element.86), channel_id=1, source_target_pairs={{0,6},{1,7},{2,4},{3,5},{4,2},{5,3},{6,0},{7,1},{8,14},{9,15},{10,... | collective-permute-start | bytes 393224 | tf_op jit(solution)/shard_map/ppermute | solution.py:431
  32.8 3.5 %collective-permute-start.2 = (bf16[2,4,4,16,128]{4,3,2,1,0:T(8,128)(2,1)}, bf16[2,4,4,16,128]{4,3,2,1,0:T(8,128)(2,1)S(1)}, u32[]{:S(2)}, u32[]{:S(2)}) collective-permute-start(bf16[2,4,4,16,128]{4,3,2,1,0:T(8,128)(2,1)} %get-tuple-element.66), channel_id=1, source_target_pairs={{0,10},{1,11},{2,8},{3,9},{4,14},{5,15},{6,12},{7,13},{8,2},{9,3},... | collective-permute-start | bytes 393224 | tf_op jit(solution)/shard_map/ppermute | solution.py:431
  37.5 1.9 %collective-permute-done.7.refs_9_ = bf16[2,4,4,16,128]{4,3,2,1,0:T(8,128)(2,1)S(1)} collective-permute-done((bf16[2,4,4,16,128]{4,3,2,1,0:T(8,128)(2,1)}, bf16[2,4,4,16,128]{4,3,2,1,0:T(8,128)(2,1)S(1)}, u32[]{:S(2)}, u32[]{:S(2)}) %collective-permute-start.7) | collective-permute-done | bytes 131104 | tf_op jit(solution)/shard_map/ppermute | solution.py:431
  39.8 3.1 %collective-permute-done.14.refs_11_ = bf16[2,4,4,16,128]{4,3,2,1,0:T(8,128)(2,1)S(1)} collective-permute-done((bf16[2,4,4,16,128]{4,3,2,1,0:T(8,128)(2,1)}, bf16[2,4,4,16,128]{4,3,2,1,0:T(8,128)(2,1)S(1)}, u32[]{:S(2)}, u32[]{:S(2)}) %collective-permute-start.14) | collective-permute-done | bytes 131104 | tf_op jit(solution)/shard_map/ppermute | solution.py:431
  43.9 5.6 %cross.1 = (bf16[16,2,128,128]{3,2,1,0:T(8,128)(2,1)S(1)}, f32[16,2,4,4,16,128]{5,4,3,2,1,0:T(8,128)S(1)}, bf16[4,2,2048,256]{3,2,1,0:T(8,128)(2,1)S(1)}) custom-call(s32[4,8,2]{2,1,0:T(8,128)S(1)} %copy.10.pairs_ref, f32[1024]{0:T(1024)S(1)} %reshape.6.inverse_ref, bf16[2,4,4,16,128]{4,3,2,1,0:T(8,128)(2,1)S(1)} %collective-permute-done.9.refs_0_, ...), custom_call_target="tpu_custom_call" | custom-call | flops 54525952 | bytes 4194304 | tf_op jit(solution)/shard_map/cross/pallas_call | solution.py:263
  49.5 4.5 %collective-permute-done.8.refs_2_ = bf16[2,4,4,16,128]{4,3,2,1,0:T(8,128)(2,1)S(1)} collective-permute-done((bf16[2,4,4,16,128]{4,3,2,1,0:T(8,128)(2,1)}, bf16[2,4,4,16,128]{4,3,2,1,0:T(8,128)(2,1)S(1)}, u32[]{:S(2)}, u32[]{:S(2)}) %collective-permute-start.8) | collective-permute-done | bytes 131104 | tf_op jit(solution)/shard_map/ppermute | solution.py:431
  54.0 3.8 %cross_rest.1 = (bf16[16,2,128,128]{3,2,1,0:T(8,128)(2,1)S(1)}, f32[16,2,4,4,16,128]{5,4,3,2,1,0:T(8,128)S(1)}, bf16[2,128,128]{2,1,0:T(8,128)(2,1)S(1)}, bf16[2...) custom-call(s32[4,8,2]{2,1,0:T(8,128)S(1)} %copy.10.pairs_ref, ...), custom_call_target="tpu_custom_call", output_to_operand_aliasing={{0}: (5, {}), {1}: (6, {})} | custom-call | flops 12582912 | bytes 4194304 | tf_op jit(solution)/shard_map/cross_rest/pallas_call | solution.py:263
  57.8 2.5 %collective-permute-start.24 = (bf16[2,128,128]{2,1,0:T(8,128)(2,1)S(1)}, bf16[2,128,128]{2,1,0:T(8,128)(2,1)S(1)}, u32[]{:S(2)}, u32[]{:S(2)}) collective-permute-start(bf16[2,128,128]{2,1,0:T(8,128)(2,1)S(1)} %get-tuple-element.107), channel_id=1, source_target_pairs={{0,12},{1,13},{2,14},{3,15},{4,8},{5,9},{6,10},{7,11},{8,4},{9,5},... | collective-permute-start | bytes 196616 | tf_op jit(solution)/shard_map/ppermute | solution.py:431
  61.7 3.4 %collective-permute-start.21 = (bf16[2,128,128]{2,1,0:T(8,128)(2,1)S(1)}, bf16[2,128,128]{2,1,0:T(8,128)(2,1)S(1)}, u32[]{:S(2)}, u32[]{:S(2)}) collective-permute-start(bf16[2,128,128]{2,1,0:T(8,128)(2,1)S(1)} %get-tuple-element.102), channel_id=1, source_target_pairs={{0,14},{1,15},{2,12},{3,13},{4,10},{5,11},{6,8},{7,9},{8,6},{9,7},... | collective-permute-start | bytes 196616 | tf_op jit(solution)/shard_map/ppermute | solution.py:431
  65.8 1.9 %collective-permute-start.27 = (bf16[2,128,128]{2,1,0:T(8,128)(2,1)S(1)}, bf16[2,128,128]{2,1,0:T(8,128)(2,1)S(1)}, u32[]{:S(2)}, u32[]{:S(2)}) collective-permute-start(bf16[2,128,128]{2,1,0:T(8,128)(2,1)S(1)} %get-tuple-element.112), channel_id=1, source_target_pairs={{0,15},{1,14},{2,13},{3,12},{4,11},{5,10},{6,9},{7,8},{8,7},{9,6},... | collective-permute-start | bytes 196616 | tf_op jit(solution)/shard_map/ppermute | solution.py:431
  67.7 2.5 %collective-permute-start.19 = (bf16[2,128,128]{2,1,0:T(8,128)(2,1)S(1)}, bf16[2,128,128]{2,1,0:T(8,128)(2,1)S(1)}, u32[]{:S(2)}, u32[]{:S(2)}) collective-permute-start(bf16[2,128,128]{2,1,0:T(8,128)(2,1)S(1)} %get-tuple-element.98), channel_id=1, source_target_pairs={{0,8},{1,9},{2,10},{3,11},{4,12},{5,13},{6,14},{7,15},{8,0},{9,1},... | collective-permute-start | bytes 196616 | tf_op jit(solution)/shard_map/ppermute | solution.py:431
  73.0 2.2 %collective-permute-start.17 = (bf16[2,128,128]{2,1,0:T(8,128)(2,1)S(1)}, bf16[2,128,128]{2,1,0:T(8,128)(2,1)S(1)}, u32[]{:S(2)}, u32[]{:S(2)}) collective-permute-start(bf16[2,128,128]{2,1,0:T(8,128)(2,1)S(1)} %get-tuple-element.94), channel_id=1, source_target_pairs={{0,10},{1,11},{2,8},{3,9},{4,14},{5,15},{6,12},{7,13},{8,2},{9,3},... | collective-permute-start | bytes 196616 | tf_op jit(solution)/shard_map/ppermute | solution.py:431
  75.2 3.3 %collective-permute-start.20 = (bf16[2,128,128]{2,1,0:T(8,128)(2,1)S(1)}, bf16[2,128,128]{2,1,0:T(8,128)(2,1)S(1)}, u32[]{:S(2)}, u32[]{:S(2)}) collective-permute-start(bf16[2,128,128]{2,1,0:T(8,128)(2,1)S(1)} %get-tuple-element.99), channel_id=1, source_target_pairs={{0,7},{1,6},{2,5},{3,4},{4,3},{5,2},{6,1},{7,0},{8,15},{9,14},{10,... | collective-permute-start | bytes 196616 | tf_op jit(solution)/shard_map/ppermute | solution.py:431
  80.2 2.2 %lags_first.1 = (f32[4,2,128,256]{3,2,1,0:T(8,128)S(1)}, f32[128,128]{1,0:T(8,128)S(1)}) custom-call(bf16[2,128,128]{2,1,0:T(8,128)(2,1)S(1)} %get-tuple-element.106.refs_0_, bf16[2,128,128]{2,1,0:T(8,128)(2,1)S(1)} %collective-permute-done.24.refs_1_, bf16[2,128,128]{2,1,0:T(8,128)(2,1)S(1)} %collective-permute-done.25.refs_2_, ...), custom_call_target="tpu_custom_call" | custom-call | flops 1073741824 | bytes 4194304 | tf_op jit(solution)/shard_map/lags_first/pallas_call | solution.py:410
  82.4 2.2 %collective-permute-done.23.refs_2_ = bf16[2,128,128]{2,1,0:T(8,128)(2,1)S(1)} collective-permute-done((bf16[2,128,128]{2,1,0:T(8,128)(2,1)S(1)}, bf16[2,128,128]{2,1,0:T(8,128)(2,1)S(1)}, u32[]{:S(2)}, u32[]{:S(2)}) %collective-permute-start.23) | collective-permute-done | bytes 65568 | tf_op jit(solution)/shard_map/ppermute | solution.py:431
  84.6 1.5 %lags.1 = f32[128,2048]{1,0:T(8,128)} custom-call(bf16[2,128,128]{2,1,0:T(8,128)(2,1)S(1)} %collective-permute-done.17.refs_0_, bf16[2,128,128]{2,1,0:T(8,128)(2,1)S(1)} %collective-permute-done.20.refs_1_, bf16[2,128,128]{2,1,0:T(8,128)(2,1)S(1)} %collective-permute-done.23.refs_2_, bf16[4,2,2048,256]{3,2,1,0:T(8,128)(2,1)S(1)} %get-tuple-element.105.refs_13_.refs_3_, ...), custom_call_target="tpu_custom_call" | custom-call | flops 1073741824 | bytes 4194304 | tf_op jit(solution)/shard_map/lags/pallas_call | solution.py:410
  (51 shorter events, 11.7 us)
Async XLA Ops:
  2.7 13.4 %collective-permute-start.10 = (bf16[2,4,4,16,128]{4,3,2,1,0:T(8,128)(2,1)}, bf16[2,4,4,16,128]{4,3,2,1,0:T(8,128)(2,1)S(1)}, u32[]{:S(2)}, u32[]{:S(2)}) collective-permute-start(bf16[2,4,4,16,128]{4,3,2,1,0:T(8,128)(2,1)} %get-tuple-element.78), channel_id=1, source_target_pairs={{0,1},{1,0},{2,3},{3,2},{4,5},{5,4},{6,7},{7,6},{8,9},{9,8},{10,11... | collective-permute-start | bytes 393224 | tf_op jit(solution)/shard_map/ppermute | solution.py:431
  2.8 14.8 %collective-permute-start.9 = (bf16[2,4,4,16,128]{4,3,2,1,0:T(8,128)(2,1)}, bf16[2,4,4,16,128]{4,3,2,1,0:T(8,128)(2,1)S(1)}, u32[]{:S(2)}, u32[]{:S(2)}) collective-permute-start(bf16[2,4,4,16,128]{4,3,2,1,0:T(8,128)(2,1)} %get-tuple-element.77), channel_id=1, source_target_pairs={{0,12},{1,13},{2,14},{3,15},{4,8},{5,9},{6,10},{7,11},{8,4},{9,5},... | collective-permute-start | bytes 393224 | tf_op jit(solution)/shard_map/ppermute | solution.py:431
  7.6 10.4 %collective-permute-start = (bf16[2,4,4,16,128]{4,3,2,1,0:T(8,128)(2,1)}, bf16[2,4,4,16,128]{4,3,2,1,0:T(8,128)(2,1)S(1)}, u32[]{:S(2)}, u32[]{:S(2)}) collective-permute-start(bf16[2,4,4,16,128]{4,3,2,1,0:T(8,128)(2,1)} %get-tuple-element.64), channel_id=1, source_target_pairs={{0,13},{1,12},{2,15},{3,14},{4,9},{5,8},{6,11},{7,10},{8,5},{9,4},... | collective-permute-start | bytes 393224 | tf_op jit(solution)/shard_map/ppermute | solution.py:431
  11.4 14.2 %collective-permute-start.3 = (bf16[2,4,4,16,128]{4,3,2,1,0:T(8,128)(2,1)}, bf16[2,4,4,16,128]{4,3,2,1,0:T(8,128)(2,1)S(1)}, u32[]{:S(2)}, u32[]{:S(2)}) collective-permute-start(bf16[2,4,4,16,128]{4,3,2,1,0:T(8,128)(2,1)} %get-tuple-element.69), channel_id=1, source_target_pairs={{0,2},{1,3},{2,0},{3,1},{4,6},{5,7},{6,4},{7,5},{8,10},{9,11},{10,... | collective-permute-start | bytes 393224 | tf_op jit(solution)/shard_map/ppermute | solution.py:431
  12.8 13.7 %collective-permute-start.6 = (bf16[2,4,4,16,128]{4,3,2,1,0:T(8,128)(2,1)}, bf16[2,4,4,16,128]{4,3,2,1,0:T(8,128)(2,1)S(1)}, u32[]{:S(2)}, u32[]{:S(2)}) collective-permute-start(bf16[2,4,4,16,128]{4,3,2,1,0:T(8,128)(2,1)} %get-tuple-element.74), channel_id=1, source_target_pairs={{0,14},{1,15},{2,12},{3,13},{4,10},{5,11},{6,8},{7,9},{8,6},{9,7},... | collective-permute-start | bytes 393224 | tf_op jit(solution)/shard_map/ppermute | solution.py:431
  16.1 13.9 %collective-permute-start.12 = (bf16[2,4,4,16,128]{4,3,2,1,0:T(8,128)(2,1)}, bf16[2,4,4,16,128]{4,3,2,1,0:T(8,128)(2,1)S(1)}, u32[]{:S(2)}, u32[]{:S(2)}) collective-permute-start(bf16[2,4,4,16,128]{4,3,2,1,0:T(8,128)(2,1)} %get-tuple-element.82), channel_id=1, source_target_pairs={{0,15},{1,14},{2,13},{3,12},{4,11},{5,10},{6,9},{7,8},{8,7},{9,6},... | collective-permute-start | bytes 393224 | tf_op jit(solution)/shard_map/ppermute | solution.py:431
  17.7 14.4 %collective-permute-start.11 = (bf16[2,4,4,16,128]{4,3,2,1,0:T(8,128)(2,1)}, bf16[2,4,4,16,128]{4,3,2,1,0:T(8,128)(2,1)S(1)}, u32[]{:S(2)}, u32[]{:S(2)}) collective-permute-start(bf16[2,4,4,16,128]{4,3,2,1,0:T(8,128)(2,1)} %get-tuple-element.80), channel_id=1, source_target_pairs={{0,3},{1,2},{2,1},{3,0},{4,7},{5,6},{6,5},{7,4},{8,11},{9,10},{10,... | collective-permute-start | bytes 393224 | tf_op jit(solution)/shard_map/ppermute | solution.py:431
  18.0 14.8 %collective-permute-start.1 = (bf16[2,4,4,16,128]{4,3,2,1,0:T(8,128)(2,1)}, bf16[2,4,4,16,128]{4,3,2,1,0:T(8,128)(2,1)S(1)}, u32[]{:S(2)}, u32[]{:S(2)}) collective-permute-start(bf16[2,4,4,16,128]{4,3,2,1,0:T(8,128)(2,1)} %get-tuple-element.65), channel_id=1, source_target_pairs={{0,4},{1,5},{2,6},{3,7},{4,0},{5,1},{6,2},{7,3},{8,12},{9,13},{10,... | collective-permute-start | bytes 393224 | tf_op jit(solution)/shard_map/ppermute | solution.py:431
  25.5 10.7 %collective-permute-start.4 = (bf16[2,4,4,16,128]{4,3,2,1,0:T(8,128)(2,1)}, bf16[2,4,4,16,128]{4,3,2,1,0:T(8,128)(2,1)S(1)}, u32[]{:S(2)}, u32[]{:S(2)}) collective-permute-start(bf16[2,4,4,16,128]{4,3,2,1,0:T(8,128)(2,1)} %get-tuple-element.70), channel_id=1, source_target_pairs={{0,8},{1,9},{2,10},{3,11},{4,12},{5,13},{6,14},{7,15},{8,0},{9,1},... | collective-permute-start | bytes 393224 | tf_op jit(solution)/shard_map/ppermute | solution.py:431
  26.5 12.9 %collective-permute-start.7 = (bf16[2,4,4,16,128]{4,3,2,1,0:T(8,128)(2,1)}, bf16[2,4,4,16,128]{4,3,2,1,0:T(8,128)(2,1)S(1)}, u32[]{:S(2)}, u32[]{:S(2)}) collective-permute-start(bf16[2,4,4,16,128]{4,3,2,1,0:T(8,128)(2,1)} %get-tuple-element.75), channel_id=1, source_target_pairs={{0,5},{1,4},{2,7},{3,6},{4,1},{5,0},{6,3},{7,2},{8,13},{9,12},{10,... | collective-permute-start | bytes 393224 | tf_op jit(solution)/shard_map/ppermute | solution.py:431
  30.0 13.0 %collective-permute-start.14 = (bf16[2,4,4,16,128]{4,3,2,1,0:T(8,128)(2,1)}, bf16[2,4,4,16,128]{4,3,2,1,0:T(8,128)(2,1)S(1)}, u32[]{:S(2)}, u32[]{:S(2)}) collective-permute-start(bf16[2,4,4,16,128]{4,3,2,1,0:T(8,128)(2,1)} %get-tuple-element.86), channel_id=1, source_target_pairs={{0,6},{1,7},{2,4},{3,5},{4,2},{5,3},{6,0},{7,1},{8,14},{9,15},{10,... | collective-permute-start | bytes 393224 | tf_op jit(solution)/shard_map/ppermute | solution.py:431
  32.0 10.9 %collective-permute-start.13 = (bf16[2,4,4,16,128]{4,3,2,1,0:T(8,128)(2,1)}, bf16[2,4,4,16,128]{4,3,2,1,0:T(8,128)(2,1)S(1)}, u32[]{:S(2)}, u32[]{:S(2)}) collective-permute-start(bf16[2,4,4,16,128]{4,3,2,1,0:T(8,128)(2,1)} %get-tuple-element.84), channel_id=1, source_target_pairs={{0,9},{1,8},{2,11},{3,10},{4,13},{5,12},{6,15},{7,14},{8,1},{9,0},... | collective-permute-start | bytes 393224 | tf_op jit(solution)/shard_map/ppermute | solution.py:431
  32.8 16.7 %collective-permute-start.2 = (bf16[2,4,4,16,128]{4,3,2,1,0:T(8,128)(2,1)}, bf16[2,4,4,16,128]{4,3,2,1,0:T(8,128)(2,1)S(1)}, u32[]{:S(2)}, u32[]{:S(2)}) collective-permute-start(bf16[2,4,4,16,128]{4,3,2,1,0:T(8,128)(2,1)} %get-tuple-element.66), channel_id=1, source_target_pairs={{0,10},{1,11},{2,8},{3,9},{4,14},{5,15},{6,12},{7,13},{8,2},{9,3},... | collective-permute-start | bytes 393224 | tf_op jit(solution)/shard_map/ppermute | solution.py:431
  36.2 13.3 %collective-permute-start.5 = (bf16[2,4,4,16,128]{4,3,2,1,0:T(8,128)(2,1)}, bf16[2,4,4,16,128]{4,3,2,1,0:T(8,128)(2,1)S(1)}, u32[]{:S(2)}, u32[]{:S(2)}) collective-permute-start(bf16[2,4,4,16,128]{4,3,2,1,0:T(8,128)(2,1)} %get-tuple-element.71), channel_id=1, source_target_pairs={{0,7},{1,6},{2,5},{3,4},{4,3},{5,2},{6,1},{7,0},{8,15},{9,14},{10,... | collective-permute-start | bytes 393224 | tf_op jit(solution)/shard_map/ppermute | solution.py:431
  39.5 14.5 %collective-permute-start.8 = (bf16[2,4,4,16,128]{4,3,2,1,0:T(8,128)(2,1)}, bf16[2,4,4,16,128]{4,3,2,1,0:T(8,128)(2,1)S(1)}, u32[]{:S(2)}, u32[]{:S(2)}) collective-permute-start(bf16[2,4,4,16,128]{4,3,2,1,0:T(8,128)(2,1)} %get-tuple-element.76), channel_id=1, source_target_pairs={{0,11},{1,10},{2,9},{3,8},{4,15},{5,14},{6,13},{7,12},{8,3},{9,2},... | collective-permute-start | bytes 393224 | tf_op jit(solution)/shard_map/ppermute | solution.py:431
  57.8 7.3 %collective-permute-start.24 = (bf16[2,128,128]{2,1,0:T(8,128)(2,1)S(1)}, bf16[2,128,128]{2,1,0:T(8,128)(2,1)S(1)}, u32[]{:S(2)}, u32[]{:S(2)}) collective-permute-start(bf16[2,128,128]{2,1,0:T(8,128)(2,1)S(1)} %get-tuple-element.107), channel_id=1, source_target_pairs={{0,12},{1,13},{2,14},{3,15},{4,8},{5,9},{6,10},{7,11},{8,4},{9,5},... | collective-permute-start | bytes 196616 | tf_op jit(solution)/shard_map/ppermute | solution.py:431
  61.7 8.4 %collective-permute-start.21 = (bf16[2,128,128]{2,1,0:T(8,128)(2,1)S(1)}, bf16[2,128,128]{2,1,0:T(8,128)(2,1)S(1)}, u32[]{:S(2)}, u32[]{:S(2)}) collective-permute-start(bf16[2,128,128]{2,1,0:T(8,128)(2,1)S(1)} %get-tuple-element.102), channel_id=1, source_target_pairs={{0,14},{1,15},{2,12},{3,13},{4,10},{5,11},{6,8},{7,9},{8,6},{9,7},... | collective-permute-start | bytes 196616 | tf_op jit(solution)/shard_map/ppermute | solution.py:431
  65.8 7.1 %collective-permute-start.27 = (bf16[2,128,128]{2,1,0:T(8,128)(2,1)S(1)}, bf16[2,128,128]{2,1,0:T(8,128)(2,1)S(1)}, u32[]{:S(2)}, u32[]{:S(2)}) collective-permute-start(bf16[2,128,128]{2,1,0:T(8,128)(2,1)S(1)} %get-tuple-element.112), channel_id=1, source_target_pairs={{0,15},{1,14},{2,13},{3,12},{4,11},{5,10},{6,9},{7,8},{8,7},{9,6},... | collective-permute-start | bytes 196616 | tf_op jit(solution)/shard_map/ppermute | solution.py:431
  67.7 7.5 %collective-permute-start.19 = (bf16[2,128,128]{2,1,0:T(8,128)(2,1)S(1)}, bf16[2,128,128]{2,1,0:T(8,128)(2,1)S(1)}, u32[]{:S(2)}, u32[]{:S(2)}) collective-permute-start(bf16[2,128,128]{2,1,0:T(8,128)(2,1)S(1)} %get-tuple-element.98), channel_id=1, source_target_pairs={{0,8},{1,9},{2,10},{3,11},{4,12},{5,13},{6,14},{7,15},{8,0},{9,1},... | collective-permute-start | bytes 196616 | tf_op jit(solution)/shard_map/ppermute | solution.py:431
  70.1 8.4 %collective-permute-start.22 = (bf16[2,128,128]{2,1,0:T(8,128)(2,1)S(1)}, bf16[2,128,128]{2,1,0:T(8,128)(2,1)S(1)}, u32[]{:S(2)}, u32[]{:S(2)}) collective-permute-start(bf16[2,128,128]{2,1,0:T(8,128)(2,1)S(1)} %get-tuple-element.103), channel_id=1, source_target_pairs={{0,5},{1,4},{2,7},{3,6},{4,1},{5,0},{6,3},{7,2},{8,13},{9,12},{10,... | collective-permute-start | bytes 196616 | tf_op jit(solution)/shard_map/ppermute | solution.py:431
  71.4 7.4 %collective-permute-start.28 = (bf16[2,128,128]{2,1,0:T(8,128)(2,1)S(1)}, bf16[2,128,128]{2,1,0:T(8,128)(2,1)S(1)}, u32[]{:S(2)}, u32[]{:S(2)}) collective-permute-start(bf16[2,128,128]{2,1,0:T(8,128)(2,1)S(1)} %get-tuple-element.114), channel_id=1, source_target_pairs={{0,9},{1,8},{2,11},{3,10},{4,13},{5,12},{6,15},{7,14},{8,1},{9,0},... | collective-permute-start | bytes 196616 | tf_op jit(solution)/shard_map/ppermute | solution.py:431
  72.9 7.3 %collective-permute-start.29 = (bf16[2,128,128]{2,1,0:T(8,128)(2,1)S(1)}, bf16[2,128,128]{2,1,0:T(8,128)(2,1)S(1)}, u32[]{:S(2)}, u32[]{:S(2)}) collective-permute-start(bf16[2,128,128]{2,1,0:T(8,128)(2,1)S(1)} %get-tuple-element.116), channel_id=1, source_target_pairs={{0,6},{1,7},{2,4},{3,5},{4,2},{5,3},{6,0},{7,1},{8,14},{9,15},{10,... | collective-permute-start | bytes 196616 | tf_op jit(solution)/shard_map/ppermute | solution.py:431
  73.0 9.3 %collective-permute-start.17 = (bf16[2,128,128]{2,1,0:T(8,128)(2,1)S(1)}, bf16[2,128,128]{2,1,0:T(8,128)(2,1)S(1)}, u32[]{:S(2)}, u32[]{:S(2)}) collective-permute-start(bf16[2,128,128]{2,1,0:T(8,128)(2,1)S(1)} %get-tuple-element.94), channel_id=1, source_target_pairs={{0,10},{1,11},{2,8},{3,9},{4,14},{5,15},{6,12},{7,13},{8,2},{9,3},... | collective-permute-start | bytes 196616 | tf_op jit(solution)/shard_map/ppermute | solution.py:431
  75.2 7.2 %collective-permute-start.20 = (bf16[2,128,128]{2,1,0:T(8,128)(2,1)S(1)}, bf16[2,128,128]{2,1,0:T(8,128)(2,1)S(1)}, u32[]{:S(2)}, u32[]{:S(2)}) collective-permute-start(bf16[2,128,128]{2,1,0:T(8,128)(2,1)S(1)} %get-tuple-element.99), channel_id=1, source_target_pairs={{0,7},{1,6},{2,5},{3,4},{4,3},{5,2},{6,1},{7,0},{8,15},{9,14},{10,... | collective-permute-start | bytes 196616 | tf_op jit(solution)/shard_map/ppermute | solution.py:431
  (9 other events, 106.5 us)

commit v7 on v6

--- a/solution.py
+++ b/solution.py
@@ -13,7 +13,7 @@
 LAGS = 2048
 MIB = 1 << 20
 ORDER = (12, 1, 13, 2, 14, 3, 15, 4, 8, 5, 9, 6, 10, 7, 11)
-FIRST = 3
+FIRST = 2
 LATE = 3
 
 
@@ -73,10 +73,15 @@
 
 
 def piece_kernel(aways, counts_ref, masks_ref, spectra_ref, *refs):
-    out_refs, raw_ref, rows_ref, sems = refs[: len(aways)], refs[-3], refs[-2], refs[-1]
+    out_refs, (raw_ref, rows_ref, held_ref, number_ref, sems) = refs[: len(aways)], refs[len(aways) :]
     me = lax.axis_index("sta")
     parts, days, windows, slots, bins = raw_ref.shape[1:]
-    count = counts_ref[me]
+    small = [
+        pltpu.make_async_copy(counts_ref, number_ref, sems.at[len(aways)]),
+        pltpu.make_async_copy(masks_ref, held_ref, sems.at[len(aways) + 1]),
+    ]
+    for copy in small:
+        copy.start()
     loads = []
     for n, away in enumerate(aways):
         columns = pl.ds(pl.multiple_of((me ^ away) * bins, 128), bins)
@@ -84,10 +89,13 @@
             pltpu.make_async_copy(spectra_ref.at[:, :, :, :, columns], raw_ref.at[n], sems.at[n])
         )
         loads[n].start()
+    for copy in small:
+        copy.wait()
+    count = number_ref[me]
     lane = lax.broadcasted_iota(jnp.int32, masks_ref.shape[1:], 1)
     wide = []
     for d in range(days):
-        mine = jnp.where(lane == me, masks_ref[d], 0)
+        mine = jnp.where(lane == me, held_ref[d], 0)
         keep = (jnp.sum(mine, axis=1, keepdims=True) > 0).astype(jnp.float32)
         wide.append(jnp.broadcast_to(keep, (windows, bins)))
     live = [jnp.where(slot < count, 1.0, 0.0) for slot in range(slots)]
@@ -115,8 +123,8 @@
     return pl.pallas_call(
         functools.partial(piece_kernel, aways),
         in_specs=[
-            pl.BlockSpec(memory_space=pltpu.SMEM),
-            pl.BlockSpec(memory_space=pltpu.VMEM),
+            pl.BlockSpec(memory_space=pl.ANY),
+            pl.BlockSpec(memory_space=pl.ANY),
             pl.BlockSpec(memory_space=pl.ANY),
         ],
         out_specs=[pl.BlockSpec(memory_space=pltpu.VMEM)] * len(aways),
@@ -124,7 +132,9 @@
         scratch_shapes=[
             pltpu.VMEM((len(aways), parts, days, windows, slots, bins), jnp.bfloat16),
             pltpu.VMEM((days, windows * slots, bins), jnp.float32),
-            pltpu.SemaphoreType.DMA((len(aways),)),
+            pltpu.VMEM(window_masks.shape, jnp.int32),
+            pltpu.SMEM(block_counts.shape, jnp.int32),
+            pltpu.SemaphoreType.DMA((len(aways) + 2,)),
         ],
         compiler_params=pltpu.CompilerParams(vmem_limit_bytes=60 * MIB),
         name=name,
@@ -199,7 +209,7 @@
     return stacked
 
 
-def cross_kernel(sources, late, aliased, pairs_ref, inverse_ref, *refs):
+def cross_kernel(sources, late, aliased, rounds, pairs, pairs_ref, inverse_ref, *refs):
     block_refs, refs = refs[: len(sources)], refs[len(sources) + aliased :]
     if late:
         table_ref, out_ref, blocks_ref, held_ref, sem = refs
@@ -209,7 +219,6 @@
     else:
         out_ref, blocks_ref, *share_refs = refs
     block_count, _, days, slots, _, bins = blocks_ref.shape
-    rounds, pairs = pairs_ref.shape[0], pairs_ref.shape[1]
     rows = lax.broadcasted_iota(jnp.int32, (8, bins), 0)
     held = days * pairs // block_count
     me = lax.axis_index("sta")
@@ -224,9 +233,9 @@
         else:
             blocks_ref[me ^ source] = ref[...].astype(jnp.float32)
 
-    def one_pair(index, carry):
-        r, p = index // pairs, index % pairs
-        a, b = pairs_ref[r, p, 0], pairs_ref[r, p, 1]
+    def one_pair(r, p):
+        a = pairs_ref[(r * pairs + p) * 2]
+        b = pairs_ref[(r * pairs + p) * 2 + 1]
 
         def work():
             stacked = pair_stack(a, b, inverse_ref, blocks_ref, rows)
@@ -235,15 +244,25 @@
                 for c in range(2):
                     out_ref[(p * days + d) // held, c, pl.ds(row, slots * slots), :] = stacked[d][c]
 
-        if len(late) == 0 and aliased == 0:
+        if late:
+            waits = [(x ^ me) == away for x in (a, b) for away in late]
+            pl.when(jnp.logical_not(functools.reduce(jnp.logical_or, waits)))(work)
+        else:
             work()
-        else:
-            waits = [(x ^ me) == away for x in (a, b) for away in late or sources]
-            waits = functools.reduce(jnp.logical_or, waits)
-            pl.when(jnp.logical_not(waits) if late else waits)(work)
+
+    def any_pair(index, carry):
+        one_pair(index // pairs, index % pairs)
         return carry
 
-    lax.fori_loop(0, rounds * pairs, one_pair, 0)
+    def late_pairs(r, carry):
+        for source in sources:
+            one_pair(r, pairs_ref[(rounds * pairs) * 2 + r * block_count + (me ^ source)])
+        return carry
+
+    if aliased:
+        lax.fori_loop(0, rounds, late_pairs, 0)
+    else:
+        lax.fori_loop(0, rounds * pairs, any_pair, 0)
     for share_ref, away in zip(share_refs, (0,) + ORDER):
         share_ref[...] = out_ref[me ^ away]
     if late:
@@ -258,10 +277,12 @@
     stack = rounds * held * slots * slots
     spread = devices if started else 0
     tables = [] if table is None else [table]
+    blocks_of = pair_table[..., None] == jnp.arange(devices, dtype=jnp.int32)
+    owner = jnp.sum(blocks_of * jnp.arange(pairs, dtype=jnp.int32)[:, None, None], axis=(1, 2))
     wide = 4 * devices * parts * days * slots * windows * max(bins, 128)
     work = int(rounds * pairs * days * slots * slots * windows * bins * share)
     return pl.pallas_call(
-        functools.partial(cross_kernel, sources, late, len(started)),
+        functools.partial(cross_kernel, sources, late, len(started), rounds, pairs),
         in_specs=[pl.BlockSpec(memory_space=pltpu.SMEM)] * 2
         + [pl.BlockSpec(memory_space=pltpu.VMEM)] * (len(blocks) + len(started))
         + [pl.BlockSpec(memory_space=pl.ANY)] * len(tables),
@@ -279,7 +300,7 @@
             flops=16 * work, bytes_accessed=4 << 20, transcendentals=0
         ),
         name="cross_rest" if started else "cross",
-    )(pair_table, inverse, *blocks, *started, *tables)
+    )(jnp.concatenate([pair_table.reshape(-1), owner.reshape(-1)]), inverse, *blocks, *started, *tables)
 
 
 def quarter_turns(depth):

time: 86.4 us -> 84.4 us (0.977)
  Pallas kernels: 19.4 us -> 16.7 us
  starting transfers between devices: 50.9 us -> 52.4 us
  waiting for transfers between devices: 14.4 us -> 13.3 us
    pallas_call x2, Pallas kernels: 6.39 us -> 4.82 us  [pieces(): pl.pallas_call(functools.partial(piece_kernel, aways), in_specs=[pl.Block...]
    ppermute x30, starting transfers between devices: 50.9 us -> 52.4 us  [swap(): share = lax.ppermute(share, 'sta', [(n, n ^ away) for n in range(devices)])]
    pallas_call x2, Pallas kernels: 9.38 us -> 8.07 us  [cross(): pl.pallas_call(functools.partial(cross_kernel, sources, late, len(started...]
    ppermute x30, waiting for transfers between devices: 14.4 us -> 13.3 us  [swap(): share = lax.ppermute(share, 'sta', [(n, n ^ away) for n in range(devices)])]
  transfers between devices with their start and end apart: 30 -> 30, of which waited for: 6 -> 7; matrix products, arithmetic and copies ran while one was open for 0% -> 1% of each run, Pallas kernels for 13% -> 13%
where the time goes in v7:
time: 84.4 us; the launch traced here: 84.3 us
  starting transfers between devices  52.4 us (62%)
  Pallas kernels  16.7 us (20%)
  waiting for transfers between devices  13.3 us (16%)
  local copies, waits for them, and re-layouts  1.27 us (2%)
    ppermute x30, starting transfers between devices, swap(): share = lax.ppermute(share, 'sta', [(n, n ^ away) for n in range(devices)])  52.4 us
    ppermute x30, waiting for transfers between devices, swap(): share = lax.ppermute(share, 'sta', [(n, n ^ away) for n in range(devices)])  13.3 us
    pallas_call x2, Pallas kernels, cross(): pl.pallas_call(functools.partial(cross_kernel, sources, late, len(started...  8.07 us
    pallas_call x2, Pallas kernels, pieces(): pl.pallas_call(functools.partial(piece_kernel, aways), in_specs=[pl.Block...  4.82 us
    pallas_call x2, Pallas kernels, lags(): pl.pallas_call(body, in_specs=[vmem] * (len(stacked) + 1 + len(started)),...  3.86 us
  transfers between devices with their start and end apart: 30, of which 7 were waited for; matrix products, arithmetic and copies ran while one was open for 1% of the time, Pallas kernels for 13%

profile of v7, /device:TPU:1, one launch (start us, length us, event | category | flops | bytes accessed | tf_op | source)
XLA Modules:
  0.0 84.3 jit_solution(10128095310634230403)
XLA Ops:
  0.0 1.8 %pack_first.1 = (bf16[2,4,4,16,128]{4,3,2,1,0:T(8,128)(2,1)}, bf16[2,4,4,16,128]{4,3,2,1,0:T(8,128)(2,1)}) custom-call(s32[16]{0:T(128)} %counts_ref.3, s32[4,16,16]{2,1,0:T(8,128)} %masks_ref.3, bf16[2,4,16,4,2048]{4,3,2,1,0:T(4,128)(2,1)} %spectra_ref.3), custom_call_target="tpu_custom_call" | custom-call | tf_op jit(solution)/shard_map/pack_first/pallas_call | solution.py:123
  1.8 4.2 %collective-permute-start.9 = (bf16[2,4,4,16,128]{4,3,2,1,0:T(8,128)(2,1)}, bf16[2,4,4,16,128]{4,3,2,1,0:T(8,128)(2,1)S(1)}, u32[]{:S(2)}, u32[]{:S(2)}) collective-permute-start(bf16[2,4,4,16,128]{4,3,2,1,0:T(8,128)(2,1)} %get-tuple-element.77), channel_id=1, source_target_pairs={{0,12},{1,13},{2,14},{3,15},{4,8},{5,9},{6,10},{7,11},{8,4},{9,5},... | collective-permute-start | bytes 393224 | tf_op jit(solution)/shard_map/ppermute | solution.py:452
  6.9 3.1 %pack_rest.1 = (bf16[2,4,4,16,128]{4,3,2,1,0:T(8,128)(2,1)}, bf16[2,4,4,16,128]{4,3,2,1,0:T(8,128)(2,1)}, bf16[2,4,4,16,128]{4,3,2,1,0:T(8,128)(2,1)}, bf16[2,4,...) custom-call(s32[16]{0:T(128)} %counts_ref.3, ...), custom_call_target="tpu_custom_call" | custom-call | tf_op jit(solution)/shard_map/pack_rest/pallas_call | solution.py:123
  11.4 3.0 %collective-permute-start.6 = (bf16[2,4,4,16,128]{4,3,2,1,0:T(8,128)(2,1)}, bf16[2,4,4,16,128]{4,3,2,1,0:T(8,128)(2,1)S(1)}, u32[]{:S(2)}, u32[]{:S(2)}) collective-permute-start(bf16[2,4,4,16,128]{4,3,2,1,0:T(8,128)(2,1)} %get-tuple-element.74), channel_id=1, source_target_pairs={{0,14},{1,15},{2,12},{3,13},{4,10},{5,11},{6,8},{7,9},{8,6},{9,7},... | collective-permute-start | bytes 393224 | tf_op jit(solution)/shard_map/ppermute | solution.py:452
  14.4 1.9 %collective-permute-start.12 = (bf16[2,4,4,16,128]{4,3,2,1,0:T(8,128)(2,1)}, bf16[2,4,4,16,128]{4,3,2,1,0:T(8,128)(2,1)S(1)}, u32[]{:S(2)}, u32[]{:S(2)}) collective-permute-start(bf16[2,4,4,16,128]{4,3,2,1,0:T(8,128)(2,1)} %get-tuple-element.82), channel_id=1, source_target_pairs={{0,15},{1,14},{2,13},{3,12},{4,11},{5,10},{6,9},{7,8},{8,7},{9,6},... | collective-permute-start | bytes 393224 | tf_op jit(solution)/shard_map/ppermute | solution.py:452
  17.9 5.8 %collective-permute-start.1 = (bf16[2,4,4,16,128]{4,3,2,1,0:T(8,128)(2,1)}, bf16[2,4,4,16,128]{4,3,2,1,0:T(8,128)(2,1)S(1)}, u32[]{:S(2)}, u32[]{:S(2)}) collective-permute-start(bf16[2,4,4,16,128]{4,3,2,1,0:T(8,128)(2,1)} %get-tuple-element.65), channel_id=1, source_target_pairs={{0,4},{1,5},{2,6},{3,7},{4,0},{5,1},{6,2},{7,3},{8,12},{9,13},{10,... | collective-permute-start | bytes 393224 | tf_op jit(solution)/shard_map/ppermute | solution.py:452
  23.8 1.4 %collective-permute-start.4 = (bf16[2,4,4,16,128]{4,3,2,1,0:T(8,128)(2,1)}, bf16[2,4,4,16,128]{4,3,2,1,0:T(8,128)(2,1)S(1)}, u32[]{:S(2)}, u32[]{:S(2)}) collective-permute-start(bf16[2,4,4,16,128]{4,3,2,1,0:T(8,128)(2,1)} %get-tuple-element.70), channel_id=1, source_target_pairs={{0,8},{1,9},{2,10},{3,11},{4,12},{5,13},{6,14},{7,15},{8,0},{9,1},... | collective-permute-start | bytes 393224 | tf_op jit(solution)/shard_map/ppermute | solution.py:452
  25.2 2.9 %collective-permute-start.7 = (bf16[2,4,4,16,128]{4,3,2,1,0:T(8,128)(2,1)}, bf16[2,4,4,16,128]{4,3,2,1,0:T(8,128)(2,1)S(1)}, u32[]{:S(2)}, u32[]{:S(2)}) collective-permute-start(bf16[2,4,4,16,128]{4,3,2,1,0:T(8,128)(2,1)} %get-tuple-element.75), channel_id=1, source_target_pairs={{0,5},{1,4},{2,7},{3,6},{4,1},{5,0},{6,3},{7,2},{8,13},{9,12},{10,... | collective-permute-start | bytes 393224 | tf_op jit(solution)/shard_map/ppermute | solution.py:452
  28.3 2.0 %collective-permute-start.14 = (bf16[2,4,4,16,128]{4,3,2,1,0:T(8,128)(2,1)}, bf16[2,4,4,16,128]{4,3,2,1,0:T(8,128)(2,1)S(1)}, u32[]{:S(2)}, u32[]{:S(2)}) collective-permute-start(bf16[2,4,4,16,128]{4,3,2,1,0:T(8,128)(2,1)} %get-tuple-element.86), channel_id=1, source_target_pairs={{0,6},{1,7},{2,4},{3,5},{4,2},{5,3},{6,0},{7,1},{8,14},{9,15},{10,... | collective-permute-start | bytes 393224 | tf_op jit(solution)/shard_map/ppermute | solution.py:452
  30.9 4.5 %collective-permute-start.2 = (bf16[2,4,4,16,128]{4,3,2,1,0:T(8,128)(2,1)}, bf16[2,4,4,16,128]{4,3,2,1,0:T(8,128)(2,1)S(1)}, u32[]{:S(2)}, u32[]{:S(2)}) collective-permute-start(bf16[2,4,4,16,128]{4,3,2,1,0:T(8,128)(2,1)} %get-tuple-element.66), channel_id=1, source_target_pairs={{0,10},{1,11},{2,8},{3,9},{4,14},{5,15},{6,12},{7,13},{8,2},{9,3},... | collective-permute-start | bytes 393224 | tf_op jit(solution)/shard_map/ppermute | solution.py:452
  35.4 1.9 %collective-permute-start.5 = (bf16[2,4,4,16,128]{4,3,2,1,0:T(8,128)(2,1)}, bf16[2,4,4,16,128]{4,3,2,1,0:T(8,128)(2,1)S(1)}, u32[]{:S(2)}, u32[]{:S(2)}) collective-permute-start(bf16[2,4,4,16,128]{4,3,2,1,0:T(8,128)(2,1)} %get-tuple-element.71), channel_id=1, source_target_pairs={{0,7},{1,6},{2,5},{3,4},{4,3},{5,2},{6,1},{7,0},{8,15},{9,14},{10,... | collective-permute-start | bytes 393224 | tf_op jit(solution)/shard_map/ppermute | solution.py:452
  39.0 2.3 %collective-permute-done.14.refs_11_ = bf16[2,4,4,16,128]{4,3,2,1,0:T(8,128)(2,1)S(1)} collective-permute-done((bf16[2,4,4,16,128]{4,3,2,1,0:T(8,128)(2,1)}, bf16[2,4,4,16,128]{4,3,2,1,0:T(8,128)(2,1)S(1)}, u32[]{:S(2)}, u32[]{:S(2)}) %collective-permute-start.14) | collective-permute-done | bytes 131104 | tf_op jit(solution)/shard_map/ppermute | solution.py:452
  42.2 5.2 %cross.1 = (bf16[16,2,128,128]{3,2,1,0:T(8,128)(2,1)S(1)}, f32[16,2,4,4,16,128]{5,4,3,2,1,0:T(8,128)S(1)}, bf16[4,2,2048,256]{3,2,1,0:T(8,128)(2,1)S(1)}) custom-call(s32[128]{0:T(128)S(1)} %pad_add_fusion.pairs_ref, f32[1024]{0:T(1024)S(1)} %reshape.17.inverse_ref, bf16[2,4,4,16,128]{4,3,2,1,0:T(8,128)(2,1)S(1)} %collective-permute-done.9.refs_0_, ...), custom_call_target="tpu_custom_call" | custom-call | flops 54525952 | bytes 4194304 | tf_op jit(solution)/shard_map/cross/pallas_call | solution.py:284
  47.4 5.1 %collective-permute-done.8.refs_2_ = bf16[2,4,4,16,128]{4,3,2,1,0:T(8,128)(2,1)S(1)} collective-permute-done((bf16[2,4,4,16,128]{4,3,2,1,0:T(8,128)(2,1)}, bf16[2,4,4,16,128]{4,3,2,1,0:T(8,128)(2,1)S(1)}, u32[]{:S(2)}, u32[]{:S(2)}) %collective-permute-start.8) | collective-permute-done | bytes 131104 | tf_op jit(solution)/shard_map/ppermute | solution.py:452
  52.5 2.9 %cross_rest.1 = (bf16[16,2,128,128]{3,2,1,0:T(8,128)(2,1)S(1)}, f32[16,2,4,4,16,128]{5,4,3,2,1,0:T(8,128)S(1)}, bf16[2,128,128]{2,1,0:T(8,128)(2,1)S(1)}, bf16[2...) custom-call(s32[128]{0:T(128)S(1)} %pad_add_fusion.pairs_ref, ...), custom_call_target="tpu_custom_call", output_to_operand_aliasing={{0}: (5, {}), {1}: (6, {})} | custom-call | flops 12582912 | bytes 4194304 | tf_op jit(solution)/shard_map/cross_rest/pallas_call | solution.py:284
  55.4 3.4 %collective-permute-start.24 = (bf16[2,128,128]{2,1,0:T(8,128)(2,1)S(1)}, bf16[2,128,128]{2,1,0:T(8,128)(2,1)S(1)}, u32[]{:S(2)}, u32[]{:S(2)}) collective-permute-start(bf16[2,128,128]{2,1,0:T(8,128)(2,1)S(1)} %get-tuple-element.107), channel_id=1, source_target_pairs={{0,12},{1,13},{2,14},{3,15},{4,8},{5,9},{6,10},{7,11},{8,4},{9,5},... | collective-permute-start | bytes 196616 | tf_op jit(solution)/shard_map/ppermute | solution.py:452
  59.5 4.2 %collective-permute-start.21 = (bf16[2,128,128]{2,1,0:T(8,128)(2,1)S(1)}, bf16[2,128,128]{2,1,0:T(8,128)(2,1)S(1)}, u32[]{:S(2)}, u32[]{:S(2)}) collective-permute-start(bf16[2,128,128]{2,1,0:T(8,128)(2,1)S(1)} %get-tuple-element.102), channel_id=1, source_target_pairs={{0,14},{1,15},{2,12},{3,13},{4,10},{5,11},{6,8},{7,9},{8,6},{9,7},... | collective-permute-start | bytes 196616 | tf_op jit(solution)/shard_map/ppermute | solution.py:452
  64.3 1.7 %collective-permute-start.27 = (bf16[2,128,128]{2,1,0:T(8,128)(2,1)S(1)}, bf16[2,128,128]{2,1,0:T(8,128)(2,1)S(1)}, u32[]{:S(2)}, u32[]{:S(2)}) collective-permute-start(bf16[2,128,128]{2,1,0:T(8,128)(2,1)S(1)} %get-tuple-element.112), channel_id=1, source_target_pairs={{0,15},{1,14},{2,13},{3,12},{4,11},{5,10},{6,9},{7,8},{8,7},{9,6},... | collective-permute-start | bytes 196616 | tf_op jit(solution)/shard_map/ppermute | solution.py:452
  66.0 2.7 %collective-permute-start.19 = (bf16[2,128,128]{2,1,0:T(8,128)(2,1)S(1)}, bf16[2,128,128]{2,1,0:T(8,128)(2,1)S(1)}, u32[]{:S(2)}, u32[]{:S(2)}) collective-permute-start(bf16[2,128,128]{2,1,0:T(8,128)(2,1)S(1)} %get-tuple-element.98), channel_id=1, source_target_pairs={{0,8},{1,9},{2,10},{3,11},{4,12},{5,13},{6,14},{7,15},{8,0},{9,1},... | collective-permute-start | bytes 196616 | tf_op jit(solution)/shard_map/ppermute | solution.py:452
  71.4 2.3 %collective-permute-start.17 = (bf16[2,128,128]{2,1,0:T(8,128)(2,1)S(1)}, bf16[2,128,128]{2,1,0:T(8,128)(2,1)S(1)}, u32[]{:S(2)}, u32[]{:S(2)}) collective-permute-start(bf16[2,128,128]{2,1,0:T(8,128)(2,1)S(1)} %get-tuple-element.94), channel_id=1, source_target_pairs={{0,10},{1,11},{2,8},{3,9},{4,14},{5,15},{6,12},{7,13},{8,2},{9,3},... | collective-permute-start | bytes 196616 | tf_op jit(solution)/shard_map/ppermute | solution.py:452
  73.7 3.2 %collective-permute-start.20 = (bf16[2,128,128]{2,1,0:T(8,128)(2,1)S(1)}, bf16[2,128,128]{2,1,0:T(8,128)(2,1)S(1)}, u32[]{:S(2)}, u32[]{:S(2)}) collective-permute-start(bf16[2,128,128]{2,1,0:T(8,128)(2,1)S(1)} %get-tuple-element.99), channel_id=1, source_target_pairs={{0,7},{1,6},{2,5},{3,4},{4,3},{5,2},{6,1},{7,0},{8,15},{9,14},{10,... | collective-permute-start | bytes 196616 | tf_op jit(solution)/shard_map/ppermute | solution.py:452
  77.7 2.4 %lags_first.1 = (f32[4,2,128,256]{3,2,1,0:T(8,128)S(1)}, f32[128,128]{1,0:T(8,128)S(1)}) custom-call(bf16[2,128,128]{2,1,0:T(8,128)(2,1)S(1)} %get-tuple-element.106.refs_0_, bf16[2,128,128]{2,1,0:T(8,128)(2,1)S(1)} %collective-permute-done.24.refs_1_, bf16[2,128,128]{2,1,0:T(8,128)(2,1)S(1)} %collective-permute-done.25.refs_2_, ...), custom_call_target="tpu_custom_call" | custom-call | flops 1073741824 | bytes 4194304 | tf_op jit(solution)/shard_map/lags_first/pallas_call | solution.py:431
  80.1 2.7 %collective-permute-done.23.refs_2_ = bf16[2,128,128]{2,1,0:T(8,128)(2,1)S(1)} collective-permute-done((bf16[2,128,128]{2,1,0:T(8,128)(2,1)S(1)}, bf16[2,128,128]{2,1,0:T(8,128)(2,1)S(1)}, u32[]{:S(2)}, u32[]{:S(2)}) %collective-permute-start.23) | collective-permute-done | bytes 65568 | tf_op jit(solution)/shard_map/ppermute | solution.py:452
  82.8 1.5 %lags.1 = f32[128,2048]{1,0:T(8,128)} custom-call(bf16[2,128,128]{2,1,0:T(8,128)(2,1)S(1)} %collective-permute-done.17.refs_0_, bf16[2,128,128]{2,1,0:T(8,128)(2,1)S(1)} %collective-permute-done.20.refs_1_, bf16[2,128,128]{2,1,0:T(8,128)(2,1)S(1)} %collective-permute-done.23.refs_2_, bf16[4,2,2048,256]{3,2,1,0:T(8,128)(2,1)S(1)} %get-tuple-element.105.refs_13_.refs_3_, ...), custom_call_target="tpu_custom_call" | custom-call | flops 1073741824 | bytes 4194304 | tf_op jit(solution)/shard_map/lags/pallas_call | solution.py:431
  (55 shorter events, 12.3 us)
Async XLA Ops:
  1.8 12.6 %collective-permute-start.9 = (bf16[2,4,4,16,128]{4,3,2,1,0:T(8,128)(2,1)}, bf16[2,4,4,16,128]{4,3,2,1,0:T(8,128)(2,1)S(1)}, u32[]{:S(2)}, u32[]{:S(2)}) collective-permute-start(bf16[2,4,4,16,128]{4,3,2,1,0:T(8,128)(2,1)} %get-tuple-element.77), channel_id=1, source_target_pairs={{0,12},{1,13},{2,14},{3,15},{4,8},{5,9},{6,10},{7,11},{8,4},{9,5},... | collective-permute-start | bytes 393224 | tf_op jit(solution)/shard_map/ppermute | solution.py:452
  6.0 8.4 %collective-permute-start.10 = (bf16[2,4,4,16,128]{4,3,2,1,0:T(8,128)(2,1)}, bf16[2,4,4,16,128]{4,3,2,1,0:T(8,128)(2,1)S(1)}, u32[]{:S(2)}, u32[]{:S(2)}) collective-permute-start(bf16[2,4,4,16,128]{4,3,2,1,0:T(8,128)(2,1)} %get-tuple-element.78), channel_id=1, source_target_pairs={{0,1},{1,0},{2,3},{3,2},{4,5},{5,4},{6,7},{7,6},{8,9},{9,8},{10,11... | collective-permute-start | bytes 393224 | tf_op jit(solution)/shard_map/ppermute | solution.py:452
  10.0 7.9 %collective-permute-start = (bf16[2,4,4,16,128]{4,3,2,1,0:T(8,128)(2,1)}, bf16[2,4,4,16,128]{4,3,2,1,0:T(8,128)(2,1)S(1)}, u32[]{:S(2)}, u32[]{:S(2)}) collective-permute-start(bf16[2,4,4,16,128]{4,3,2,1,0:T(8,128)(2,1)} %get-tuple-element.64), channel_id=1, source_target_pairs={{0,13},{1,12},{2,15},{3,14},{4,9},{5,8},{6,11},{7,10},{8,5},{9,4},... | collective-permute-start | bytes 393224 | tf_op jit(solution)/shard_map/ppermute | solution.py:452
  10.1 13.7 %collective-permute-start.3 = (bf16[2,4,4,16,128]{4,3,2,1,0:T(8,128)(2,1)}, bf16[2,4,4,16,128]{4,3,2,1,0:T(8,128)(2,1)S(1)}, u32[]{:S(2)}, u32[]{:S(2)}) collective-permute-start(bf16[2,4,4,16,128]{4,3,2,1,0:T(8,128)(2,1)} %get-tuple-element.69), channel_id=1, source_target_pairs={{0,2},{1,3},{2,0},{3,1},{4,6},{5,7},{6,4},{7,5},{8,10},{9,11},{10,... | collective-permute-start | bytes 393224 | tf_op jit(solution)/shard_map/ppermute | solution.py:452
  11.4 13.8 %collective-permute-start.6 = (bf16[2,4,4,16,128]{4,3,2,1,0:T(8,128)(2,1)}, bf16[2,4,4,16,128]{4,3,2,1,0:T(8,128)(2,1)S(1)}, u32[]{:S(2)}, u32[]{:S(2)}) collective-permute-start(bf16[2,4,4,16,128]{4,3,2,1,0:T(8,128)(2,1)} %get-tuple-element.74), channel_id=1, source_target_pairs={{0,14},{1,15},{2,12},{3,13},{4,10},{5,11},{6,8},{7,9},{8,6},{9,7},... | collective-permute-start | bytes 393224 | tf_op jit(solution)/shard_map/ppermute | solution.py:452
  14.4 13.9 %collective-permute-start.12 = (bf16[2,4,4,16,128]{4,3,2,1,0:T(8,128)(2,1)}, bf16[2,4,4,16,128]{4,3,2,1,0:T(8,128)(2,1)S(1)}, u32[]{:S(2)}, u32[]{:S(2)}) collective-permute-start(bf16[2,4,4,16,128]{4,3,2,1,0:T(8,128)(2,1)} %get-tuple-element.82), channel_id=1, source_target_pairs={{0,15},{1,14},{2,13},{3,12},{4,11},{5,10},{6,9},{7,8},{8,7},{9,6},... | collective-permute-start | bytes 393224 | tf_op jit(solution)/shard_map/ppermute | solution.py:452
  16.3 14.0 %collective-permute-start.11 = (bf16[2,4,4,16,128]{4,3,2,1,0:T(8,128)(2,1)}, bf16[2,4,4,16,128]{4,3,2,1,0:T(8,128)(2,1)S(1)}, u32[]{:S(2)}, u32[]{:S(2)}) collective-permute-start(bf16[2,4,4,16,128]{4,3,2,1,0:T(8,128)(2,1)} %get-tuple-element.80), channel_id=1, source_target_pairs={{0,3},{1,2},{2,1},{3,0},{4,7},{5,6},{6,5},{7,4},{8,11},{9,10},{10,... | collective-permute-start | bytes 393224 | tf_op jit(solution)/shard_map/ppermute | solution.py:452
  17.9 12.9 %collective-permute-start.1 = (bf16[2,4,4,16,128]{4,3,2,1,0:T(8,128)(2,1)}, bf16[2,4,4,16,128]{4,3,2,1,0:T(8,128)(2,1)S(1)}, u32[]{:S(2)}, u32[]{:S(2)}) collective-permute-start(bf16[2,4,4,16,128]{4,3,2,1,0:T(8,128)(2,1)} %get-tuple-element.65), channel_id=1, source_target_pairs={{0,4},{1,5},{2,6},{3,7},{4,0},{5,1},{6,2},{7,3},{8,12},{9,13},{10,... | collective-permute-start | bytes 393224 | tf_op jit(solution)/shard_map/ppermute | solution.py:452
  23.8 11.6 %collective-permute-start.4 = (bf16[2,4,4,16,128]{4,3,2,1,0:T(8,128)(2,1)}, bf16[2,4,4,16,128]{4,3,2,1,0:T(8,128)(2,1)S(1)}, u32[]{:S(2)}, u32[]{:S(2)}) collective-permute-start(bf16[2,4,4,16,128]{4,3,2,1,0:T(8,128)(2,1)} %get-tuple-element.70), channel_id=1, source_target_pairs={{0,8},{1,9},{2,10},{3,11},{4,12},{5,13},{6,14},{7,15},{8,0},{9,1},... | collective-permute-start | bytes 393224 | tf_op jit(solution)/shard_map/ppermute | solution.py:452
  25.2 12.4 %collective-permute-start.7 = (bf16[2,4,4,16,128]{4,3,2,1,0:T(8,128)(2,1)}, bf16[2,4,4,16,128]{4,3,2,1,0:T(8,128)(2,1)S(1)}, u32[]{:S(2)}, u32[]{:S(2)}) collective-permute-start(bf16[2,4,4,16,128]{4,3,2,1,0:T(8,128)(2,1)} %get-tuple-element.75), channel_id=1, source_target_pairs={{0,5},{1,4},{2,7},{3,6},{4,1},{5,0},{6,3},{7,2},{8,13},{9,12},{10,... | collective-permute-start | bytes 393224 | tf_op jit(solution)/shard_map/ppermute | solution.py:452
  28.3 13.0 %collective-permute-start.14 = (bf16[2,4,4,16,128]{4,3,2,1,0:T(8,128)(2,1)}, bf16[2,4,4,16,128]{4,3,2,1,0:T(8,128)(2,1)S(1)}, u32[]{:S(2)}, u32[]{:S(2)}) collective-permute-start(bf16[2,4,4,16,128]{4,3,2,1,0:T(8,128)(2,1)} %get-tuple-element.86), channel_id=1, source_target_pairs={{0,6},{1,7},{2,4},{3,5},{4,2},{5,3},{6,0},{7,1},{8,14},{9,15},{10,... | collective-permute-start | bytes 393224 | tf_op jit(solution)/shard_map/ppermute | solution.py:452
  30.3 11.0 %collective-permute-start.13 = (bf16[2,4,4,16,128]{4,3,2,1,0:T(8,128)(2,1)}, bf16[2,4,4,16,128]{4,3,2,1,0:T(8,128)(2,1)S(1)}, u32[]{:S(2)}, u32[]{:S(2)}) collective-permute-start(bf16[2,4,4,16,128]{4,3,2,1,0:T(8,128)(2,1)} %get-tuple-element.84), channel_id=1, source_target_pairs={{0,9},{1,8},{2,11},{3,10},{4,13},{5,12},{6,15},{7,14},{8,1},{9,0},... | collective-permute-start | bytes 393224 | tf_op jit(solution)/shard_map/ppermute | solution.py:452
  30.9 16.5 %collective-permute-start.2 = (bf16[2,4,4,16,128]{4,3,2,1,0:T(8,128)(2,1)}, bf16[2,4,4,16,128]{4,3,2,1,0:T(8,128)(2,1)S(1)}, u32[]{:S(2)}, u32[]{:S(2)}) collective-permute-start(bf16[2,4,4,16,128]{4,3,2,1,0:T(8,128)(2,1)} %get-tuple-element.66), channel_id=1, source_target_pairs={{0,10},{1,11},{2,8},{3,9},{4,14},{5,15},{6,12},{7,13},{8,2},{9,3},... | collective-permute-start | bytes 393224 | tf_op jit(solution)/shard_map/ppermute | solution.py:452
  35.4 12.0 %collective-permute-start.5 = (bf16[2,4,4,16,128]{4,3,2,1,0:T(8,128)(2,1)}, bf16[2,4,4,16,128]{4,3,2,1,0:T(8,128)(2,1)S(1)}, u32[]{:S(2)}, u32[]{:S(2)}) collective-permute-start(bf16[2,4,4,16,128]{4,3,2,1,0:T(8,128)(2,1)} %get-tuple-element.71), channel_id=1, source_target_pairs={{0,7},{1,6},{2,5},{3,4},{4,3},{5,2},{6,1},{7,0},{8,15},{9,14},{10,... | collective-permute-start | bytes 393224 | tf_op jit(solution)/shard_map/ppermute | solution.py:452
  37.6 14.9 %collective-permute-start.8 = (bf16[2,4,4,16,128]{4,3,2,1,0:T(8,128)(2,1)}, bf16[2,4,4,16,128]{4,3,2,1,0:T(8,128)(2,1)S(1)}, u32[]{:S(2)}, u32[]{:S(2)}) collective-permute-start(bf16[2,4,4,16,128]{4,3,2,1,0:T(8,128)(2,1)} %get-tuple-element.76), channel_id=1, source_target_pairs={{0,11},{1,10},{2,9},{3,8},{4,15},{5,14},{6,13},{7,12},{8,3},{9,2},... | collective-permute-start | bytes 393224 | tf_op jit(solution)/shard_map/ppermute | solution.py:452
  55.4 8.3 %collective-permute-start.24 = (bf16[2,128,128]{2,1,0:T(8,128)(2,1)S(1)}, bf16[2,128,128]{2,1,0:T(8,128)(2,1)S(1)}, u32[]{:S(2)}, u32[]{:S(2)}) collective-permute-start(bf16[2,128,128]{2,1,0:T(8,128)(2,1)S(1)} %get-tuple-element.107), channel_id=1, source_target_pairs={{0,12},{1,13},{2,14},{3,15},{4,8},{5,9},{6,10},{7,11},{8,4},{9,5},... | collective-permute-start | bytes 196616 | tf_op jit(solution)/shard_map/ppermute | solution.py:452
  58.8 7.2 %collective-permute-start.15 = (bf16[2,128,128]{2,1,0:T(8,128)(2,1)S(1)}, bf16[2,128,128]{2,1,0:T(8,128)(2,1)S(1)}, u32[]{:S(2)}, u32[]{:S(2)}) collective-permute-start(bf16[2,128,128]{2,1,0:T(8,128)(2,1)S(1)} %get-tuple-element.92), channel_id=1, source_target_pairs={{0,13},{1,12},{2,15},{3,14},{4,9},{5,8},{6,11},{7,10},{8,5},{9,4},... | collective-permute-start | bytes 196616 | tf_op jit(solution)/shard_map/ppermute | solution.py:452
  59.3 6.7 %collective-permute-start.18 = (bf16[2,128,128]{2,1,0:T(8,128)(2,1)S(1)}, bf16[2,128,128]{2,1,0:T(8,128)(2,1)S(1)}, u32[]{:S(2)}, u32[]{:S(2)}) collective-permute-start(bf16[2,128,128]{2,1,0:T(8,128)(2,1)S(1)} %get-tuple-element.97), channel_id=1, source_target_pairs={{0,2},{1,3},{2,0},{3,1},{4,6},{5,7},{6,4},{7,5},{8,10},{9,11},{10,... | collective-permute-start | bytes 196616 | tf_op jit(solution)/shard_map/ppermute | solution.py:452
  59.5 9.2 %collective-permute-start.21 = (bf16[2,128,128]{2,1,0:T(8,128)(2,1)S(1)}, bf16[2,128,128]{2,1,0:T(8,128)(2,1)S(1)}, u32[]{:S(2)}, u32[]{:S(2)}) collective-permute-start(bf16[2,128,128]{2,1,0:T(8,128)(2,1)S(1)} %get-tuple-element.102), channel_id=1, source_target_pairs={{0,14},{1,15},{2,12},{3,13},{4,10},{5,11},{6,8},{7,9},{8,6},{9,7},... | collective-permute-start | bytes 196616 | tf_op jit(solution)/shard_map/ppermute | solution.py:452
  64.3 7.1 %collective-permute-start.27 = (bf16[2,128,128]{2,1,0:T(8,128)(2,1)S(1)}, bf16[2,128,128]{2,1,0:T(8,128)(2,1)S(1)}, u32[]{:S(2)}, u32[]{:S(2)}) collective-permute-start(bf16[2,128,128]{2,1,0:T(8,128)(2,1)S(1)} %get-tuple-element.112), channel_id=1, source_target_pairs={{0,15},{1,14},{2,13},{3,12},{4,11},{5,10},{6,9},{7,8},{8,7},{9,6},... | collective-permute-start | bytes 196616 | tf_op jit(solution)/shard_map/ppermute | solution.py:452
  66.0 7.7 %collective-permute-start.19 = (bf16[2,128,128]{2,1,0:T(8,128)(2,1)S(1)}, bf16[2,128,128]{2,1,0:T(8,128)(2,1)S(1)}, u32[]{:S(2)}, u32[]{:S(2)}) collective-permute-start(bf16[2,128,128]{2,1,0:T(8,128)(2,1)S(1)} %get-tuple-element.98), channel_id=1, source_target_pairs={{0,8},{1,9},{2,10},{3,11},{4,12},{5,13},{6,14},{7,15},{8,0},{9,1},... | collective-permute-start | bytes 196616 | tf_op jit(solution)/shard_map/ppermute | solution.py:452
  68.7 8.2 %collective-permute-start.22 = (bf16[2,128,128]{2,1,0:T(8,128)(2,1)S(1)}, bf16[2,128,128]{2,1,0:T(8,128)(2,1)S(1)}, u32[]{:S(2)}, u32[]{:S(2)}) collective-permute-start(bf16[2,128,128]{2,1,0:T(8,128)(2,1)S(1)} %get-tuple-element.103), channel_id=1, source_target_pairs={{0,5},{1,4},{2,7},{3,6},{4,1},{5,0},{6,3},{7,2},{8,13},{9,12},{10,... | collective-permute-start | bytes 196616 | tf_op jit(solution)/shard_map/ppermute | solution.py:452
  69.5 7.8 %collective-permute-start.28 = (bf16[2,128,128]{2,1,0:T(8,128)(2,1)S(1)}, bf16[2,128,128]{2,1,0:T(8,128)(2,1)S(1)}, u32[]{:S(2)}, u32[]{:S(2)}) collective-permute-start(bf16[2,128,128]{2,1,0:T(8,128)(2,1)S(1)} %get-tuple-element.114), channel_id=1, source_target_pairs={{0,9},{1,8},{2,11},{3,10},{4,13},{5,12},{6,15},{7,14},{8,1},{9,0},... | collective-permute-start | bytes 196616 | tf_op jit(solution)/shard_map/ppermute | solution.py:452
  71.4 8.7 %collective-permute-start.17 = (bf16[2,128,128]{2,1,0:T(8,128)(2,1)S(1)}, bf16[2,128,128]{2,1,0:T(8,128)(2,1)S(1)}, u32[]{:S(2)}, u32[]{:S(2)}) collective-permute-start(bf16[2,128,128]{2,1,0:T(8,128)(2,1)S(1)} %get-tuple-element.94), channel_id=1, source_target_pairs={{0,10},{1,11},{2,8},{3,9},{4,14},{5,15},{6,12},{7,13},{8,2},{9,3},... | collective-permute-start | bytes 196616 | tf_op jit(solution)/shard_map/ppermute | solution.py:452
  (9 other events, 102.7 us)

commit v8 on v7

--- a/solution.py
+++ b/solution.py
@@ -12,8 +12,9 @@
 
 LAGS = 2048
 MIB = 1 << 20
-ORDER = (12, 1, 13, 2, 14, 3, 15, 4, 8, 5, 9, 6, 10, 7, 11)
+ORDER = (12, 1, 13, 2, 14, 3, 15, 4, 9, 5, 10, 6, 11, 7, 8)
 FIRST = 2
+BACK = (12, 4, 13, 5, 14, 6, 15, 7, 8, 1, 9, 2, 10, 3, 11)
 LATE = 3
 
 
@@ -263,7 +264,7 @@
         lax.fori_loop(0, rounds, late_pairs, 0)
     else:
         lax.fori_loop(0, rounds * pairs, any_pair, 0)
-    for share_ref, away in zip(share_refs, (0,) + ORDER):
+    for share_ref, away in zip(share_refs, (0,) + BACK):
         share_ref[...] = out_ref[me ^ away]
     if late:
         fetch.wait()
@@ -487,7 +488,7 @@
         shares = cross(
             blocks[-1 - LATE : -1], late, inverse, pair_table, devices, (), tuple(started)
         )[2:]
-        sources = (0,) + ORDER
+        sources = (0,) + BACK
         received = swap(shares, sources, devices)
     else:
         stacked, _ = cross(blocks, sources, inverse, pair_table, devices)

time: 84.4 us -> 83.6 us (level)
  waiting for transfers between devices: 13.3 us -> 10.7 us
  starting transfers between devices: 52.4 us -> 54.8 us
    ppermute x30, waiting for transfers between devices: 13.3 us -> 10.7 us  [swap(): share = lax.ppermute(share, 'sta', [(n, n ^ away) for n in range(devices)])]
    ppermute x30, starting transfers between devices: 52.4 us -> 54.8 us  [swap(): share = lax.ppermute(share, 'sta', [(n, n ^ away) for n in range(devices)])]
  transfers between devices with their start and end apart: 30 -> 30, of which waited for: 7 -> 10; matrix products, arithmetic and copies ran while one was open for 1% -> 1% of each run, Pallas kernels for 13% -> 13%
where the time goes in v8:
time: 83.6 us; the launch traced here: 84 us
  starting transfers between devices  54.8 us (66%)
  Pallas kernels  16.8 us (20%)
  waiting for transfers between devices  10.7 us (13%)
  local copies, waits for them, and re-layouts  1.27 us (2%)
    ppermute x30, starting transfers between devices, swap(): share = lax.ppermute(share, 'sta', [(n, n ^ away) for n in range(devices)])  54.8 us
    ppermute x30, waiting for transfers between devices, swap(): share = lax.ppermute(share, 'sta', [(n, n ^ away) for n in range(devices)])  10.7 us
    pallas_call x2, Pallas kernels, cross(): pl.pallas_call(functools.partial(cross_kernel, sources, late, len(started...  8.07 us
    pallas_call x2, Pallas kernels, pieces(): pl.pallas_call(functools.partial(piece_kernel, aways), in_specs=[pl.Block...  4.82 us
    pallas_call x2, Pallas kernels, lags(): pl.pallas_call(body, in_specs=[vmem] * (len(stacked) + 1 + len(started)),...  3.87 us
  transfers between devices with their start and end apart: 30, of which 10 were waited for; matrix products, arithmetic and copies ran while one was open for 1% of the time, Pallas kernels for 13%

profile of v8, /device:TPU:1, one launch (start us, length us, event | category | flops | bytes accessed | tf_op | source)
XLA Modules:
  0.0 84.0 jit_solution(12247135333739246828)
XLA Ops:
  0.0 1.8 %pack_first.1 = (bf16[2,4,4,16,128]{4,3,2,1,0:T(8,128)(2,1)}, bf16[2,4,4,16,128]{4,3,2,1,0:T(8,128)(2,1)}) custom-call(s32[16]{0:T(128)} %counts_ref.3, s32[4,16,16]{2,1,0:T(8,128)} %masks_ref.3, bf16[2,4,16,4,2048]{4,3,2,1,0:T(4,128)(2,1)} %spectra_ref.3), custom_call_target="tpu_custom_call" | custom-call | tf_op jit(solution)/shard_map/pack_first/pallas_call | solution.py:124
  1.8 4.2 %collective-permute-start.9 = (bf16[2,4,4,16,128]{4,3,2,1,0:T(8,128)(2,1)}, bf16[2,4,4,16,128]{4,3,2,1,0:T(8,128)(2,1)S(1)}, u32[]{:S(2)}, u32[]{:S(2)}) collective-permute-start(bf16[2,4,4,16,128]{4,3,2,1,0:T(8,128)(2,1)} %get-tuple-element.77), channel_id=1, source_target_pairs={{0,12},{1,13},{2,14},{3,15},{4,8},{5,9},{6,10},{7,11},{8,4},{9,5},... | collective-permute-start | bytes 393224 | tf_op jit(solution)/shard_map/ppermute | solution.py:453
  6.9 3.1 %pack_rest.1 = (bf16[2,4,4,16,128]{4,3,2,1,0:T(8,128)(2,1)}, bf16[2,4,4,16,128]{4,3,2,1,0:T(8,128)(2,1)}, bf16[2,4,4,16,128]{4,3,2,1,0:T(8,128)(2,1)}, bf16[2,4,...) custom-call(s32[16]{0:T(128)} %counts_ref.3, ...), custom_call_target="tpu_custom_call" | custom-call | tf_op jit(solution)/shard_map/pack_rest/pallas_call | solution.py:124
  11.4 3.0 %collective-permute-start.6 = (bf16[2,4,4,16,128]{4,3,2,1,0:T(8,128)(2,1)}, bf16[2,4,4,16,128]{4,3,2,1,0:T(8,128)(2,1)S(1)}, u32[]{:S(2)}, u32[]{:S(2)}) collective-permute-start(bf16[2,4,4,16,128]{4,3,2,1,0:T(8,128)(2,1)} %get-tuple-element.74), channel_id=1, source_target_pairs={{0,14},{1,15},{2,12},{3,13},{4,10},{5,11},{6,8},{7,9},{8,6},{9,7},... | collective-permute-start | bytes 393224 | tf_op jit(solution)/shard_map/ppermute | solution.py:453
  14.4 1.9 %collective-permute-start.12 = (bf16[2,4,4,16,128]{4,3,2,1,0:T(8,128)(2,1)}, bf16[2,4,4,16,128]{4,3,2,1,0:T(8,128)(2,1)S(1)}, u32[]{:S(2)}, u32[]{:S(2)}) collective-permute-start(bf16[2,4,4,16,128]{4,3,2,1,0:T(8,128)(2,1)} %get-tuple-element.82), channel_id=1, source_target_pairs={{0,15},{1,14},{2,13},{3,12},{4,11},{5,10},{6,9},{7,8},{8,7},{9,6},... | collective-permute-start | bytes 393224 | tf_op jit(solution)/shard_map/ppermute | solution.py:453
  17.9 5.8 %collective-permute-start.1 = (bf16[2,4,4,16,128]{4,3,2,1,0:T(8,128)(2,1)}, bf16[2,4,4,16,128]{4,3,2,1,0:T(8,128)(2,1)S(1)}, u32[]{:S(2)}, u32[]{:S(2)}) collective-permute-start(bf16[2,4,4,16,128]{4,3,2,1,0:T(8,128)(2,1)} %get-tuple-element.65), channel_id=1, source_target_pairs={{0,4},{1,5},{2,6},{3,7},{4,0},{5,1},{6,2},{7,3},{8,12},{9,13},{10,... | collective-permute-start | bytes 393224 | tf_op jit(solution)/shard_map/ppermute | solution.py:453
  24.3 3.8 %collective-permute-start.7 = (bf16[2,4,4,16,128]{4,3,2,1,0:T(8,128)(2,1)}, bf16[2,4,4,16,128]{4,3,2,1,0:T(8,128)(2,1)S(1)}, u32[]{:S(2)}, u32[]{:S(2)}) collective-permute-start(bf16[2,4,4,16,128]{4,3,2,1,0:T(8,128)(2,1)} %get-tuple-element.75), channel_id=1, source_target_pairs={{0,5},{1,4},{2,7},{3,6},{4,1},{5,0},{6,3},{7,2},{8,13},{9,12},{10,... | collective-permute-start | bytes 393224 | tf_op jit(solution)/shard_map/ppermute | solution.py:453
  28.3 2.0 %collective-permute-start.14 = (bf16[2,4,4,16,128]{4,3,2,1,0:T(8,128)(2,1)}, bf16[2,4,4,16,128]{4,3,2,1,0:T(8,128)(2,1)S(1)}, u32[]{:S(2)}, u32[]{:S(2)}) collective-permute-start(bf16[2,4,4,16,128]{4,3,2,1,0:T(8,128)(2,1)} %get-tuple-element.86), channel_id=1, source_target_pairs={{0,6},{1,7},{2,4},{3,5},{4,2},{5,3},{6,0},{7,1},{8,14},{9,15},{10,... | collective-permute-start | bytes 393224 | tf_op jit(solution)/shard_map/ppermute | solution.py:453
  30.3 4.2 %collective-permute-start.13 = (bf16[2,4,4,16,128]{4,3,2,1,0:T(8,128)(2,1)}, bf16[2,4,4,16,128]{4,3,2,1,0:T(8,128)(2,1)S(1)}, u32[]{:S(2)}, u32[]{:S(2)}) collective-permute-start(bf16[2,4,4,16,128]{4,3,2,1,0:T(8,128)(2,1)} %get-tuple-element.84), channel_id=1, source_target_pairs={{0,10},{1,11},{2,8},{3,9},{4,14},{5,15},{6,12},{7,13},{8,2},{9,3},... | collective-permute-start | bytes 393224 | tf_op jit(solution)/shard_map/ppermute | solution.py:453
  34.7 2.4 %collective-permute-start.5 = (bf16[2,4,4,16,128]{4,3,2,1,0:T(8,128)(2,1)}, bf16[2,4,4,16,128]{4,3,2,1,0:T(8,128)(2,1)S(1)}, u32[]{:S(2)}, u32[]{:S(2)}) collective-permute-start(bf16[2,4,4,16,128]{4,3,2,1,0:T(8,128)(2,1)} %get-tuple-element.71), channel_id=1, source_target_pairs={{0,7},{1,6},{2,5},{3,4},{4,3},{5,2},{6,1},{7,0},{8,15},{9,14},{10,... | collective-permute-start | bytes 393224 | tf_op jit(solution)/shard_map/ppermute | solution.py:453
  37.2 3.3 %collective-permute-start.8 = (bf16[2,4,4,16,128]{4,3,2,1,0:T(8,128)(2,1)}, bf16[2,4,4,16,128]{4,3,2,1,0:T(8,128)(2,1)S(1)}, u32[]{:S(2)}, u32[]{:S(2)}) collective-permute-start(bf16[2,4,4,16,128]{4,3,2,1,0:T(8,128)(2,1)} %get-tuple-element.76), channel_id=1, source_target_pairs={{0,8},{1,9},{2,10},{3,11},{4,12},{5,13},{6,14},{7,15},{8,0},{9,1},... | collective-permute-start | bytes 393224 | tf_op jit(solution)/shard_map/ppermute | solution.py:453
  42.7 5.2 %cross.1 = (bf16[16,2,128,128]{3,2,1,0:T(8,128)(2,1)S(1)}, f32[16,2,4,4,16,128]{5,4,3,2,1,0:T(8,128)S(1)}, bf16[4,2,2048,256]{3,2,1,0:T(8,128)(2,1)S(1)}) custom-call(s32[128]{0:T(128)S(1)} %pad_add_fusion.pairs_ref, f32[1024]{0:T(1024)S(1)} %reshape.17.inverse_ref, bf16[2,4,4,16,128]{4,3,2,1,0:T(8,128)(2,1)S(1)} %collective-permute-done.9.refs_0_, ...), custom_call_target="tpu_custom_call" | custom-call | flops 54525952 | bytes 4194304 | tf_op jit(solution)/shard_map/cross/pallas_call | solution.py:285
  47.9 3.3 %collective-permute-done.8.refs_2_ = bf16[2,4,4,16,128]{4,3,2,1,0:T(8,128)(2,1)S(1)} collective-permute-done((bf16[2,4,4,16,128]{4,3,2,1,0:T(8,128)(2,1)}, bf16[2,4,4,16,128]{4,3,2,1,0:T(8,128)(2,1)S(1)}, u32[]{:S(2)}, u32[]{:S(2)}) %collective-permute-start.8) | collective-permute-done | bytes 131104 | tf_op jit(solution)/shard_map/ppermute | solution.py:453
  51.2 2.9 %cross_rest.1 = (bf16[16,2,128,128]{3,2,1,0:T(8,128)(2,1)S(1)}, f32[16,2,4,4,16,128]{5,4,3,2,1,0:T(8,128)S(1)}, bf16[2,128,128]{2,1,0:T(8,128)(2,1)S(1)}, bf16[2...) custom-call(s32[128]{0:T(128)S(1)} %pad_add_fusion.pairs_ref, ...), custom_call_target="tpu_custom_call", output_to_operand_aliasing={{0}: (5, {}), {1}: (6, {})} | custom-call | flops 12582912 | bytes 4194304 | tf_op jit(solution)/shard_map/cross_rest/pallas_call | solution.py:285
  54.1 3.8 %collective-permute-start.24 = (bf16[2,128,128]{2,1,0:T(8,128)(2,1)S(1)}, bf16[2,128,128]{2,1,0:T(8,128)(2,1)S(1)}, u32[]{:S(2)}, u32[]{:S(2)}) collective-permute-start(bf16[2,128,128]{2,1,0:T(8,128)(2,1)S(1)} %get-tuple-element.107), channel_id=1, source_target_pairs={{0,12},{1,13},{2,14},{3,15},{4,8},{5,9},{6,10},{7,11},{8,4},{9,5},... | collective-permute-start | bytes 196616 | tf_op jit(solution)/shard_map/ppermute | solution.py:453
  57.9 1.8 %collective-permute-start.15 = (bf16[2,128,128]{2,1,0:T(8,128)(2,1)S(1)}, bf16[2,128,128]{2,1,0:T(8,128)(2,1)S(1)}, u32[]{:S(2)}, u32[]{:S(2)}) collective-permute-start(bf16[2,128,128]{2,1,0:T(8,128)(2,1)S(1)} %get-tuple-element.92), channel_id=1, source_target_pairs={{0,13},{1,12},{2,15},{3,14},{4,9},{5,8},{6,11},{7,10},{8,5},{9,4},... | collective-permute-start | bytes 196616 | tf_op jit(solution)/shard_map/ppermute | solution.py:453
  59.7 2.9 %collective-permute-start.21 = (bf16[2,128,128]{2,1,0:T(8,128)(2,1)S(1)}, bf16[2,128,128]{2,1,0:T(8,128)(2,1)S(1)}, u32[]{:S(2)}, u32[]{:S(2)}) collective-permute-start(bf16[2,128,128]{2,1,0:T(8,128)(2,1)S(1)} %get-tuple-element.102), channel_id=1, source_target_pairs={{0,14},{1,15},{2,12},{3,13},{4,10},{5,11},{6,8},{7,9},{8,6},{9,7},... | collective-permute-start | bytes 196616 | tf_op jit(solution)/shard_map/ppermute | solution.py:453
  63.1 2.7 %collective-permute-start.27 = (bf16[2,128,128]{2,1,0:T(8,128)(2,1)S(1)}, bf16[2,128,128]{2,1,0:T(8,128)(2,1)S(1)}, u32[]{:S(2)}, u32[]{:S(2)}) collective-permute-start(bf16[2,128,128]{2,1,0:T(8,128)(2,1)S(1)} %get-tuple-element.112), channel_id=1, source_target_pairs={{0,15},{1,14},{2,13},{3,12},{4,11},{5,10},{6,9},{7,8},{8,7},{9,6},... | collective-permute-start | bytes 196616 | tf_op jit(solution)/shard_map/ppermute | solution.py:453
  67.8 1.5 %collective-permute-start.22 = (bf16[2,128,128]{2,1,0:T(8,128)(2,1)S(1)}, bf16[2,128,128]{2,1,0:T(8,128)(2,1)S(1)}, u32[]{:S(2)}, u32[]{:S(2)}) collective-permute-start(bf16[2,128,128]{2,1,0:T(8,128)(2,1)S(1)} %get-tuple-element.103), channel_id=1, source_target_pairs={{0,1},{1,0},{2,3},{3,2},{4,5},{5,4},{6,7},{7,6},{8,9},{9,8},{10,11... | collective-permute-start | bytes 196616 | tf_op jit(solution)/shard_map/ppermute | solution.py:453
  72.2 2.3 %collective-permute-start.17 = (bf16[2,128,128]{2,1,0:T(8,128)(2,1)S(1)}, bf16[2,128,128]{2,1,0:T(8,128)(2,1)S(1)}, u32[]{:S(2)}, u32[]{:S(2)}) collective-permute-start(bf16[2,128,128]{2,1,0:T(8,128)(2,1)S(1)} %get-tuple-element.94), channel_id=1, source_target_pairs={{0,10},{1,11},{2,8},{3,9},{4,14},{5,15},{6,12},{7,13},{8,2},{9,3},... | collective-permute-start | bytes 196616 | tf_op jit(solution)/shard_map/ppermute | solution.py:453
  74.5 1.9 %collective-permute-start.20 = (bf16[2,128,128]{2,1,0:T(8,128)(2,1)S(1)}, bf16[2,128,128]{2,1,0:T(8,128)(2,1)S(1)}, u32[]{:S(2)}, u32[]{:S(2)}) collective-permute-start(bf16[2,128,128]{2,1,0:T(8,128)(2,1)S(1)} %get-tuple-element.99), channel_id=1, source_target_pairs={{0,3},{1,2},{2,1},{3,0},{4,7},{5,6},{6,5},{7,4},{8,11},{9,10},{10,... | collective-permute-start | bytes 196616 | tf_op jit(solution)/shard_map/ppermute | solution.py:453
  77.1 2.4 %lags_first.1 = (f32[4,2,128,256]{3,2,1,0:T(8,128)S(1)}, f32[128,128]{1,0:T(8,128)S(1)}) custom-call(bf16[2,128,128]{2,1,0:T(8,128)(2,1)S(1)} %get-tuple-element.106.refs_0_, bf16[2,128,128]{2,1,0:T(8,128)(2,1)S(1)} %collective-permute-done.24.refs_1_, bf16[2,128,128]{2,1,0:T(8,128)(2,1)S(1)} %collective-permute-done.25.refs_2_, ...), custom_call_target="tpu_custom_call" | custom-call | flops 1073741824 | bytes 4194304 | tf_op jit(solution)/shard_map/lags_first/pallas_call | solution.py:432
  80.2 2.3 %collective-permute-done.23.refs_2_ = bf16[2,128,128]{2,1,0:T(8,128)(2,1)S(1)} collective-permute-done((bf16[2,128,128]{2,1,0:T(8,128)(2,1)S(1)}, bf16[2,128,128]{2,1,0:T(8,128)(2,1)S(1)}, u32[]{:S(2)}, u32[]{:S(2)}) %collective-permute-start.23) | collective-permute-done | bytes 65568 | tf_op jit(solution)/shard_map/ppermute | solution.py:453
  82.5 1.5 %lags.1 = f32[128,2048]{1,0:T(8,128)} custom-call(bf16[2,128,128]{2,1,0:T(8,128)(2,1)S(1)} %collective-permute-done.17.refs_0_, bf16[2,128,128]{2,1,0:T(8,128)(2,1)S(1)} %collective-permute-done.20.refs_1_, bf16[2,128,128]{2,1,0:T(8,128)(2,1)S(1)} %collective-permute-done.23.refs_2_, bf16[4,2,2048,256]{3,2,1,0:T(8,128)(2,1)S(1)} %get-tuple-element.105.refs_13_.refs_3_, ...), custom_call_target="tpu_custom_call" | custom-call | flops 1073741824 | bytes 4194304 | tf_op jit(solution)/shard_map/lags/pallas_call | solution.py:432
  (55 shorter events, 14.1 us)
Async XLA Ops:
  1.8 12.6 %collective-permute-start.9 = (bf16[2,4,4,16,128]{4,3,2,1,0:T(8,128)(2,1)}, bf16[2,4,4,16,128]{4,3,2,1,0:T(8,128)(2,1)S(1)}, u32[]{:S(2)}, u32[]{:S(2)}) collective-permute-start(bf16[2,4,4,16,128]{4,3,2,1,0:T(8,128)(2,1)} %get-tuple-element.77), channel_id=1, source_target_pairs={{0,12},{1,13},{2,14},{3,15},{4,8},{5,9},{6,10},{7,11},{8,4},{9,5},... | collective-permute-start | bytes 393224 | tf_op jit(solution)/shard_map/ppermute | solution.py:453
  6.0 8.4 %collective-permute-start.10 = (bf16[2,4,4,16,128]{4,3,2,1,0:T(8,128)(2,1)}, bf16[2,4,4,16,128]{4,3,2,1,0:T(8,128)(2,1)S(1)}, u32[]{:S(2)}, u32[]{:S(2)}) collective-permute-start(bf16[2,4,4,16,128]{4,3,2,1,0:T(8,128)(2,1)} %get-tuple-element.78), channel_id=1, source_target_pairs={{0,1},{1,0},{2,3},{3,2},{4,5},{5,4},{6,7},{7,6},{8,9},{9,8},{10,11... | collective-permute-start | bytes 393224 | tf_op jit(solution)/shard_map/ppermute | solution.py:453
  10.0 7.9 %collective-permute-start = (bf16[2,4,4,16,128]{4,3,2,1,0:T(8,128)(2,1)}, bf16[2,4,4,16,128]{4,3,2,1,0:T(8,128)(2,1)S(1)}, u32[]{:S(2)}, u32[]{:S(2)}) collective-permute-start(bf16[2,4,4,16,128]{4,3,2,1,0:T(8,128)(2,1)} %get-tuple-element.64), channel_id=1, source_target_pairs={{0,13},{1,12},{2,15},{3,14},{4,9},{5,8},{6,11},{7,10},{8,5},{9,4},... | collective-permute-start | bytes 393224 | tf_op jit(solution)/shard_map/ppermute | solution.py:453
  10.1 13.7 %collective-permute-start.3 = (bf16[2,4,4,16,128]{4,3,2,1,0:T(8,128)(2,1)}, bf16[2,4,4,16,128]{4,3,2,1,0:T(8,128)(2,1)S(1)}, u32[]{:S(2)}, u32[]{:S(2)}) collective-permute-start(bf16[2,4,4,16,128]{4,3,2,1,0:T(8,128)(2,1)} %get-tuple-element.69), channel_id=1, source_target_pairs={{0,2},{1,3},{2,0},{3,1},{4,6},{5,7},{6,4},{7,5},{8,10},{9,11},{10,... | collective-permute-start | bytes 393224 | tf_op jit(solution)/shard_map/ppermute | solution.py:453
  11.4 12.9 %collective-permute-start.6 = (bf16[2,4,4,16,128]{4,3,2,1,0:T(8,128)(2,1)}, bf16[2,4,4,16,128]{4,3,2,1,0:T(8,128)(2,1)S(1)}, u32[]{:S(2)}, u32[]{:S(2)}) collective-permute-start(bf16[2,4,4,16,128]{4,3,2,1,0:T(8,128)(2,1)} %get-tuple-element.74), channel_id=1, source_target_pairs={{0,14},{1,15},{2,12},{3,13},{4,10},{5,11},{6,8},{7,9},{8,6},{9,7},... | collective-permute-start | bytes 393224 | tf_op jit(solution)/shard_map/ppermute | solution.py:453
  14.4 13.9 %collective-permute-start.12 = (bf16[2,4,4,16,128]{4,3,2,1,0:T(8,128)(2,1)}, bf16[2,4,4,16,128]{4,3,2,1,0:T(8,128)(2,1)S(1)}, u32[]{:S(2)}, u32[]{:S(2)}) collective-permute-start(bf16[2,4,4,16,128]{4,3,2,1,0:T(8,128)(2,1)} %get-tuple-element.82), channel_id=1, source_target_pairs={{0,15},{1,14},{2,13},{3,12},{4,11},{5,10},{6,9},{7,8},{8,7},{9,6},... | collective-permute-start | bytes 393224 | tf_op jit(solution)/shard_map/ppermute | solution.py:453
  16.3 14.0 %collective-permute-start.11 = (bf16[2,4,4,16,128]{4,3,2,1,0:T(8,128)(2,1)}, bf16[2,4,4,16,128]{4,3,2,1,0:T(8,128)(2,1)S(1)}, u32[]{:S(2)}, u32[]{:S(2)}) collective-permute-start(bf16[2,4,4,16,128]{4,3,2,1,0:T(8,128)(2,1)} %get-tuple-element.80), channel_id=1, source_target_pairs={{0,3},{1,2},{2,1},{3,0},{4,7},{5,6},{6,5},{7,4},{8,11},{9,10},{10,... | collective-permute-start | bytes 393224 | tf_op jit(solution)/shard_map/ppermute | solution.py:453
  17.9 16.5 %collective-permute-start.1 = (bf16[2,4,4,16,128]{4,3,2,1,0:T(8,128)(2,1)}, bf16[2,4,4,16,128]{4,3,2,1,0:T(8,128)(2,1)S(1)}, u32[]{:S(2)}, u32[]{:S(2)}) collective-permute-start(bf16[2,4,4,16,128]{4,3,2,1,0:T(8,128)(2,1)} %get-tuple-element.65), channel_id=1, source_target_pairs={{0,4},{1,5},{2,6},{3,7},{4,0},{5,1},{6,2},{7,3},{8,12},{9,13},{10,... | collective-permute-start | bytes 393224 | tf_op jit(solution)/shard_map/ppermute | solution.py:453
  23.8 11.0 %collective-permute-start.4 = (bf16[2,4,4,16,128]{4,3,2,1,0:T(8,128)(2,1)}, bf16[2,4,4,16,128]{4,3,2,1,0:T(8,128)(2,1)S(1)}, u32[]{:S(2)}, u32[]{:S(2)}) collective-permute-start(bf16[2,4,4,16,128]{4,3,2,1,0:T(8,128)(2,1)} %get-tuple-element.70), channel_id=1, source_target_pairs={{0,9},{1,8},{2,11},{3,10},{4,13},{5,12},{6,15},{7,14},{8,1},{9,0},... | collective-permute-start | bytes 393224 | tf_op jit(solution)/shard_map/ppermute | solution.py:453
  24.3 12.9 %collective-permute-start.7 = (bf16[2,4,4,16,128]{4,3,2,1,0:T(8,128)(2,1)}, bf16[2,4,4,16,128]{4,3,2,1,0:T(8,128)(2,1)S(1)}, u32[]{:S(2)}, u32[]{:S(2)}) collective-permute-start(bf16[2,4,4,16,128]{4,3,2,1,0:T(8,128)(2,1)} %get-tuple-element.75), channel_id=1, source_target_pairs={{0,5},{1,4},{2,7},{3,6},{4,1},{5,0},{6,3},{7,2},{8,13},{9,12},{10,... | collective-permute-start | bytes 393224 | tf_op jit(solution)/shard_map/ppermute | solution.py:453
  28.3 13.5 %collective-permute-start.14 = (bf16[2,4,4,16,128]{4,3,2,1,0:T(8,128)(2,1)}, bf16[2,4,4,16,128]{4,3,2,1,0:T(8,128)(2,1)S(1)}, u32[]{:S(2)}, u32[]{:S(2)}) collective-permute-start(bf16[2,4,4,16,128]{4,3,2,1,0:T(8,128)(2,1)} %get-tuple-element.86), channel_id=1, source_target_pairs={{0,6},{1,7},{2,4},{3,5},{4,2},{5,3},{6,0},{7,1},{8,14},{9,15},{10,... | collective-permute-start | bytes 393224 | tf_op jit(solution)/shard_map/ppermute | solution.py:453
  30.3 11.5 %collective-permute-start.13 = (bf16[2,4,4,16,128]{4,3,2,1,0:T(8,128)(2,1)}, bf16[2,4,4,16,128]{4,3,2,1,0:T(8,128)(2,1)S(1)}, u32[]{:S(2)}, u32[]{:S(2)}) collective-permute-start(bf16[2,4,4,16,128]{4,3,2,1,0:T(8,128)(2,1)} %get-tuple-element.84), channel_id=1, source_target_pairs={{0,10},{1,11},{2,8},{3,9},{4,14},{5,15},{6,12},{7,13},{8,2},{9,3},... | collective-permute-start | bytes 393224 | tf_op jit(solution)/shard_map/ppermute | solution.py:453
  34.5 13.5 %collective-permute-start.2 = (bf16[2,4,4,16,128]{4,3,2,1,0:T(8,128)(2,1)}, bf16[2,4,4,16,128]{4,3,2,1,0:T(8,128)(2,1)S(1)}, u32[]{:S(2)}, u32[]{:S(2)}) collective-permute-start(bf16[2,4,4,16,128]{4,3,2,1,0:T(8,128)(2,1)} %get-tuple-element.66), channel_id=1, source_target_pairs={{0,11},{1,10},{2,9},{3,8},{4,15},{5,14},{6,13},{7,12},{8,3},{9,2},... | collective-permute-start | bytes 393224 | tf_op jit(solution)/shard_map/ppermute | solution.py:453
  34.7 13.2 %collective-permute-start.5 = (bf16[2,4,4,16,128]{4,3,2,1,0:T(8,128)(2,1)}, bf16[2,4,4,16,128]{4,3,2,1,0:T(8,128)(2,1)S(1)}, u32[]{:S(2)}, u32[]{:S(2)}) collective-permute-start(bf16[2,4,4,16,128]{4,3,2,1,0:T(8,128)(2,1)} %get-tuple-element.71), channel_id=1, source_target_pairs={{0,7},{1,6},{2,5},{3,4},{4,3},{5,2},{6,1},{7,0},{8,15},{9,14},{10,... | collective-permute-start | bytes 393224 | tf_op jit(solution)/shard_map/ppermute | solution.py:453
  37.2 14.0 %collective-permute-start.8 = (bf16[2,4,4,16,128]{4,3,2,1,0:T(8,128)(2,1)}, bf16[2,4,4,16,128]{4,3,2,1,0:T(8,128)(2,1)S(1)}, u32[]{:S(2)}, u32[]{:S(2)}) collective-permute-start(bf16[2,4,4,16,128]{4,3,2,1,0:T(8,128)(2,1)} %get-tuple-element.76), channel_id=1, source_target_pairs={{0,8},{1,9},{2,10},{3,11},{4,12},{5,13},{6,14},{7,15},{8,0},{9,1},... | collective-permute-start | bytes 393224 | tf_op jit(solution)/shard_map/ppermute | solution.py:453
  54.1 8.5 %collective-permute-start.24 = (bf16[2,128,128]{2,1,0:T(8,128)(2,1)S(1)}, bf16[2,128,128]{2,1,0:T(8,128)(2,1)S(1)}, u32[]{:S(2)}, u32[]{:S(2)}) collective-permute-start(bf16[2,128,128]{2,1,0:T(8,128)(2,1)S(1)} %get-tuple-element.107), channel_id=1, source_target_pairs={{0,12},{1,13},{2,14},{3,15},{4,8},{5,9},{6,10},{7,11},{8,4},{9,5},... | collective-permute-start | bytes 196616 | tf_op jit(solution)/shard_map/ppermute | solution.py:453
  57.9 7.8 %collective-permute-start.15 = (bf16[2,128,128]{2,1,0:T(8,128)(2,1)S(1)}, bf16[2,128,128]{2,1,0:T(8,128)(2,1)S(1)}, u32[]{:S(2)}, u32[]{:S(2)}) collective-permute-start(bf16[2,128,128]{2,1,0:T(8,128)(2,1)S(1)} %get-tuple-element.92), channel_id=1, source_target_pairs={{0,13},{1,12},{2,15},{3,14},{4,9},{5,8},{6,11},{7,10},{8,5},{9,4},... | collective-permute-start | bytes 196616 | tf_op jit(solution)/shard_map/ppermute | solution.py:453
  59.7 7.0 %collective-permute-start.18 = (bf16[2,128,128]{2,1,0:T(8,128)(2,1)S(1)}, bf16[2,128,128]{2,1,0:T(8,128)(2,1)S(1)}, u32[]{:S(2)}, u32[]{:S(2)}) collective-permute-start(bf16[2,128,128]{2,1,0:T(8,128)(2,1)S(1)} %get-tuple-element.97), channel_id=1, source_target_pairs={{0,5},{1,4},{2,7},{3,6},{4,1},{5,0},{6,3},{7,2},{8,13},{9,12},{10,... | collective-permute-start | bytes 196616 | tf_op jit(solution)/shard_map/ppermute | solution.py:453
  59.7 8.1 %collective-permute-start.21 = (bf16[2,128,128]{2,1,0:T(8,128)(2,1)S(1)}, bf16[2,128,128]{2,1,0:T(8,128)(2,1)S(1)}, u32[]{:S(2)}, u32[]{:S(2)}) collective-permute-start(bf16[2,128,128]{2,1,0:T(8,128)(2,1)S(1)} %get-tuple-element.102), channel_id=1, source_target_pairs={{0,14},{1,15},{2,12},{3,13},{4,10},{5,11},{6,8},{7,9},{8,6},{9,7},... | collective-permute-start | bytes 196616 | tf_op jit(solution)/shard_map/ppermute | solution.py:453
  66.7 7.8 %collective-permute-start.19 = (bf16[2,128,128]{2,1,0:T(8,128)(2,1)S(1)}, bf16[2,128,128]{2,1,0:T(8,128)(2,1)S(1)}, u32[]{:S(2)}, u32[]{:S(2)}) collective-permute-start(bf16[2,128,128]{2,1,0:T(8,128)(2,1)S(1)} %get-tuple-element.98), channel_id=1, source_target_pairs={{0,8},{1,9},{2,10},{3,11},{4,12},{5,13},{6,14},{7,15},{8,0},{9,1},... | collective-permute-start | bytes 196616 | tf_op jit(solution)/shard_map/ppermute | solution.py:453
  67.8 8.6 %collective-permute-start.22 = (bf16[2,128,128]{2,1,0:T(8,128)(2,1)S(1)}, bf16[2,128,128]{2,1,0:T(8,128)(2,1)S(1)}, u32[]{:S(2)}, u32[]{:S(2)}) collective-permute-start(bf16[2,128,128]{2,1,0:T(8,128)(2,1)S(1)} %get-tuple-element.103), channel_id=1, source_target_pairs={{0,1},{1,0},{2,3},{3,2},{4,5},{5,4},{6,7},{7,6},{8,9},{9,8},{10,11... | collective-permute-start | bytes 196616 | tf_op jit(solution)/shard_map/ppermute | solution.py:453
  69.3 7.8 %collective-permute-start.28 = (bf16[2,128,128]{2,1,0:T(8,128)(2,1)S(1)}, bf16[2,128,128]{2,1,0:T(8,128)(2,1)S(1)}, u32[]{:S(2)}, u32[]{:S(2)}) collective-permute-start(bf16[2,128,128]{2,1,0:T(8,128)(2,1)S(1)} %get-tuple-element.114), channel_id=1, source_target_pairs={{0,9},{1,8},{2,11},{3,10},{4,13},{5,12},{6,15},{7,14},{8,1},{9,0},... | collective-permute-start | bytes 196616 | tf_op jit(solution)/shard_map/ppermute | solution.py:453
  70.0 7.1 %collective-permute-start.29 = (bf16[2,128,128]{2,1,0:T(8,128)(2,1)S(1)}, bf16[2,128,128]{2,1,0:T(8,128)(2,1)S(1)}, u32[]{:S(2)}, u32[]{:S(2)}) collective-permute-start(bf16[2,128,128]{2,1,0:T(8,128)(2,1)S(1)} %get-tuple-element.116), channel_id=1, source_target_pairs={{0,2},{1,3},{2,0},{3,1},{4,6},{5,7},{6,4},{7,5},{8,10},{9,11},{10,... | collective-permute-start | bytes 196616 | tf_op jit(solution)/shard_map/ppermute | solution.py:453
  72.2 7.5 %collective-permute-start.17 = (bf16[2,128,128]{2,1,0:T(8,128)(2,1)S(1)}, bf16[2,128,128]{2,1,0:T(8,128)(2,1)S(1)}, u32[]{:S(2)}, u32[]{:S(2)}) collective-permute-start(bf16[2,128,128]{2,1,0:T(8,128)(2,1)S(1)} %get-tuple-element.94), channel_id=1, source_target_pairs={{0,10},{1,11},{2,8},{3,9},{4,14},{5,15},{6,12},{7,13},{8,2},{9,3},... | collective-permute-start | bytes 196616 | tf_op jit(solution)/shard_map/ppermute | solution.py:453
  (9 other events, 106.5 us)
